TPU v7x, 256 devices: a whole 4x4x8 slice. The times are simulated.
256 devices in a mesh: dp: 8 (over x, core), seg: 4 (over y), grp: 8 (over z).
Axes of the slice: x: 4, y: 4, z: 8, core: 2. Of those that a mesh axis runs over, the one named last changes fastest.
Arguments:
- query: bfloat16 [8, 4096, 2048], P('dp', ('seg', 'grp')), may hold values from -6 to 6
- key: bfloat16 [8, 4096, 2048], P('dp', ('seg', 'grp')), may hold values from -6 to 6
- value: bfloat16 [8, 4096, 2048], P('dp', ('seg', 'grp')), may hold values from -6 to 6
- dout: bfloat16 [8, 4096, 2048], P('dp', ('seg', 'grp')), may hold values from -0.125 to 0.125
- gate_in: bfloat16 [8, 4096, 16], P('dp', ('seg', 'grp'))
- gate_bias: float32 [16], replicated, may hold values from -1 to 1
- offsets: int32 [8, 4], P('dp'), may hold values from 0 to 4095, as said below
Outputs:
- query_grad: bfloat16 [8, 4096, 2048], P('dp', ('seg', 'grp'))
- key_grad: bfloat16 [8, 4096, 2048], P('dp', ('seg', 'grp'))
- value_grad: bfloat16 [8, 4096, 2048], P('dp', ('seg', 'grp'))
- gate_grad: bfloat16 [8, 4096, 16], P('dp', ('seg', 'grp'))
- bias_grad: float32 [16], replicated
Inputs may be any that keep to these rules, and one draw needn't show every extreme that they name: `offsets`: each row holds 4 document starts in increasing order; the first is 0 and the last is 4095.
All inputs are finite; a program needn't handle non-finite values.
Results may differ from a plain program's by a relative error of at most 0.0045.
Values may be sent and summed in bfloat16 or wider, within the bound.
No kernel may reach another device: no remote copies, remote signals or barrier semaphores. Data moves between devices by JAX's collectives and lax.ppermute only.
A program may use at most 192 MiB of HBM per device.

v0:
```python
import jax
import jax.numpy as jnp
from jax import lax
from jax.experimental import pallas as pl
from jax.experimental.pallas import tpu as pltpu
from jax.sharding import PartitionSpec as P

HEAD_DIM = 128
SCALE = HEAD_DIM ** (-0.5)
DOCS = 4
LINE = ("seg", "grp")
ALL = ("dp", "seg", "grp")
TAIL = 16
F32 = jnp.float32
BF16 = jnp.bfloat16
VMEM = pl.BlockSpec(memory_space=pltpu.VMEM)
SMEM = pl.BlockSpec(memory_space=pltpu.SMEM)
HIGHEST = lax.Precision.HIGHEST


def nn(a, b, precision=None):
    return lax.dot_general(
        a, b, (((1,), (0,)), ((), ())), precision=precision, preferred_element_type=F32
    )


def nt(a, b, precision=None):
    return lax.dot_general(
        a, b, (((1,), (1,)), ((), ())), precision=precision, preferred_element_type=F32
    )


def tn(a, b, precision=None):
    return lax.dot_general(
        a, b, (((0,), (0,)), ((), ())), precision=precision, preferred_element_type=F32
    )


def split2(x):
    hi = x.astype(BF16)
    return hi, (x - hi.astype(F32)).astype(BF16)


def encode(x):
    top = jnp.maximum(jnp.max(jnp.abs(x), axis=0, keepdims=True), 1e-30)
    power = jnp.ceil(jnp.log2(top))
    steps = jnp.clip(jnp.floor(x * jnp.exp2(15.0 - power) + 0.5), -32767.0, 32767.0)
    return whole16(steps), power


def whole16(x):
    return x.astype(jnp.int32).astype(jnp.int16)


def wide(x):
    return x.astype(jnp.int32).astype(F32)


def rows16(*rows):
    at = lax.broadcasted_iota(jnp.int32, (TAIL, HEAD_DIM), 0)
    total = jnp.zeros((TAIL, HEAD_DIM), F32)
    for i, row in enumerate(rows):
        total = jnp.where(at == i, row, total)
    return whole16(total)


def doc_of(pos, offsets_ref):
    total = (pos >= offsets_ref[0, 0]).astype(jnp.int32)
    for i in range(1, DOCS):
        total = total + (pos >= offsets_ref[0, i]).astype(jnp.int32)
    return total


def decays(gate_ref, bias_ref, offsets_ref):
    length = gate_ref.shape[1]
    first = (lax.axis_index("seg") * lax.axis_size("grp") + lax.axis_index("grp")) * length
    logits = gate_ref[0].astype(F32) + bias_ref[...]
    step = -(jnp.maximum(logits, 0.0) + jnp.log1p(jnp.exp(-jnp.abs(logits))))
    rows = lax.broadcasted_iota(jnp.int32, (length, length), 0)
    cols = lax.broadcasted_iota(jnp.int32, (length, length), 1)
    causal = rows >= cols
    cumulative = nn(causal.astype(F32), step, HIGHEST)
    doc = doc_of(first + lax.broadcasted_iota(jnp.int32, (length, 1), 0), offsets_ref)
    doc_last = doc_of(first + length - 1, offsets_ref)
    before = jnp.where(first > 0, doc_of(first - 1, offsets_ref), -1)
    last_total = cumulative[length - 1 :, :]
    entry = jnp.exp(cumulative) * (doc == before).astype(F32)
    tail = jnp.exp(last_total - cumulative) * (doc == doc_last).astype(F32)
    through = jnp.where(doc_last == before, jnp.maximum(last_total, -120.0), -128.0)
    return first, logits, step, causal, cumulative, doc, entry, tail, through


def states_kernel(query_ref, key_ref, value_ref, dout_ref, gate_ref, bias_ref, offsets_ref, pay_ref):
    heads = bias_ref.shape[1]
    _, _, _, _, _, _, entry, tail, through = decays(gate_ref, bias_ref, offsets_ref)
    coarse = jnp.floor(through * 256.0 + 0.5)
    fine = jnp.floor((through - coarse / 256.0) * 8388608.0 + 0.5)
    for h in range(heads):
        cols = pl.ds(h * HEAD_DIM, HEAD_DIM)
        one = slice(h, h + 1)
        for slot, left_ref, right_ref, weight in (
            (2 * h, key_ref, value_ref, tail[:, one]),
            (2 * h + 1, query_ref, dout_ref, entry[:, one] * SCALE),
        ):
            upper, lower = split2(left_ref[0, :, cols].astype(F32) * weight)
            right = right_ref[0, :, cols]
            steps, power = encode(tn(upper, right) + tn(lower, right))
            pay_ref[slot, 0:HEAD_DIM, :] = steps
            pay_ref[slot, HEAD_DIM : HEAD_DIM + TAIL, :] = rows16(power, coarse[:, one], fine[:, one])


def scan_kernel(pay_ref, out_ref):
    count = pay_ref.shape[0]
    mine = lax.axis_index("seg") * lax.axis_size("grp") + lax.axis_index("grp")
    backward = lax.rem(mine, 2) == 1

    def turn(step, carry):
        chunk = jnp.where(backward, count - 1 - step, step)
        steps, power = encode(carry)
        out_ref[chunk, 0:HEAD_DIM, :] = steps
        out_ref[chunk, HEAD_DIM : HEAD_DIM + TAIL, :] = rows16(power)
        tail = wide(pay_ref[chunk, HEAD_DIM : HEAD_DIM + TAIL, :])
        passing = jnp.exp(tail[1:2] / 256.0 + tail[2:3] / 8388608.0)
        own = wide(pay_ref[chunk, 0:HEAD_DIM, :]) * jnp.exp2(tail[0:1] - 15.0)
        return passing * carry + own

    lax.fori_loop(0, count, turn, jnp.zeros((HEAD_DIM, HEAD_DIM), F32), unroll=4)


def grads_kernel(
    query_ref, key_ref, value_ref, dout_ref, gate_ref, bias_ref, offsets_ref, state_ref,
    dq_ref, dk_ref, dv_ref, dgate_ref, dbias_ref,
):
    length = gate_ref.shape[1]
    heads = bias_ref.shape[1]
    first, logits, step, causal, cumulative, doc, entry, tail, through = decays(
        gate_ref, bias_ref, offsets_ref
    )
    cumulative_row = lax.dot_general(
        step, causal.astype(F32), (((0,), (1,)), ((), ())), precision=HIGHEST, preferred_element_type=F32
    )
    doc_row = doc_of(first + lax.broadcasted_iota(jnp.int32, (1, length), 1), offsets_ref)
    linked = causal & (doc == doc_row)
    lane = lax.broadcasted_iota(jnp.int32, (length, heads), 1)
    sublane = lax.broadcasted_iota(jnp.int32, (heads, length), 0)
    ends = jnp.zeros((length, heads), F32)
    starts = jnp.zeros((length, heads), F32)
    ends_row = jnp.zeros((heads, length), F32)
    whole = jnp.zeros((1, heads), F32)
    for h in range(heads):
        cols = pl.ds(h * HEAD_DIM, HEAD_DIM)
        one = slice(h, h + 1)
        q, k, v, d = (ref[0, :, cols] for ref in (query_ref, key_ref, value_ref, dout_ref))
        q32, k32 = q.astype(F32), k.astype(F32)
        state32, grad32 = (
            wide(state_ref[slot, 0:HEAD_DIM, :])
            * jnp.exp2(wide(state_ref[slot, HEAD_DIM : HEAD_DIM + TAIL, :])[0:1] - 15.0)
            for slot in (2 * h, 2 * h + 1)
        )
        state, state_low = split2(state32)
        grad, grad_low = split2(grad32)
        weights = jnp.where(
            linked, jnp.exp(jnp.where(linked, cumulative[:, one] - cumulative_row[one, :], 0.0)), 0.0
        ) * SCALE
        probs = nt(q, k) * weights
        dprobs = nt(d, v)
        pairs = probs * dprobs
        probs = probs.astype(BF16)
        dscores = (dprobs * weights).astype(BF16)
        dq_inter = (entry[:, one] * SCALE) * (nt(d, state) + nt(d, state_low))
        dk_inter = tail[:, one] * (nt(v, grad) + nt(v, grad_low))
        dq_ref[0, :, cols] = (nn(dscores, k) + dq_inter).astype(BF16)
        dk_ref[0, :, cols] = (tn(dscores, q) + dk_inter).astype(BF16)
        dv_ref[0, :, cols] = (tn(probs, d) + tail[:, one] * nn(k, grad)).astype(BF16)
        at_end = jnp.sum(pairs + q32 * dq_inter, axis=1, keepdims=True)
        at_start = jnp.sum(k32 * dk_inter, axis=1, keepdims=True)
        product = jnp.sum(state32 * grad32, keepdims=True)
        ends = jnp.where(lane == h, at_end, ends)
        starts = jnp.where(lane == h, at_start, starts)
        ends_row = jnp.where(sublane == h, jnp.sum(pairs, axis=0, keepdims=True), ends_row)
        whole = jnp.where(lane[0:1] == h, product, whole)
    causal = causal.astype(F32)
    after = tn(causal, ends, HIGHEST) - lax.dot_general(
        causal, ends_row, (((0,), (1,)), ((), ())), precision=HIGHEST, preferred_element_type=F32
    )
    earlier = nn(causal, starts, HIGHEST) - starts
    dstep = after + earlier + jnp.exp(through) * whole
    dlogit = -dstep / (1.0 + jnp.exp(-logits))
    dgate_ref[0] = dlogit.astype(BF16)
    dbias_ref[...] = jnp.sum(dlogit, axis=0, keepdims=True)


PARAMS = pltpu.CompilerParams(vmem_limit_bytes=48 * 1024 * 1024)


def shards(query, key, value, dout, gate_in, gate_bias, offsets):
    heads = gate_bias.shape[0]
    count = lax.axis_size("seg") * lax.axis_size("grp")
    bias_row = gate_bias.reshape(1, heads)
    inputs = (query, key, value, dout, gate_in, bias_row, offsets)
    specs = [VMEM] * 6 + [SMEM]
    pay = pl.pallas_call(
        states_kernel,
        out_shape=jax.ShapeDtypeStruct((2 * heads, HEAD_DIM + TAIL, HEAD_DIM), jnp.int16),
        in_specs=specs,
        out_specs=VMEM,
        compiler_params=PARAMS,
    )(*inputs)
    pay = lax.all_to_all(pay, LINE, split_axis=0, concat_axis=0, tiled=True)
    carried = pl.pallas_call(
        scan_kernel,
        out_shape=jax.ShapeDtypeStruct((count, HEAD_DIM + TAIL, HEAD_DIM), jnp.int16),
        in_specs=[VMEM],
        out_specs=VMEM,
        compiler_params=PARAMS,
    )(pay)
    carried = lax.all_to_all(carried, LINE, split_axis=0, concat_axis=0, tiled=True)
    like = jax.ShapeDtypeStruct(query.shape, BF16)
    dq, dk, dv, dgate, dbias = pl.pallas_call(
        grads_kernel,
        out_shape=(
            like,
            like,
            like,
            jax.ShapeDtypeStruct(gate_in.shape, BF16),
            jax.ShapeDtypeStruct((1, heads), F32),
        ),
        in_specs=specs + [VMEM],
        out_specs=(VMEM,) * 5,
        compiler_params=PARAMS,
    )(*inputs, carried)
    everywhere = lax.all_to_all(
        jnp.broadcast_to(dbias[None], (lax.axis_size(ALL), 1, heads)), ALL, split_axis=0, concat_axis=0, tiled=True
    )
    return dq, dk, dv, dgate, jnp.sum(everywhere, axis=(0, 1))


def solution(mesh):
    rows = P("dp", LINE, None)
    return jax.shard_map(
        shards,
        mesh=mesh,
        in_specs=(rows, rows, rows, rows, rows, P(), P("dp", None)),
        out_specs=(rows, rows, rows, rows, P()),
        check_vma=False,
    )
```

profile of v0, /device:TPU:1, one launch (start us, length us, event | category | flops | bytes accessed | tf_op | source)
XLA Modules:
  0.0 121.3 jit_solution(6344999654474131404)
XLA Ops:
  0.6 0.8 copy.19.gate_ref
  1.4 0.0 copy-start
  1.4 1.0 copy-done
  2.5 0.0 copy-start.2
  2.5 1.0 copy-done.2
  3.5 0.0 copy-start.4
  3.5 1.0 copy-done.4
  4.6 0.0 copy-start.6
  4.6 1.0 copy-done.6
  5.6 0.0 copy-start.7
  5.6 0.7 copy-done.7
  6.3 0.0 copy-start.8
  6.3 0.7 copy-done.8
  6.9 3.4 %shard_map.110 = s16[32,144,128]{2,1,0:T(8,128)(2,1)S(1)} custom-call(bf16[1,128,2048]{2,1,0:T(8,128)(2,1)S(1)} %copy-done, bf16[1,128,2048]{2,1,0:T(8,128)(2,1)S(1)} %copy-done.2, bf16[1,128,2048]{2,1,0:T(8,128)(2,1)S(1)} %copy-done.4, bf16[1,128,2048]{2,1,0:T(8,128)(2,1)S(1)} %copy-done.6, bf16[1,128,16]{2,1,0:T(8,128)(2,1)S(1)} %copy.19.gate_ref, ...), custom_call_target="tpu_custom_call" | custom-call | tf_op jit(solution)/shard_map/pallas_call | solution.py:202
  10.4 42.9 %all_to_all.15.pay_ref = s16[32,144,128]{2,1,0:T(8,128)(2,1)S(1)} all-to-all(s16[32,144,128]{2,1,0:T(8,128)(2,1)S(1)} %shard_map.110), channel_id=1, replica_groups=mesh['dp'=8,'seg'=4,'grp'=8] {'seg','grp'}, dimensions={0} | all-to-all | bytes 2359296 | tf_op jit(solution)/shard_map/all_to_all | solution.py:209
  53.3 1.1 shard_map.111
  54.5 0.0 copy-start.1
  54.5 0.0 copy-start.3
  54.5 0.0 copy-start.5
  54.5 35.7 %all_to_all.16.state_ref = s16[32,144,128]{2,1,0:T(8,128)(2,1)S(1)} all-to-all(s16[32,144,128]{2,1,0:T(8,128)(2,1)S(1)} %shard_map.111), channel_id=1, replica_groups=mesh['dp'=8,'seg'=4,'grp'=8] {'seg','grp'}, dimensions={0} | all-to-all | bytes 2359296 | tf_op jit(solution)/shard_map/all_to_all | solution.py:217
  90.2 0.0 copy-done.1
  90.2 0.0 copy-done.3
  90.2 0.0 copy-done.5
  90.2 7.0 %shard_map.112 = (bf16[1,128,2048]{2,1,0:T(8,128)(2,1)}, bf16[1,128,2048]{2,1,0:T(8,128)(2,1)}, bf16[1,128,2048]{2,1,0:T(8,128)(2,1)}, bf16[1,128,16]{2,1,0:T(8,128)(2,1)S(1)}, f32[1,16]{1,0:T(1,128)S(1)}) custom-call(bf16[1,128,2048]{2,1,0:T(8,128)(2,1)S(1)} %copy-done.1, bf16[1,128,2048]{2,1,0:T(8,128)(2,1)S(1)} %copy-done.3, ...), custom_call_target="tpu_custom_call" | custom-call | tf_op jit(solution)/shard_map/pallas_call | solution.py:219
  97.2 0.7 broadcast_in_dim.9
  98.0 9.6 %all-to-all-start.2 = ((f32[256,1,16]{2,1,0:T(1,128)}), f32[256,1,16]{2,1,0:T(1,128)S(1)}, u32[]{:S(2)}, u32[]{:S(2)}) async-start(f32[256,1,16]{2,1,0:T(1,128)} %broadcast_in_dim.9), calls=%async_computation.2 | async-start | bytes 262144 | tf_op jit(solution)/shard_map/all_to_all | solution.py:232
  107.6 0.7 copy.21
  108.2 12.3 %all-to-all-done.2 = f32[256,1,16]{2,1,0:T(1,128)S(1)} async-done(((f32[256,1,16]{2,1,0:T(1,128)}), f32[256,1,16]{2,1,0:T(1,128)S(1)}, u32[]{:S(2)}, u32[]{:S(2)}) %all-to-all-start.2) | async-done | bytes 16416 | tf_op jit(solution)/shard_map/all_to_all | solution.py:232
  120.6 0.8 reduce_sum.9
Async XLA Ops:
  1.4 1.0 copy-start
  2.5 1.0 copy-start.2
  3.5 1.0 copy-start.4
  4.6 1.0 copy-start.6
  5.6 0.7 copy-start.7
  6.3 0.7 copy-start.8
  54.5 35.8 %copy-start.1 = (bf16[1,128,2048]{2,1,0:T(8,128)(2,1)S(1)}, bf16[1,128,2048]{2,1,0:T(8,128)(2,1)}, u32[]{:S(2)}) copy-start(bf16[1,128,2048]{2,1,0:T(8,128)(2,1)} %query_ref.3) | copy-start | bytes 1572868
  54.5 35.8 %copy-start.3 = (bf16[1,128,2048]{2,1,0:T(8,128)(2,1)S(1)}, bf16[1,128,2048]{2,1,0:T(8,128)(2,1)}, u32[]{:S(2)}) copy-start(bf16[1,128,2048]{2,1,0:T(8,128)(2,1)} %key_ref.3) | copy-start | bytes 1572868
  54.5 35.7 %copy-start.5 = (bf16[1,128,2048]{2,1,0:T(8,128)(2,1)S(1)}, bf16[1,128,2048]{2,1,0:T(8,128)(2,1)}, u32[]{:S(2)}) copy-start(bf16[1,128,2048]{2,1,0:T(8,128)(2,1)} %value_ref.3) | copy-start | bytes 1572868
  98.0 22.6 %all-to-all-start.2 = ((f32[256,1,16]{2,1,0:T(1,128)}), f32[256,1,16]{2,1,0:T(1,128)S(1)}, u32[]{:S(2)}, u32[]{:S(2)}) async-start(f32[256,1,16]{2,1,0:T(1,128)} %broadcast_in_dim.9), calls=%async_computation.2 | async-start | bytes 262144 | tf_op jit(solution)/shard_map/all_to_all | solution.py:232
where the time goes:
time: 122 us; the launch traced here: 121 us
  blocking collectives  78.7 us (65%)
  waiting for transfers between devices  12.3 us (10%)
  Pallas kernels  11.6 us (10%)
  starting transfers between devices  9.59 us (8%)
  local copies, waits for them, and re-layouts  7.68 us (6%)
    all_to_all x1, blocking collectives, shards(): pay = lax.all_to_all(pay, LINE, split_axis=0, concat_axis=0, tiled=True)  42.9 us
    all_to_all x1, blocking collectives, shards(): lax.all_to_all(carried, LINE, split_axis=0, concat_axis=0, tiled=True)  35.7 us
    all_to_all x1, waiting for transfers between devices, shards(): lax.all_to_all(jnp.broadcast_to(dbias[None], (lax.axis_size(ALL), 1, head...  12.3 us
    all_to_all x1, starting transfers between devices, shards(): lax.all_to_all(jnp.broadcast_to(dbias[None], (lax.axis_size(ALL), 1, head...  9.59 us
    pallas_call x1, Pallas kernels, shards(): pl.pallas_call(grads_kernel, out_shape=(like, like, like, jax.ShapeDtypeS...  7.02 us
    unnamed x20, local copies, waits for them, and re-layouts  6.97 us
    pallas_call x1, Pallas kernels, shards(): pl.pallas_call(states_kernel, out_shape=jax.ShapeDtypeStruct((2 * heads,...  3.44 us
  transfers between devices with their start and end apart: 1, of which 1 were waited for; matrix products, arithmetic and copies ran while one was open for 1% of the time, Pallas kernels for 0%

commit v1 on v0

v1 whole, which is shorter than its diff:
```python
import jax
import jax.numpy as jnp
from jax import lax
from jax.experimental import pallas as pl
from jax.experimental.pallas import tpu as pltpu
from jax.sharding import PartitionSpec as P

HEAD_DIM = 128
SCALE = HEAD_DIM ** (-0.5)
DOCS = 4
LINE = ("seg", "grp")
ALL = ("dp", "seg", "grp")
TAIL = 16
LANES = 128
F32 = jnp.float32
BF16 = jnp.bfloat16
I16 = jnp.int16
VMEM = pl.BlockSpec(memory_space=pltpu.VMEM)
SMEM = pl.BlockSpec(memory_space=pltpu.SMEM)
HBM = pl.BlockSpec(memory_space=pl.ANY)
HIGHEST = lax.Precision.HIGHEST
PARAMS = pltpu.CompilerParams(vmem_limit_bytes=48 * 1024 * 1024)


def dot(a, b, over, precision=None):
    return lax.dot_general(
        a, b, (((over[0],), (over[1],)), ((), ())), precision=precision, preferred_element_type=F32
    )


def nn(a, b, precision=None):
    return dot(a, b, (1, 0), precision)


def nt(a, b, precision=None):
    return dot(a, b, (1, 1), precision)


def tn(a, b, precision=None):
    return dot(a, b, (0, 0), precision)


def split2(x):
    hi = x.astype(BF16)
    return hi, (x - hi.astype(F32)).astype(BF16)


def matrix(m):
    return pl.ds(m * HEAD_DIM, HEAD_DIM)


def tail_of(ref):
    return pl.ds(ref.shape[-2] - TAIL, TAIL)


def encode(x):
    top = jnp.maximum(jnp.max(jnp.abs(x), axis=0, keepdims=True), 1e-30)
    power = jnp.ceil(jnp.log2(top))
    return jnp.clip(jnp.floor(x * jnp.exp2(15.0 - power) + 0.5), -32767.0, 32767.0), power


def decode(steps, power):
    return wide(steps) * jnp.exp2(power - 15.0)


def log_parts(log):
    log = jnp.maximum(log, -128.0)
    coarse = jnp.floor(log * 256.0 + 0.5)
    return coarse, jnp.floor((log - coarse / 256.0) * 8388608.0 + 0.5)


def log_whole(coarse, fine):
    return coarse / 256.0 + fine / 8388608.0


def whole16(x):
    return x.astype(jnp.int32).astype(I16)


def wide(x):
    return x.astype(jnp.int32).astype(F32)


def rows16(*rows):
    at = lax.broadcasted_iota(jnp.int32, (TAIL, LANES), 0)
    total = jnp.zeros((TAIL, LANES), F32)
    for i, row in enumerate(rows):
        total = jnp.where(at == i, row, total)
    return whole16(total)


def iota(shape, dim):
    return lax.broadcasted_iota(jnp.int32, shape, dim)


def doc_of(pos, offsets_ref):
    total = (pos >= offsets_ref[0, 0]).astype(jnp.int32)
    for i in range(1, DOCS):
        total = total + (pos >= offsets_ref[0, i]).astype(jnp.int32)
    return total


def decays(gate_ref, bias_ref, offsets_ref):
    heads, length = gate_ref.shape[1:]
    first = (lax.axis_index("seg") * lax.axis_size("grp") + lax.axis_index("grp")) * length
    same = iota((heads, heads), 0) == iota((heads, heads), 1)
    bias = jnp.sum(jnp.where(same, bias_ref[...], 0.0), axis=1, keepdims=True)
    logits = gate_ref[0].astype(F32) + bias
    step = -(jnp.maximum(logits, 0.0) + jnp.log1p(jnp.exp(-jnp.abs(logits))))
    causal = iota((length, length), 0) >= iota((length, length), 1)
    cumulative = nt(causal.astype(F32), step, HIGHEST)
    doc = doc_of(first + iota((length, 1), 0), offsets_ref)
    doc_last = doc_of(first + length - 1, offsets_ref)
    before = jnp.where(first > 0, doc_of(first - 1, offsets_ref), -1)
    last_total = cumulative[length - 1 :, :]
    entry = jnp.exp(cumulative) * (doc == before).astype(F32)
    tail = jnp.exp(last_total - cumulative) * (doc == doc_last).astype(F32)
    passes = doc_last == before
    return first, logits, step, causal, cumulative, doc, entry, tail, passes


def states_kernel(
    query_ref, key_ref, value_ref, dout_ref, gate_ref, bias_ref, offsets_ref, pay_ref, held, sems
):
    heads = bias_ref.shape[1]
    parts = sems.shape[1]
    width = query_ref.shape[2] // parts
    copies = [
        [
            pltpu.make_async_copy(
                ref.at[0, :, pl.ds(p * width, width)], held.at[i, :, pl.ds(p * width, width)], sems.at[i, p]
            )
            for i, ref in enumerate((query_ref, key_ref, value_ref, dout_ref))
        ]
        for p in range(parts)
    ]
    for group in copies:
        for copy in group:
            copy.start()
    _, _, _, _, cumulative, _, entry, tail, passes = decays(gate_ref, bias_ref, offsets_ref)
    coarse, fine = log_parts(jnp.where(passes, jnp.maximum(cumulative[-1:, :], -120.0), -128.0))
    powers = {}
    for h in range(heads):
        if h % (heads // parts) == 0:
            for copy in copies[h // (heads // parts)]:
                copy.wait()
        cols = matrix(h)
        one = slice(h, h + 1)
        slot, m = divmod(h, 2)
        for place, left, right, weight in (
            (m, 1, 2, tail[:, one]),
            (2 + m, 0, 3, entry[:, one] * SCALE),
        ):
            upper, lower = split2(held[left, :, cols].astype(F32) * weight)
            right = held[right, :, cols]
            steps, powers[place] = encode(tn(upper, right) + tn(lower, right))
            pay_ref[slot, matrix(place), :] = whole16(steps)
        if m == 1:
            pay_ref[slot, tail_of(pay_ref), :] = rows16(
                *(powers[i] for i in range(4)),
                *(x[:, i : i + 1] for i in (h - 1, h) for x in (coarse, fine)),
            )


def totals_kernel(pay_ref, *send_refs):
    count = pay_ref.shape[0]
    tails = [wide(pay_ref[c, tail_of(pay_ref), :]) for c in range(count)]
    mine, segments = lax.axis_index("seg"), lax.axis_size("seg")
    ends, logs = [], []
    for m in range(2):
        log = [log_whole(t[4 + 2 * m : 5 + 2 * m], t[5 + 2 * m : 6 + 2 * m]) for t in tails]
        for place, order in ((m, range(count)), (2 + m, range(count - 1, -1, -1))):
            carry = jnp.zeros((HEAD_DIM, HEAD_DIM), F32)
            for c in order:
                carry = jnp.exp(log[c]) * carry + decode(
                    pay_ref[c, matrix(place), :], tails[c][place : place + 1]
                )
            ends.append(encode(carry))
        logs.extend(log_parts(sum(log)))
    for distance, send_ref in enumerate(send_refs, 1):
        later = mine + distance < segments
        for m in range(2):
            send_ref[matrix(m), :] = whole16(jnp.where(later, ends[2 * m][0], ends[2 * m + 1][0]))
        send_ref[tail_of(send_ref), :] = rows16(
            *(jnp.where(later, ends[2 * m][1], ends[2 * m + 1][1]) for m in range(2)), *logs
        )


def scan_kernel(pay_ref, *refs):
    *got_refs, out_ref = refs
    count = pay_ref.shape[0]
    mine = lax.axis_index("seg")
    tails = [wide(pay_ref[c, tail_of(pay_ref), :]) for c in range(count)]
    got_tails = [wide(ref[tail_of(ref), :]) for ref in got_refs]
    powers = [[None] * 4 for _ in range(count)]
    for m in range(2):
        log = [log_whole(t[4 + 2 * m : 5 + 2 * m], t[5 + 2 * m : 6 + 2 * m]) for t in tails]
        sent = [
            (jnp.exp(log_whole(t[2 + 2 * m : 3 + 2 * m], t[3 + 2 * m : 4 + 2 * m])), decode(ref[matrix(m), :], t[m : m + 1]))
            for ref, t in zip(got_refs, got_tails)
        ]
        state = jnp.zeros((HEAD_DIM, HEAD_DIM), F32)
        for d in range(len(sent), 0, -1):
            state = jnp.where(mine >= d, sent[d - 1][0] * state + sent[d - 1][1], state)
        grad = jnp.zeros((HEAD_DIM, HEAD_DIM), F32)
        for d in range(1, len(sent) + 1):
            grad = jnp.where(mine < d, sent[d - 1][0] * grad + sent[d - 1][1], grad)
        for place, carry, order in ((m, state, range(count)), (2 + m, grad, range(count - 1, -1, -1))):
            for i, c in enumerate(order):
                steps, powers[c][place] = encode(carry)
                out_ref[c, matrix(place), :] = whole16(steps)
                if i < count - 1:
                    carry = jnp.exp(log[c]) * carry + decode(
                        pay_ref[c, matrix(place), :], tails[c][place : place + 1]
                    )
    for c in range(count):
        out_ref[c, tail_of(out_ref), :] = rows16(*powers[c])


def grads_kernel(
    query_ref, key_ref, value_ref, dout_ref, gate_ref, bias_ref, offsets_ref, state_ref,
    dq_ref, dk_ref, dv_ref, dgate_ref, dbias_ref,
):
    heads, length = gate_ref.shape[1:]
    first, logits, step, causal, cumulative, doc, entry, tail, passes = decays(
        gate_ref, bias_ref, offsets_ref
    )
    cumulative_row = nt(step, causal.astype(F32), HIGHEST)
    linked = causal & (doc == doc_of(first + iota((1, length), 1), offsets_ref))
    lane = iota((length, heads), 1)
    sublane = iota((heads, length), 0)
    ends = jnp.zeros((length, heads), F32)
    starts = jnp.zeros((length, heads), F32)
    ends_row = jnp.zeros((heads, length), F32)
    whole = jnp.zeros((heads, 1), F32)
    for h in range(heads):
        cols = matrix(h)
        one = slice(h, h + 1)
        q, k, v, d = (ref[0, :, cols] for ref in (query_ref, key_ref, value_ref, dout_ref))
        q32, k32 = q.astype(F32), k.astype(F32)
        slot, m = divmod(h, 2)
        powers = wide(state_ref[slot, tail_of(state_ref), :])
        state32, grad32 = (
            decode(state_ref[slot, matrix(place), :], powers[place : place + 1]) for place in (m, 2 + m)
        )
        state, state_low = split2(state32)
        grad, grad_low = split2(grad32)
        weights = jnp.where(
            linked, jnp.exp(jnp.where(linked, cumulative[:, one] - cumulative_row[one, :], 0.0)), 0.0
        ) * SCALE
        probs = nt(q, k) * weights
        dprobs = nt(d, v)
        pairs = probs * dprobs
        probs = probs.astype(BF16)
        dscores = (dprobs * weights).astype(BF16)
        dq_inter = (entry[:, one] * SCALE) * (nt(d, state) + nt(d, state_low))
        dk_inter = tail[:, one] * (nt(v, grad) + nt(v, grad_low))
        dq_ref[0, :, cols] = (nn(dscores, k) + dq_inter).astype(BF16)
        dk_ref[0, :, cols] = (tn(dscores, q) + dk_inter).astype(BF16)
        dv_ref[0, :, cols] = (tn(probs, d) + tail[:, one] * nn(k, grad)).astype(BF16)
        at_end = jnp.sum(pairs + q32 * dq_inter, axis=1, keepdims=True)
        at_start = jnp.sum(k32 * dk_inter, axis=1, keepdims=True)
        product = jnp.sum(state32 * grad32, keepdims=True)
        ends = jnp.where(lane == h, at_end, ends)
        starts = jnp.where(lane == h, at_start, starts)
        ends_row = jnp.where(sublane == h, jnp.sum(pairs, axis=0, keepdims=True), ends_row)
        whole = jnp.where(sublane[:, :1] == h, product, whole)
    through = jnp.where(passes, jnp.exp(cumulative_row[:, length - 1 :]), 0.0)
    causal = causal.astype(F32)
    earlier = (iota((length, length), 0) < iota((length, length), 1)).astype(F32)
    dstep = (
        tn(ends, causal, HIGHEST)
        - nn(ends_row, causal, HIGHEST)
        + tn(starts, earlier, HIGHEST)
        + through * whole
    )
    dlogit = -dstep / (1.0 + jnp.exp(-logits))
    dgate_ref[0] = dlogit.astype(BF16)
    same = iota((heads, heads), 0) == iota((heads, heads), 1)
    dbias_ref[...] = jnp.sum(
        jnp.where(same, jnp.sum(dlogit, axis=1, keepdims=True), 0.0), axis=0, keepdims=True
    )


def call(kernel, out_shape, in_specs, **more):
    several = isinstance(out_shape, tuple)
    return pl.pallas_call(
        kernel,
        out_shape=out_shape,
        in_specs=in_specs,
        out_specs=(VMEM,) * len(out_shape) if several else VMEM,
        compiler_params=PARAMS,
        **more,
    )


def shards(query, key, value, dout, gate_in, gate_bias, offsets):
    heads = gate_bias.shape[0]
    count, segments = lax.axis_size("grp"), lax.axis_size("seg")
    gates = jnp.swapaxes(gate_in, 1, 2)
    rest = (gates, gate_bias.reshape(1, heads), offsets)
    packed = jax.ShapeDtypeStruct((count, 4 * HEAD_DIM + TAIL, LANES), I16)
    pay = call(
        states_kernel,
        packed,
        [HBM] * 4 + [VMEM] * 2 + [SMEM],
        scratch_shapes=[pltpu.VMEM((4,) + query.shape[1:], BF16), pltpu.SemaphoreType.DMA((4, 4))],
    )(query, key, value, dout, *rest)
    pay = lax.all_to_all(pay, "grp", split_axis=0, concat_axis=0, tiled=True)
    total = jax.ShapeDtypeStruct((2 * HEAD_DIM + TAIL, LANES), I16)
    sends = call(totals_kernel, (total,) * (segments - 1), [VMEM])(pay)
    got = [
        lax.ppermute(send, "seg", [(i, (i + d) % segments) for i in range(segments)])
        for d, send in enumerate(sends, 1)
    ]
    carried = call(scan_kernel, packed, [VMEM] * segments)(pay, *got)
    carried = lax.all_to_all(carried, "grp", split_axis=0, concat_axis=0, tiled=True)
    like = jax.ShapeDtypeStruct(query.shape, BF16)
    dq, dk, dv, dgate, dbias = call(
        grads_kernel,
        (
            like,
            like,
            like,
            jax.ShapeDtypeStruct(gates.shape, BF16),
            jax.ShapeDtypeStruct((1, heads), F32),
        ),
        [VMEM] * 6 + [SMEM, VMEM],
    )(query, key, value, dout, *rest, carried)
    everywhere = lax.all_to_all(
        jnp.broadcast_to(dbias[None], (lax.axis_size(ALL), 1, heads)), ALL, split_axis=0, concat_axis=0, tiled=True
    )
    return dq, dk, dv, jnp.swapaxes(dgate, 1, 2), jnp.sum(everywhere, axis=(0, 1))


def solution(mesh):
    rows = P("dp", LINE, None)
    return jax.shard_map(
        shards,
        mesh=mesh,
        in_specs=(rows, rows, rows, rows, rows, P(), P("dp", None)),
        out_specs=(rows, rows, rows, rows, P()),
        check_vma=False,
    )
```

time: 122 us -> 119 us (0.975)
  blocking collectives: 78.7 us -> 90.1 us
  waiting for transfers between devices: 12.3 us -> 2.38 us
  starting transfers between devices: 9.59 us -> 5.08 us
  local copies, waits for them, and re-layouts: 7.68 us -> 6.26 us
  Pallas kernels: 11.6 us -> 12.9 us
    all_to_all x1 -> x0, waiting for transfers between devices: 12.3 us -> none  [shards(): lax.all_to_all(jnp.broadcast_to(dbias[None], (lax.axis_size(ALL), 1, head...]
    all_to_all x2 -> x3, blocking collectives: 78.7 us -> 90.1 us  [the longest x1 36.5 us: shards(): pay = lax.all_to_all(pay, 'grp', split_axis=0, concat_axis=0, tiled=True)]
    all_to_all x1 -> x0, starting transfers between devices: 9.59 us -> none  [shards(): lax.all_to_all(jnp.broadcast_to(dbias[None], (lax.axis_size(ALL), 1, head...]
    ppermute x0 -> x3, starting transfers between devices: none -> 5.08 us  [shards(): lax.ppermute(send, 'seg', [(i, (i + d) % segments) for i in range(segment...]
    ppermute x0 -> x3, waiting for transfers between devices: none -> 2.38 us  [shards(): lax.ppermute(send, 'seg', [(i, (i + d) % segments) for i in range(segment...]
    pallas_call x3 -> x4, Pallas kernels: 11.6 us -> 12.9 us  [the longest x1 7.07 us: shards(): call(grads_kernel, (like, like, like, jax.ShapeDtypeStruct(gates.shape, B...]
    unnamed x20 -> x26, local copies, waits for them, and re-layouts: 6.97 us -> 6.19 us
  transfers between devices with their start and end apart: 1 -> 3, of which waited for: 1 -> 2; matrix products, arithmetic and copies ran while one was open for 1% -> 0% of each run, Pallas kernels for 0% -> 0%
where the time goes in v1:
time: 119 us; the launch traced here: 118 us
  blocking collectives  90.1 us (76%)
  Pallas kernels  12.9 us (11%)
  local copies, waits for them, and re-layouts  6.26 us (5%)
  starting transfers between devices  5.08 us (4%)
  waiting for transfers between devices  2.38 us (2%)
    all_to_all x1, blocking collectives, shards(): pay = lax.all_to_all(pay, 'grp', split_axis=0, concat_axis=0, tiled=True)  36.5 us
    all_to_all x1, blocking collectives, shards(): lax.all_to_all(carried, 'grp', split_axis=0, concat_axis=0, tiled=True)  28.8 us
    all_to_all x1, blocking collectives, shards(): lax.all_to_all(jnp.broadcast_to(dbias[None], (lax.axis_size(ALL), 1, head...  24.9 us
    pallas_call x1, Pallas kernels, shards(): call(grads_kernel, (like, like, like, jax.ShapeDtypeStruct(gates.shape, B...  7.07 us
    unnamed x26, local copies, waits for them, and re-layouts  6.19 us
    ppermute x3, starting transfers between devices, shards(): lax.ppermute(send, 'seg', [(i, (i + d) % segments) for i in range(segment...  5.08 us
    pallas_call x1, Pallas kernels, shards(): call(states_kernel, packed, [HBM] * 4 + [VMEM] * 2 + [SMEM], scratch_shap...  4.26 us
    ppermute x3, waiting for transfers between devices, shards(): lax.ppermute(send, 'seg', [(i, (i + d) % segments) for i in range(segment...  2.38 us
  transfers between devices with their start and end apart: 3, of which 2 were waited for; matrix products, arithmetic and copies ran while one was open for 0% of the time, Pallas kernels for 0%

profile of v1, /device:TPU:1, one launch (start us, length us, event | category | flops | bytes accessed | tf_op | source)
XLA Modules:
  0.0 118.3 jit_solution(7583848151567808858)
XLA Ops:
  0.6 0.0 copy-start
  0.6 1.0 copy-done
  1.7 0.0 copy-start.2
  1.7 1.0 copy-done.2
  2.7 0.0 copy-start.4
  2.7 1.0 copy-done.4
  3.8 0.0 copy-start.6
  3.8 1.0 copy-done.6
  4.8 0.0 copy-start.7
  4.8 0.7 copy-done.7
  5.5 0.0 copy-start.9
  5.5 0.7 copy-done.9
  6.1 0.0 copy-start.11
  6.1 0.7 copy-done.11
  6.8 4.3 %shard_map.110 = s16[8,528,128]{2,1,0:T(8,128)(2,1)S(1)} custom-call(bf16[1,128,2048]{2,1,0:T(8,128)(2,1)S(1)} %copy-done, bf16[1,128,2048]{2,1,0:T(8,128)(2,1)S(1)} %copy-done.2, bf16[1,128,2048]{2,1,0:T(8,128)(2,1)S(1)} %copy-done.4, bf16[1,128,2048]{2,1,0:T(8,128)(2,1)S(1)} %copy-done.6, bf16[1,16,128]{2,1,0:T(8,128)(2,1)S(1)} %bitcast.4, ...), custom_call_target="tpu_custom_call" | custom-call | tf_op jit(solution)/shard_map/pallas_call | solution.py:303
  11.1 36.5 %all_to_all.15.pay_ref = s16[8,528,128]{2,1,0:T(8,128)(2,1)S(1)} all-to-all(s16[8,528,128]{2,1,0:T(8,128)(2,1)S(1)} %shard_map.110), channel_id=1, replica_groups=mesh['dp'=8,'seg'=4,'grp'=8] {'grp'}, dimensions={0} | all-to-all | bytes 2162688 | tf_op jit(solution)/shard_map/all_to_all | solution.py:309
  47.6 0.5 shard_map.111
  48.1 1.3 %collective-permute-start = (s16[272,128]{1,0:T(8,128)(2,1)S(1)}, s16[272,128]{1,0:T(8,128)(2,1)S(1)}, u32[]{:S(2)}, u32[]{:S(2)}) collective-permute-start(s16[272,128]{1,0:T(8,128)(2,1)S(1)} %get-tuple-element.13), channel_id=1, source_target_pairs={{0,8},{8,16},{16,24},{24,0},{1,9},{9,17},{17,25},{25,1},{2,10},{10... | collective-permute-start | bytes 208904 | tf_op jit(solution)/shard_map/ppermute | solution.py:313
  49.4 2.7 %collective-permute-start.1 = (s16[272,128]{1,0:T(8,128)(2,1)S(1)}, s16[272,128]{1,0:T(8,128)(2,1)S(1)}, u32[]{:S(2)}, u32[]{:S(2)}) collective-permute-start(s16[272,128]{1,0:T(8,128)(2,1)S(1)} %get-tuple-element.14), channel_id=1, source_target_pairs={{0,16},{8,24},{16,0},{24,8},{1,17},{9,25},{17,1},{25,9},{2,18},{10... | collective-permute-start | bytes 208904 | tf_op jit(solution)/shard_map/ppermute | solution.py:313
  52.1 1.1 collective-permute-start.2
  53.1 0.0 collective-permute-done.refs_0_
  53.1 1.4 %collective-permute-done.1.refs_1_ = s16[272,128]{1,0:T(8,128)(2,1)S(1)} collective-permute-done((s16[272,128]{1,0:T(8,128)(2,1)S(1)}, s16[272,128]{1,0:T(8,128)(2,1)S(1)}, u32[]{:S(2)}, u32[]{:S(2)}) %collective-permute-start.1) | collective-permute-done | bytes 69664 | tf_op jit(solution)/shard_map/ppermute | solution.py:313
  54.5 1.0 collective-permute-done.2.refs_2_
  55.5 1.0 shard_map.112
  56.6 0.0 copy-start.1
  56.6 0.0 copy-start.3
  56.6 0.0 copy-start.5
  56.6 0.0 copy-start.8
  56.6 0.0 copy-start.10
  56.6 0.0 copy-start.12
  56.6 28.8 %all_to_all.16.state_ref = s16[8,528,128]{2,1,0:T(8,128)(2,1)S(1)} all-to-all(s16[8,528,128]{2,1,0:T(8,128)(2,1)S(1)} %shard_map.112), channel_id=1, replica_groups=mesh['dp'=8,'seg'=4,'grp'=8] {'grp'}, dimensions={0} | all-to-all | bytes 2162688 | tf_op jit(solution)/shard_map/all_to_all | solution.py:317
  85.4 0.0 copy-done.1
  85.4 0.0 copy-done.3
  85.4 0.0 copy-done.5
  85.4 0.0 copy-done.8
  85.4 0.0 copy-done.10
  85.4 0.0 copy-done.12
  85.4 7.1 %shard_map.113 = (bf16[1,128,2048]{2,1,0:T(8,128)(2,1)}, bf16[1,128,2048]{2,1,0:T(8,128)(2,1)}, bf16[1,128,2048]{2,1,0:T(8,128)(2,1)}, bf16[1,16,128]{2,1,0:T(8,128)(2,1)}, f32[1,16]{1,0:T(1,128)S(1)}) custom-call(bf16[1,128,2048]{2,1,0:T(8,128)(2,1)S(1)} %copy-done.1, bf16[1,128,2048]{2,1,0:T(8,128)(2,1)S(1)} %copy-done.3, ...), custom_call_target="tpu_custom_call" | custom-call | tf_op jit(solution)/shard_map/pallas_call | solution.py:319
  92.5 0.1 broadcast_in_dim.9
  92.6 24.9 %all_to_all.17 = f32[256,1,16]{2,1,0:T(1,128)S(1)} all-to-all(f32[256,1,16]{2,1,0:T(1,128)S(1)} %broadcast_in_dim.9), channel_id=1, replica_groups=mesh['dp'=8,'seg'=4,'grp'=8] {'dp','seg','grp'}, dimensions={0} | all-to-all | bytes 32768 | tf_op jit(solution)/shard_map/all_to_all | solution.py:330
  117.5 0.8 reduce_sum.9
Async XLA Ops:
  0.6 1.0 copy-start
  1.7 1.0 copy-start.2
  2.7 1.0 copy-start.4
  3.8 1.0 copy-start.6
  4.8 0.7 copy-start.7
  5.5 0.7 copy-start.9
  6.1 0.7 copy-start.11
  48.1 5.1 %collective-permute-start = (s16[272,128]{1,0:T(8,128)(2,1)S(1)}, s16[272,128]{1,0:T(8,128)(2,1)S(1)}, u32[]{:S(2)}, u32[]{:S(2)}) collective-permute-start(s16[272,128]{1,0:T(8,128)(2,1)S(1)} %get-tuple-element.13), channel_id=1, source_target_pairs={{0,8},{8,16},{16,24},{24,0},{1,9},{9,17},{17,25},{25,1},{2,10},{10... | collective-permute-start | bytes 208904 | tf_op jit(solution)/shard_map/ppermute | solution.py:313
  49.4 5.1 %collective-permute-start.1 = (s16[272,128]{1,0:T(8,128)(2,1)S(1)}, s16[272,128]{1,0:T(8,128)(2,1)S(1)}, u32[]{:S(2)}, u32[]{:S(2)}) collective-permute-start(s16[272,128]{1,0:T(8,128)(2,1)S(1)} %get-tuple-element.14), channel_id=1, source_target_pairs={{0,16},{8,24},{16,0},{24,8},{1,17},{9,25},{17,1},{25,9},{2,18},{10... | collective-permute-start | bytes 208904 | tf_op jit(solution)/shard_map/ppermute | solution.py:313
  52.1 3.5 %collective-permute-start.2 = (s16[272,128]{1,0:T(8,128)(2,1)S(1)}, s16[272,128]{1,0:T(8,128)(2,1)S(1)}, u32[]{:S(2)}, u32[]{:S(2)}) collective-permute-start(s16[272,128]{1,0:T(8,128)(2,1)S(1)} %get-tuple-element.15), channel_id=1, source_target_pairs={{0,24},{8,0},{16,8},{24,16},{1,25},{9,1},{17,9},{25,17},{2,26},{10... | collective-permute-start | bytes 208904 | tf_op jit(solution)/shard_map/ppermute | solution.py:313
  56.6 28.8 %copy-start.1 = (bf16[1,128,2048]{2,1,0:T(8,128)(2,1)S(1)}, bf16[1,128,2048]{2,1,0:T(8,128)(2,1)}, u32[]{:S(2)}) copy-start(bf16[1,128,2048]{2,1,0:T(8,128)(2,1)} %query_ref.3) | copy-start | bytes 1572868
  56.6 28.8 %copy-start.3 = (bf16[1,128,2048]{2,1,0:T(8,128)(2,1)S(1)}, bf16[1,128,2048]{2,1,0:T(8,128)(2,1)}, u32[]{:S(2)}) copy-start(bf16[1,128,2048]{2,1,0:T(8,128)(2,1)} %key_ref.3) | copy-start | bytes 1572868
  56.6 28.8 %copy-start.5 = (bf16[1,128,2048]{2,1,0:T(8,128)(2,1)S(1)}, bf16[1,128,2048]{2,1,0:T(8,128)(2,1)}, u32[]{:S(2)}) copy-start(bf16[1,128,2048]{2,1,0:T(8,128)(2,1)} %value_ref.3) | copy-start | bytes 1572868
  56.6 28.8 %copy-start.8 = (bf16[1,128,16]{1,2,0:T(8,128)(2,1)S(1)}, bf16[1,128,16]{1,2,0:T(8,128)(2,1)}, u32[]{:S(2)}) copy-start(bf16[1,128,16]{1,2,0:T(8,128)(2,1)} %param.11) | copy-start | bytes 12292
  56.6 28.8 %copy-start.10 = (f32[16]{0:T(128)S(1)}, f32[16]{0:T(128)}, u32[]{:S(2)}) copy-start(f32[16]{0:T(128)} %param.12) | copy-start | bytes 196
  56.6 28.8 %copy-start.12 = (s32[1,4]{1,0:T(1,128)S(1)}, s32[1,4]{1,0:T(1,128)}, u32[]{:S(2)}) copy-start(s32[1,4]{1,0:T(1,128)} %offsets_ref.3) | copy-start | bytes 52

commit v2 on v1

--- a/solution.py
+++ b/solution.py
@@ -17,9 +17,9 @@
 I16 = jnp.int16
 VMEM = pl.BlockSpec(memory_space=pltpu.VMEM)
 SMEM = pl.BlockSpec(memory_space=pltpu.SMEM)
-HBM = pl.BlockSpec(memory_space=pl.ANY)
+HBM = pl.BlockSpec(memory_space=pltpu.HBM)
 HIGHEST = lax.Precision.HIGHEST
-PARAMS = pltpu.CompilerParams(vmem_limit_bytes=48 * 1024 * 1024)
+PARAMS = pltpu.CompilerParams(vmem_limit_bytes=20 * 1024 * 1024)
 
 
 def dot(a, b, over, precision=None):
@@ -119,24 +119,30 @@
     return first, logits, step, causal, cumulative, doc, entry, tail, passes
 
 
-def states_kernel(
-    query_ref, key_ref, value_ref, dout_ref, gate_ref, bias_ref, offsets_ref, pay_ref, held, sems
-):
-    heads = bias_ref.shape[1]
+def fetch(refs, held, sems):
     parts = sems.shape[1]
-    width = query_ref.shape[2] // parts
+    width = held.shape[2] // parts
     copies = [
         [
             pltpu.make_async_copy(
                 ref.at[0, :, pl.ds(p * width, width)], held.at[i, :, pl.ds(p * width, width)], sems.at[i, p]
             )
-            for i, ref in enumerate((query_ref, key_ref, value_ref, dout_ref))
+            for i, ref in enumerate(refs)
         ]
         for p in range(parts)
     ]
     for group in copies:
         for copy in group:
             copy.start()
+    return copies
+
+
+def states_kernel(
+    query_ref, key_ref, value_ref, dout_ref, gate_ref, bias_ref, offsets_ref, pay_ref, held, sems
+):
+    heads = bias_ref.shape[1]
+    parts = sems.shape[1]
+    copies = fetch((query_ref, key_ref, value_ref, dout_ref), held, sems)
     _, _, _, _, cumulative, _, entry, tail, passes = decays(gate_ref, bias_ref, offsets_ref)
     coarse, fine = log_parts(jnp.where(passes, jnp.maximum(cumulative[-1:, :], -120.0), -128.0))
     powers = {}
@@ -217,27 +223,64 @@
         out_ref[c, tail_of(out_ref), :] = rows16(*powers[c])
 
 
-def grads_kernel(
-    query_ref, key_ref, value_ref, dout_ref, gate_ref, bias_ref, offsets_ref, state_ref,
-    dq_ref, dk_ref, dv_ref, dgate_ref, dbias_ref,
+def local_kernel(
+    query_ref, key_ref, value_ref, dout_ref, gate_ref, bias_ref, offsets_ref,
+    dq_ref, dk_ref, dv_ref, sums_ref, held, sems,
 ):
     heads, length = gate_ref.shape[1:]
-    first, logits, step, causal, cumulative, doc, entry, tail, passes = decays(
-        gate_ref, bias_ref, offsets_ref
-    )
+    parts = sems.shape[1]
+    copies = fetch((query_ref, key_ref, value_ref, dout_ref), held, sems)
+    first, _, step, causal, cumulative, doc, _, _, _ = decays(gate_ref, bias_ref, offsets_ref)
     cumulative_row = nt(step, causal.astype(F32), HIGHEST)
     linked = causal & (doc == doc_of(first + iota((1, length), 1), offsets_ref))
     lane = iota((length, heads), 1)
     sublane = iota((heads, length), 0)
     ends = jnp.zeros((length, heads), F32)
+    ends_row = jnp.zeros((heads, length), F32)
+    for h in range(heads):
+        if h % (heads // parts) == 0:
+            for copy in copies[h // (heads // parts)]:
+                copy.wait()
+        cols = matrix(h)
+        q, k, v, d = (held[i, :, cols] for i in range(4))
+        weights = jnp.where(
+            linked,
+            jnp.exp(jnp.where(linked, cumulative[:, h : h + 1] - cumulative_row[h : h + 1, :], 0.0)),
+            0.0,
+        ) * SCALE
+        probs = nt(q, k) * weights
+        dprobs = nt(d, v)
+        pairs = probs * dprobs
+        probs = probs.astype(BF16)
+        dscores = (dprobs * weights).astype(BF16)
+        dq_ref[:, cols] = nn(dscores, k)
+        dk_ref[:, cols] = tn(dscores, q)
+        dv_ref[:, cols] = tn(probs, d)
+        ends = jnp.where(lane == h, jnp.sum(pairs, axis=1, keepdims=True), ends)
+        ends_row = jnp.where(sublane == h, jnp.sum(pairs, axis=0, keepdims=True), ends_row)
+    causal = causal.astype(F32)
+    sums_ref[...] = tn(ends, causal, HIGHEST) - nn(ends_row, causal, HIGHEST)
+
+
+def gates_kernel(
+    query_ref, key_ref, value_ref, dout_ref, gate_ref, bias_ref, offsets_ref, sums_ref, state_ref,
+    dgate_ref, dbias_ref, held, sems,
+):
+    heads, length = gate_ref.shape[1:]
+    parts = sems.shape[1]
+    copies = fetch((query_ref, key_ref, value_ref, dout_ref), held, sems)
+    _, logits, _, causal, cumulative, _, entry, tail, passes = decays(gate_ref, bias_ref, offsets_ref)
+    lane = iota((length, heads), 1)
+    same = iota((heads, heads), 0) == iota((heads, heads), 1)
+    ends = jnp.zeros((length, heads), F32)
     starts = jnp.zeros((length, heads), F32)
-    ends_row = jnp.zeros((heads, length), F32)
-    whole = jnp.zeros((heads, 1), F32)
+    whole = jnp.zeros((1, heads), F32)
     for h in range(heads):
+        if h % (heads // parts) == 0:
+            for copy in copies[h // (heads // parts)]:
+                copy.wait()
         cols = matrix(h)
         one = slice(h, h + 1)
-        q, k, v, d = (ref[0, :, cols] for ref in (query_ref, key_ref, value_ref, dout_ref))
-        q32, k32 = q.astype(F32), k.astype(F32)
         slot, m = divmod(h, 2)
         powers = wide(state_ref[slot, tail_of(state_ref), :])
         state32, grad32 = (
@@ -245,41 +288,50 @@
         )
         state, state_low = split2(state32)
         grad, grad_low = split2(grad32)
-        weights = jnp.where(
-            linked, jnp.exp(jnp.where(linked, cumulative[:, one] - cumulative_row[one, :], 0.0)), 0.0
-        ) * SCALE
-        probs = nt(q, k) * weights
-        dprobs = nt(d, v)
-        pairs = probs * dprobs
-        probs = probs.astype(BF16)
-        dscores = (dprobs * weights).astype(BF16)
-        dq_inter = (entry[:, one] * SCALE) * (nt(d, state) + nt(d, state_low))
-        dk_inter = tail[:, one] * (nt(v, grad) + nt(v, grad_low))
-        dq_ref[0, :, cols] = (nn(dscores, k) + dq_inter).astype(BF16)
-        dk_ref[0, :, cols] = (tn(dscores, q) + dk_inter).astype(BF16)
-        dv_ref[0, :, cols] = (tn(probs, d) + tail[:, one] * nn(k, grad)).astype(BF16)
-        at_end = jnp.sum(pairs + q32 * dq_inter, axis=1, keepdims=True)
-        at_start = jnp.sum(k32 * dk_inter, axis=1, keepdims=True)
-        product = jnp.sum(state32 * grad32, keepdims=True)
+        q, k, v, d = (held[i, :, cols] for i in range(4))
+        dq = (entry[:, one] * SCALE) * (nt(d, state) + nt(d, state_low))
+        dk = tail[:, one] * (nt(v, grad) + nt(v, grad_low))
+        at_end = jnp.sum(q.astype(F32) * dq, axis=1, keepdims=True)
+        at_start = jnp.sum(k.astype(F32) * dk, axis=1, keepdims=True)
         ends = jnp.where(lane == h, at_end, ends)
         starts = jnp.where(lane == h, at_start, starts)
-        ends_row = jnp.where(sublane == h, jnp.sum(pairs, axis=0, keepdims=True), ends_row)
-        whole = jnp.where(sublane[:, :1] == h, product, whole)
-    through = jnp.where(passes, jnp.exp(cumulative_row[:, length - 1 :]), 0.0)
-    causal = causal.astype(F32)
+        whole = jnp.where(lane[0:1] == h, jnp.sum(state32 * grad32, keepdims=True), whole)
+    through = jnp.where(passes, jnp.exp(cumulative[length - 1 :, :]), 0.0) * whole
     earlier = (iota((length, length), 0) < iota((length, length), 1)).astype(F32)
     dstep = (
-        tn(ends, causal, HIGHEST)
-        - nn(ends_row, causal, HIGHEST)
+        sums_ref[...]
+        + tn(ends, causal.astype(F32), HIGHEST)
         + tn(starts, earlier, HIGHEST)
-        + through * whole
+        + jnp.sum(jnp.where(same, through, 0.0), axis=1, keepdims=True)
     )
     dlogit = -dstep / (1.0 + jnp.exp(-logits))
     dgate_ref[0] = dlogit.astype(BF16)
-    same = iota((heads, heads), 0) == iota((heads, heads), 1)
     dbias_ref[...] = jnp.sum(
         jnp.where(same, jnp.sum(dlogit, axis=1, keepdims=True), 0.0), axis=0, keepdims=True
     )
+
+
+def output_kernel(
+    key_ref, value_ref, dout_ref, gate_ref, bias_ref, offsets_ref, state_ref, dq_near_ref, dk_near_ref,
+    dv_near_ref, dq_ref, dk_ref, dv_ref,
+):
+    heads = bias_ref.shape[1]
+    _, _, _, _, _, _, entry, tail, _ = decays(gate_ref, bias_ref, offsets_ref)
+    for h in range(heads):
+        cols = matrix(h)
+        one = slice(h, h + 1)
+        slot, m = divmod(h, 2)
+        powers = wide(state_ref[slot, tail_of(state_ref), :])
+        state, grad = (
+            decode(state_ref[slot, matrix(place), :], powers[place : place + 1]).astype(BF16)
+            for place in (m, 2 + m)
+        )
+        for near_ref, out_ref, far, decay in (
+            (dq_near_ref, dq_ref, nt(dout_ref[0, :, cols], state), entry[:, one] * SCALE),
+            (dk_near_ref, dk_ref, nt(value_ref[0, :, cols], grad), tail[:, one]),
+            (dv_near_ref, dv_ref, nn(key_ref[0, :, cols], grad), tail[:, one]),
+        ):
+            out_ref[0, :, cols] = (near_ref[:, cols] + decay * far).astype(BF16)
 
 
 def call(kernel, out_shape, in_specs, **more):
@@ -299,13 +351,16 @@
     count, segments = lax.axis_size("grp"), lax.axis_size("seg")
     gates = jnp.swapaxes(gate_in, 1, 2)
     rest = (gates, gate_bias.reshape(1, heads), offsets)
+    inputs = tuple(pltpu.with_memory_space_constraint(x, pltpu.HBM) for x in (query, key, value, dout)) + rest
+    fetched = [HBM] * 4 + [VMEM] * 2 + [SMEM]
+    scratch = [pltpu.VMEM((4,) + query.shape[1:], BF16), pltpu.SemaphoreType.DMA((4, 4))]
     packed = jax.ShapeDtypeStruct((count, 4 * HEAD_DIM + TAIL, LANES), I16)
     pay = call(
         states_kernel,
         packed,
-        [HBM] * 4 + [VMEM] * 2 + [SMEM],
-        scratch_shapes=[pltpu.VMEM((4,) + query.shape[1:], BF16), pltpu.SemaphoreType.DMA((4, 4))],
-    )(query, key, value, dout, *rest)
+        fetched,
+        scratch_shapes=scratch,
+    )(*inputs)
     pay = lax.all_to_all(pay, "grp", split_axis=0, concat_axis=0, tiled=True)
     total = jax.ShapeDtypeStruct((2 * HEAD_DIM + TAIL, LANES), I16)
     sends = call(totals_kernel, (total,) * (segments - 1), [VMEM])(pay)
@@ -315,20 +370,21 @@
     ]
     carried = call(scan_kernel, packed, [VMEM] * segments)(pay, *got)
     carried = lax.all_to_all(carried, "grp", split_axis=0, concat_axis=0, tiled=True)
-    like = jax.ShapeDtypeStruct(query.shape, BF16)
-    dq, dk, dv, dgate, dbias = call(
-        grads_kernel,
-        (
-            like,
-            like,
-            like,
-            jax.ShapeDtypeStruct(gates.shape, BF16),
-            jax.ShapeDtypeStruct((1, heads), F32),
-        ),
-        [VMEM] * 6 + [SMEM, VMEM],
-    )(query, key, value, dout, *rest, carried)
+    wide_like = jax.ShapeDtypeStruct(query.shape[1:], F32)
+    sums_like = jax.ShapeDtypeStruct(gates.shape[1:], F32)
+    *near, sums = call(local_kernel, (wide_like,) * 3 + (sums_like,), fetched, scratch_shapes=scratch)(*inputs)
+    dgate, dbias = call(
+        gates_kernel,
+        (jax.ShapeDtypeStruct(gates.shape, BF16), jax.ShapeDtypeStruct((1, heads), F32)),
+        fetched + [VMEM, VMEM],
+        scratch_shapes=scratch,
+    )(*inputs, sums, carried)
     everywhere = lax.all_to_all(
         jnp.broadcast_to(dbias[None], (lax.axis_size(ALL), 1, heads)), ALL, split_axis=0, concat_axis=0, tiled=True
+    )
+    like = jax.ShapeDtypeStruct(query.shape, BF16)
+    dq, dk, dv = call(output_kernel, (like,) * 3, [VMEM] * 5 + [SMEM] + [VMEM] * 4)(
+        key, value, dout, *rest, carried, *near
     )
     return dq, dk, dv, jnp.swapaxes(dgate, 1, 2), jnp.sum(everywhere, axis=(0, 1))
 

time: 119 us -> 115 us (0.966)
  blocking collectives: 90.1 us -> 36.5 us
  waiting for transfers between devices: 2.38 us -> 26.2 us
  starting transfers between devices: 5.08 us -> 19.6 us
  Pallas kernels: 12.9 us -> 21.6 us
  local copies, waits for them, and re-layouts: 6.26 us -> 9.31 us
    all_to_all x2 -> x0, blocking collectives: 53.7 us -> none  [the longest x1 28.8 us: shards(): lax.all_to_all(carried, 'grp', split_axis=0, concat_axis=0, tiled=True)]
    all_to_all x0 -> x2, waiting for transfers between devices: none -> 23.8 us  [the longest x1 17.4 us: shards(): lax.all_to_all(carried, 'grp', split_axis=0, concat_axis=0, tiled=True)]
    all_to_all x0 -> x2, starting transfers between devices: none -> 14.6 us  [the longest x1 10.8 us: shards(): lax.all_to_all(jnp.broadcast_to(dbias[None], (lax.axis_size(ALL), 1, head...]
    pallas_call x2 -> x4, Pallas kernels: 11.3 us -> 19.1 us  [the longest x1 6.14 us: shards(): call(local_kernel, (wide_like,) * 3 + (sums_like,), fetched, scratch_shap...]
    unnamed x26 -> x30, local copies, waits for them, and re-layouts: 6.19 us -> 8.59 us
  transfers between devices with their start and end apart: 3 -> 5, of which waited for: 2 -> 4; matrix products, arithmetic and copies ran while one was open for 0% -> 0% of each run, Pallas kernels for 0% -> 8%
where the time goes in v2:
time: 115 us
  blocking collectives  36.5 us (32%)
  waiting for transfers between devices  26.2 us (23%)
  Pallas kernels  21.6 us (19%)
  starting transfers between devices  19.6 us (17%)
  local copies, waits for them, and re-layouts  9.31 us (8%)
    all_to_all x1, blocking collectives, shards(): pay = lax.all_to_all(pay, 'grp', split_axis=0, concat_axis=0, tiled=True)  36.5 us
    all_to_all x1, waiting for transfers between devices, shards(): lax.all_to_all(carried, 'grp', split_axis=0, concat_axis=0, tiled=True)  17.4 us
    all_to_all x1, starting transfers between devices, shards(): lax.all_to_all(jnp.broadcast_to(dbias[None], (lax.axis_size(ALL), 1, head...  10.8 us
    unnamed x30, local copies, waits for them, and re-layouts  8.59 us
    all_to_all x1, waiting for transfers between devices, shards(): lax.all_to_all(jnp.broadcast_to(dbias[None], (lax.axis_size(ALL), 1, head...  6.42 us
    pallas_call x1, Pallas kernels, shards(): call(local_kernel, (wide_like,) * 3 + (sums_like,), fetched, scratch_shap...  6.14 us
    pallas_call x1, Pallas kernels, shards(): call(gates_kernel, (jax.ShapeDtypeStruct(gates.shape, BF16), jax.ShapeDty...  5.36 us
    ppermute x3, starting transfers between devices, shards(): lax.ppermute(send, 'seg', [(i, (i + d) % segments) for i in range(segment...  5.04 us
  transfers between devices with their start and end apart: 5, of which 4 were waited for; matrix products, arithmetic and copies ran while one was open for 0% of the time, Pallas kernels for 8%

profile of v2, /device:TPU:1, one launch (start us, length us, event | category | flops | bytes accessed | tf_op | source)
XLA Modules:
  0.0 114.7 jit_solution(5096738745262296967)
XLA Ops:
  0.6 0.0 copy-start.9
  0.6 0.7 copy-done.9
  1.3 0.0 copy-start.11
  1.3 0.7 copy-done.11
  2.0 0.0 copy-start.13
  2.0 0.7 copy-done.13
  2.6 4.6 %shard_map.110 = s16[8,528,128]{2,1,0:T(8,128)(2,1)S(1)} custom-call(bf16[1,128,2048]{2,1,0:T(8,128)(2,1)} %query_ref.5, bf16[1,128,2048]{2,1,0:T(8,128)(2,1)} %key_ref.7, bf16[1,128,2048]{2,1,0:T(8,128)(2,1)} %value_ref.7, bf16[1,128,2048]{2,1,0:T(8,128)(2,1)} %dout_ref.7, bf16[1,16,128]{2,1,0:T(8,128)(2,1)S(1)} %bitcast.4, f32[1,16]{1,0:T(1,128)S(1)} %bitcast.8, ...), custom_call_target="tpu_custom_call" | custom-call | tf_op jit(solution)/shard_map/pallas_call | solution.py:358
  7.3 36.5 %all_to_all.15.pay_ref = s16[8,528,128]{2,1,0:T(8,128)(2,1)S(1)} all-to-all(s16[8,528,128]{2,1,0:T(8,128)(2,1)S(1)} %shard_map.110), channel_id=1, replica_groups=mesh['dp'=8,'seg'=4,'grp'=8] {'grp'}, dimensions={0} | all-to-all | bytes 2162688 | tf_op jit(solution)/shard_map/all_to_all | solution.py:364
  43.8 0.5 shard_map.111
  44.3 1.4 %collective-permute-start = (s16[272,128]{1,0:T(8,128)(2,1)S(1)}, s16[272,128]{1,0:T(8,128)(2,1)S(1)}, u32[]{:S(2)}, u32[]{:S(2)}) collective-permute-start(s16[272,128]{1,0:T(8,128)(2,1)S(1)} %get-tuple-element.17), channel_id=1, source_target_pairs={{0,8},{8,16},{16,24},{24,0},{1,9},{9,17},{17,25},{25,1},{2,10},{10... | collective-permute-start | bytes 208904 | tf_op jit(solution)/shard_map/ppermute | solution.py:368
  45.7 2.6 %collective-permute-start.1 = (s16[272,128]{1,0:T(8,128)(2,1)S(1)}, s16[272,128]{1,0:T(8,128)(2,1)S(1)}, u32[]{:S(2)}, u32[]{:S(2)}) collective-permute-start(s16[272,128]{1,0:T(8,128)(2,1)S(1)} %get-tuple-element.18), channel_id=1, source_target_pairs={{0,16},{8,24},{16,0},{24,8},{1,17},{9,25},{17,1},{25,9},{2,18},{10... | collective-permute-start | bytes 208904 | tf_op jit(solution)/shard_map/ppermute | solution.py:368
  48.3 1.1 collective-permute-start.2
  49.3 0.0 collective-permute-done.refs_0_
  49.3 1.4 %collective-permute-done.1.refs_1_ = s16[272,128]{1,0:T(8,128)(2,1)S(1)} collective-permute-done((s16[272,128]{1,0:T(8,128)(2,1)S(1)}, s16[272,128]{1,0:T(8,128)(2,1)S(1)}, u32[]{:S(2)}, u32[]{:S(2)}) %collective-permute-start.1) | collective-permute-done | bytes 69664 | tf_op jit(solution)/shard_map/ppermute | solution.py:368
  50.7 1.0 collective-permute-done.2.refs_2_
  51.7 2.0 %shard_map.112 = s16[8,528,128]{2,1,0:T(8,128)(2,1)} custom-call(s16[8,528,128]{2,1,0:T(8,128)(2,1)S(1)} %all_to_all.15.pay_ref, s16[272,128]{1,0:T(8,128)(2,1)S(1)} %collective-permute-done.refs_0_, s16[272,128]{1,0:T(8,128)(2,1)S(1)} %collective-permute-done.1.refs_1_, s16[272,128]{1,0:T(8,128)(2,1)S(1)} %collective-permute-done.2.refs_2_), custom_call_target="tpu_custom_call" | custom-call | tf_op jit(solution)/shard_map/pallas_call | solution.py:371
  53.7 0.0 copy-start.10
  53.8 0.0 copy-start.12
  53.8 3.8 %all-to-all-start.1 = ((s16[8,528,128]{2,1,0:T(8,128)(2,1)}), s16[8,528,128]{2,1,0:T(8,128)(2,1)S(1)}, u32[]{:S(2)}, u32[]{:S(2)}) async-start(s16[8,528,128]{2,1,0:T(8,128)(2,1)} %shard_map.112), calls=%async_computation.1 | async-start | bytes 2162688 | tf_op jit(solution)/shard_map/all_to_all | solution.py:372
  57.5 0.0 copy-done.10
  57.5 0.0 copy-done.12
  57.5 0.0 copy-done.14
  57.5 6.1 %shard_map.113 = (f32[128,2048]{1,0:T(8,128)S(1)}, f32[128,2048]{1,0:T(8,128)S(1)}, f32[128,2048]{1,0:T(8,128)S(1)}, f32[16,128]{1,0:T(8,128)S(1)}) custom-call(bf16[1,128,2048]{2,1,0:T(8,128)(2,1)} %query_ref.5, bf16[1,128,2048]{2,1,0:T(8,128)(2,1)} %key_ref.7, bf16[1,128,2048]{2,1,0:T(8,128)(2,1)} %value_ref.7, bf16[1,128,2048]{2,1,0:T(8,128)(2,1)} %dout_ref.7, ...), custom_call_target="tpu_custom_call" | custom-call | tf_op jit(solution)/shard_map/pallas_call | solution.py:375
  63.7 0.0 copy-start.3
  63.7 1.0 copy-done.3
  64.6 0.0 copy-start.5
  64.6 1.0 copy-done.5
  65.6 0.0 copy-start.7
  65.6 1.0 copy-done.7
  66.6 17.4 %all-to-all-done.1.state_ref = s16[8,528,128]{2,1,0:T(8,128)(2,1)S(1)} async-done(((s16[8,528,128]{2,1,0:T(8,128)(2,1)}), s16[8,528,128]{2,1,0:T(8,128)(2,1)S(1)}, u32[]{:S(2)}, u32[]{:S(2)}) %all-to-all-start.1) | async-done | bytes 1081376 | tf_op jit(solution)/shard_map/all_to_all | solution.py:372
  84.0 0.0 copy-start
  84.0 0.0 copy-start.1
  84.0 0.0 copy-start.2
  84.0 5.4 %shard_map.115 = (bf16[1,16,128]{2,1,0:T(8,128)(2,1)}, f32[1,16]{1,0:T(1,128)S(1)}) custom-call(bf16[1,128,2048]{2,1,0:T(8,128)(2,1)} %query_ref.5, bf16[1,128,2048]{2,1,0:T(8,128)(2,1)} %key_ref.7, bf16[1,128,2048]{2,1,0:T(8,128)(2,1)} %value_ref.7, bf16[1,128,2048]{2,1,0:T(8,128)(2,1)} %dout_ref.7, bf16[1,16,128]{2,1,0:T(8,128)(2,1)S(1)} %bitcast.6, ...), custom_call_target="tpu_custom_call" | custom-call | tf_op jit(solution)/shard_map/pallas_call | solution.py:376
  89.3 0.7 broadcast_in_dim.9
  90.1 10.8 %all-to-all-start.2 = ((f32[256,1,16]{2,1,0:T(1,128)}), f32[256,1,16]{2,1,0:T(1,128)S(1)}, u32[]{:S(2)}, u32[]{:S(2)}) async-start(f32[256,1,16]{2,1,0:T(1,128)} %broadcast_in_dim.9), calls=%async_computation.2 | async-start | bytes 262144 | tf_op jit(solution)/shard_map/all_to_all | solution.py:382
  100.9 0.0 copy-done
  100.9 0.0 copy-done.1
  100.9 0.0 copy-done.2
  100.9 0.0 copy-start.4
  100.9 1.2 %copy-done.4 = f32[128,2048]{1,0:T(8,128)S(1)} copy-done((f32[128,2048]{1,0:T(8,128)S(1)}, f32[128,2048]{1,0:T(8,128)}, u32[]{:S(2)}) %copy-start.4) | copy-done | bytes 1048600
  102.1 0.0 copy-start.6
  102.2 1.2 %copy-done.6 = f32[128,2048]{1,0:T(8,128)S(1)} copy-done((f32[128,2048]{1,0:T(8,128)S(1)}, f32[128,2048]{1,0:T(8,128)}, u32[]{:S(2)}) %copy-start.6) | copy-done | bytes 1048600
  103.4 0.0 copy-start.8
  103.4 1.2 %copy-done.8 = f32[128,2048]{1,0:T(8,128)S(1)} copy-done((f32[128,2048]{1,0:T(8,128)S(1)}, f32[128,2048]{1,0:T(8,128)}, u32[]{:S(2)}) %copy-start.8) | copy-done | bytes 1048600
  104.6 2.9 %shard_map.114 = (bf16[1,128,2048]{2,1,0:T(8,128)(2,1)}, bf16[1,128,2048]{2,1,0:T(8,128)(2,1)}, bf16[1,128,2048]{2,1,0:T(8,128)(2,1)}) custom-call(bf16[1,128,2048]{2,1,0:T(8,128)(2,1)S(1)} %copy-done, bf16[1,128,2048]{2,1,0:T(8,128)(2,1)S(1)} %copy-done.1, bf16[1,128,2048]{2,1,0:T(8,128)(2,1)S(1)} %copy-done.2, bf16[1,16,128]{2,1,0:T(8,128)(2,1)S(1)} %bitcast.7, ...), custom_call_target="tpu_custom_call" | custom-call | tf_op jit(solution)/shard_map/pallas_call | solution.py:386
  107.5 6.4 %all-to-all-done.2 = f32[256,1,16]{2,1,0:T(1,128)S(1)} async-done(((f32[256,1,16]{2,1,0:T(1,128)}), f32[256,1,16]{2,1,0:T(1,128)S(1)}, u32[]{:S(2)}, u32[]{:S(2)}) %all-to-all-start.2) | async-done | bytes 16416 | tf_op jit(solution)/shard_map/all_to_all | solution.py:382
  113.9 0.8 reduce_sum.9
  (1 shorter events, 0.0 us)
Async XLA Ops:
  0.6 0.7 copy-start.9
  1.3 0.7 copy-start.11
  2.0 0.7 copy-start.13
  44.3 5.0 %collective-permute-start = (s16[272,128]{1,0:T(8,128)(2,1)S(1)}, s16[272,128]{1,0:T(8,128)(2,1)S(1)}, u32[]{:S(2)}, u32[]{:S(2)}) collective-permute-start(s16[272,128]{1,0:T(8,128)(2,1)S(1)} %get-tuple-element.17), channel_id=1, source_target_pairs={{0,8},{8,16},{16,24},{24,0},{1,9},{9,17},{17,25},{25,1},{2,10},{10... | collective-permute-start | bytes 208904 | tf_op jit(solution)/shard_map/ppermute | solution.py:368
  45.7 5.0 %collective-permute-start.1 = (s16[272,128]{1,0:T(8,128)(2,1)S(1)}, s16[272,128]{1,0:T(8,128)(2,1)S(1)}, u32[]{:S(2)}, u32[]{:S(2)}) collective-permute-start(s16[272,128]{1,0:T(8,128)(2,1)S(1)} %get-tuple-element.18), channel_id=1, source_target_pairs={{0,16},{8,24},{16,0},{24,8},{1,17},{9,25},{17,1},{25,9},{2,18},{10... | collective-permute-start | bytes 208904 | tf_op jit(solution)/shard_map/ppermute | solution.py:368
  48.3 3.5 %collective-permute-start.2 = (s16[272,128]{1,0:T(8,128)(2,1)S(1)}, s16[272,128]{1,0:T(8,128)(2,1)S(1)}, u32[]{:S(2)}, u32[]{:S(2)}) collective-permute-start(s16[272,128]{1,0:T(8,128)(2,1)S(1)} %get-tuple-element.19), channel_id=1, source_target_pairs={{0,24},{8,0},{16,8},{24,16},{1,25},{9,1},{17,9},{25,17},{2,26},{10... | collective-permute-start | bytes 208904 | tf_op jit(solution)/shard_map/ppermute | solution.py:368
  53.7 3.8 %copy-start.10 = (bf16[1,128,16]{1,2,0:T(8,128)(2,1)S(1)}, bf16[1,128,16]{1,2,0:T(8,128)(2,1)}, u32[]{:S(2)}) copy-start(bf16[1,128,16]{1,2,0:T(8,128)(2,1)} %param.11) | copy-start | bytes 12292
  53.8 3.8 %copy-start.12 = (f32[16]{0:T(128)S(1)}, f32[16]{0:T(128)}, u32[]{:S(2)}) copy-start(f32[16]{0:T(128)} %param.12) | copy-start | bytes 196
  53.8 3.8 %copy-start.14 = (s32[1,4]{1,0:T(1,128)S(1)}, s32[1,4]{1,0:T(1,128)}, u32[]{:S(2)}) copy-start(s32[1,4]{1,0:T(1,128)} %offsets_ref.7) | copy-start | bytes 52
  53.8 30.2 %all-to-all-start.1 = ((s16[8,528,128]{2,1,0:T(8,128)(2,1)}), s16[8,528,128]{2,1,0:T(8,128)(2,1)S(1)}, u32[]{:S(2)}, u32[]{:S(2)}) async-start(s16[8,528,128]{2,1,0:T(8,128)(2,1)} %shard_map.112), calls=%async_computation.1 | async-start | bytes 2162688 | tf_op jit(solution)/shard_map/all_to_all | solution.py:372
  63.7 1.0 copy-start.3
  64.6 1.0 copy-start.5
  65.6 1.0 copy-start.7
  84.0 16.9 %copy-start = (bf16[1,128,2048]{2,1,0:T(8,128)(2,1)S(1)}, bf16[1,128,2048]{2,1,0:T(8,128)(2,1)}, u32[]{:S(2)}) copy-start(bf16[1,128,2048]{2,1,0:T(8,128)(2,1)} %key_ref.7) | copy-start | bytes 1572868
  84.0 16.9 %copy-start.1 = (bf16[1,128,2048]{2,1,0:T(8,128)(2,1)S(1)}, bf16[1,128,2048]{2,1,0:T(8,128)(2,1)}, u32[]{:S(2)}) copy-start(bf16[1,128,2048]{2,1,0:T(8,128)(2,1)} %value_ref.7) | copy-start | bytes 1572868
  84.0 16.9 %copy-start.2 = (bf16[1,128,2048]{2,1,0:T(8,128)(2,1)S(1)}, bf16[1,128,2048]{2,1,0:T(8,128)(2,1)}, u32[]{:S(2)}) copy-start(bf16[1,128,2048]{2,1,0:T(8,128)(2,1)} %dout_ref.7) | copy-start | bytes 1572868
  90.1 23.9 %all-to-all-start.2 = ((f32[256,1,16]{2,1,0:T(1,128)}), f32[256,1,16]{2,1,0:T(1,128)S(1)}, u32[]{:S(2)}, u32[]{:S(2)}) async-start(f32[256,1,16]{2,1,0:T(1,128)} %broadcast_in_dim.9), calls=%async_computation.2 | async-start | bytes 262144 | tf_op jit(solution)/shard_map/all_to_all | solution.py:382
  100.9 1.2 %copy-start.4 = (f32[128,2048]{1,0:T(8,128)S(1)}, f32[128,2048]{1,0:T(8,128)}, u32[]{:S(2)}) copy-start(f32[128,2048]{1,0:T(8,128)} %copy-done.3) | copy-start | bytes 3145732
  102.1 1.2 %copy-start.6 = (f32[128,2048]{1,0:T(8,128)S(1)}, f32[128,2048]{1,0:T(8,128)}, u32[]{:S(2)}) copy-start(f32[128,2048]{1,0:T(8,128)} %copy-done.5) | copy-start | bytes 3145732
  103.4 1.2 %copy-start.8 = (f32[128,2048]{1,0:T(8,128)S(1)}, f32[128,2048]{1,0:T(8,128)}, u32[]{:S(2)}) copy-start(f32[128,2048]{1,0:T(8,128)} %copy-done.7) | copy-start | bytes 3145732

commit v3 on v2

v3 whole, which is shorter than its diff:
```python
import jax
import jax.numpy as jnp
from jax import lax
from jax.experimental import pallas as pl
from jax.experimental.pallas import tpu as pltpu
from jax.sharding import PartitionSpec as P

HEAD_DIM = 128
SCALE = HEAD_DIM ** (-0.5)
DOCS = 4
LINE = ("seg", "grp")
ALL = ("dp", "seg", "grp")
TAIL = 16
LANES = 128
F32 = jnp.float32
BF16 = jnp.bfloat16
I16 = jnp.int16
VMEM = pl.BlockSpec(memory_space=pltpu.VMEM)
SMEM = pl.BlockSpec(memory_space=pltpu.SMEM)
HBM = pl.BlockSpec(memory_space=pltpu.HBM)
HIGHEST = lax.Precision.HIGHEST
PARAMS = pltpu.CompilerParams(vmem_limit_bytes=20 * 1024 * 1024)


def dot(a, b, over, precision=None):
    return lax.dot_general(
        a, b, (((over[0],), (over[1],)), ((), ())), precision=precision, preferred_element_type=F32
    )


def nn(a, b, precision=None):
    return dot(a, b, (1, 0), precision)


def nt(a, b, precision=None):
    return dot(a, b, (1, 1), precision)


def tn(a, b, precision=None):
    return dot(a, b, (0, 0), precision)


def split2(x):
    hi = x.astype(BF16)
    return hi, (x - hi.astype(F32)).astype(BF16)


def matrix(m):
    return pl.ds(m * HEAD_DIM, HEAD_DIM)


def tail_of(ref):
    return pl.ds(ref.shape[-2] - TAIL, TAIL)


def iota(shape, dim):
    return lax.broadcasted_iota(jnp.int32, shape, dim)


def whole16(x):
    return x.astype(jnp.int32).astype(I16)


def wide(x):
    return x.astype(jnp.int32).astype(F32)


def encode(x):
    top = jnp.maximum(jnp.max(jnp.abs(x), axis=0, keepdims=True), 1e-30)
    power = jnp.ceil(jnp.log2(top) * 8.0)
    return jnp.clip(jnp.floor(x * jnp.exp2(15.0 - power / 8.0) + 0.5), -32767.0, 32767.0), power


def decode(steps, power):
    return wide(steps) * jnp.exp2(power / 8.0 - 15.0)


def encode2(x):
    power = jnp.ceil(jnp.log2(jnp.maximum(jnp.abs(x), 1e-30)))
    scaled = x * jnp.exp2(14.0 - power)
    high = jnp.floor(scaled + 0.5)
    return power, high, jnp.floor((scaled - high) * 16384.0 + 0.5)


def decode2(power, high, low):
    return (high + low / 16384.0) * jnp.exp2(power - 14.0)


def log_parts(log):
    coarse = jnp.floor(log * 256.0 + 0.5)
    return coarse, jnp.floor((log - coarse / 256.0) * 8388608.0 + 0.5)


def log_whole(coarse, fine):
    return coarse / 256.0 + fine / 8388608.0


def rows16(*rows):
    at = iota((TAIL, LANES), 0)
    total = jnp.zeros((TAIL, LANES), F32)
    for i, row in enumerate(rows):
        total = jnp.where(at == i, row, total)
    return whole16(total)


def doc_of(pos, offsets_ref):
    total = (pos >= offsets_ref[0, 0]).astype(jnp.int32)
    for i in range(1, DOCS):
        total = total + (pos >= offsets_ref[0, i]).astype(jnp.int32)
    return total


def place():
    return lax.axis_index("seg") * lax.axis_size("grp") + lax.axis_index("grp")


def decays(gates, bias, offsets_ref):
    heads, length = gates.shape
    first = place() * length
    same = iota((heads, heads), 0) == iota((heads, heads), 1)
    logits = gates.astype(F32) + jnp.sum(jnp.where(same, bias, 0.0), axis=1, keepdims=True)
    step = -(jnp.maximum(logits, 0.0) + jnp.log1p(jnp.exp(-jnp.abs(logits))))
    causal = iota((length, length), 0) >= iota((length, length), 1)
    cumulative = nt(causal.astype(F32), step, HIGHEST)
    doc = doc_of(first + iota((length, 1), 0), offsets_ref)
    doc_last = doc_of(first + length - 1, offsets_ref)
    before = jnp.where(first > 0, doc_of(first - 1, offsets_ref), -1)
    entry = jnp.exp(cumulative) * (doc == before).astype(F32)
    tail = jnp.exp(cumulative[length - 1 :, :] - cumulative) * (doc == doc_last).astype(F32)
    return first, logits, step, causal, cumulative, doc, entry, tail, doc_last == before


def fetch(refs, held, sems):
    parts = sems.shape[1]
    width = held.shape[2] // parts
    copies = [
        [
            pltpu.make_async_copy(
                ref.at[0, :, pl.ds(p * width, width)], held.at[i, :, pl.ds(p * width, width)], sems.at[i, p]
            )
            for i, ref in enumerate(refs)
        ]
        for p in range(parts)
    ]
    for group in copies:
        for copy in group:
            copy.start()
    return copies


def arrive(copies, head, heads):
    each = heads // len(copies)
    if head % each == 0:
        for copy in copies[head // each]:
            copy.wait()


def states_kernel(
    query_ref, key_ref, value_ref, dout_ref, gate_ref, bias_ref, offsets_ref,
    pay_ref, held, sems, gate_held, bias_held, offsets_held, small_sems,
):
    heads = bias_ref.shape[1]
    small = [
        pltpu.make_async_copy(gate_ref.at[0], gate_held, small_sems.at[0]),
        pltpu.make_async_copy(bias_ref, bias_held, small_sems.at[1]),
        pltpu.make_async_copy(offsets_ref, offsets_held, small_sems.at[2]),
    ]
    for copy in small:
        copy.start()
    copies = fetch((query_ref, key_ref, value_ref, dout_ref), held, sems)
    for copy in small:
        copy.wait()
    _, _, _, _, cumulative, _, entry, tail, passes = decays(gate_held[...], bias_held[...], offsets_held)
    coarse, fine = log_parts(jnp.where(passes, jnp.maximum(cumulative[-1:, :], -120.0), -128.0))
    powers = {}
    for h in range(heads):
        arrive(copies, h, heads)
        cols = matrix(h)
        one = slice(h, h + 1)
        slot, m = divmod(h, 2)
        for at, left, right, weight in ((m, 1, 2, tail[:, one]), (2 + m, 0, 3, entry[:, one] * SCALE)):
            upper, lower = split2(held[left, :, cols].astype(F32) * weight)
            right = held[right, :, cols]
            steps, powers[at] = encode(tn(upper, right) + tn(lower, right))
            pay_ref[slot, matrix(at), :] = whole16(steps)
        if m == 1:
            pay_ref[slot, tail_of(pay_ref), :] = rows16(
                *(powers[i] for i in range(4)),
                *(x[:, i : i + 1] for i in (h - 1, h) for x in (coarse, fine)),
            )


def chunk_logs(tails, m):
    return [log_whole(t[4 + 2 * m : 5 + 2 * m], t[5 + 2 * m : 6 + 2 * m]) for t in tails]


def totals_kernel(pay_ref, *send_refs):
    count = pay_ref.shape[0]
    tails = [wide(pay_ref[c, tail_of(pay_ref), :]) for c in range(count)]
    mine, segments = lax.axis_index("seg"), lax.axis_size("seg")
    at = iota((8, LANES), 0)
    logs = jnp.zeros((8, LANES), F32)
    for m in range(2):
        log = chunk_logs(tails, m)
        logs = jnp.where(at == m, sum(log), logs)
        ends = []
        for where, order in ((m, range(count)), (2 + m, range(count - 1, -1, -1))):
            carry = jnp.zeros((HEAD_DIM, HEAD_DIM), F32)
            for c in order:
                carry = jnp.exp(log[c]) * carry + decode(
                    pay_ref[c, matrix(where), :], tails[c][where : where + 1]
                )
            ends.append(carry)
        for distance, send_ref in enumerate(send_refs, 1):
            send_ref[matrix(m), :] = jnp.where(mine + distance < segments, *ends)
    for send_ref in send_refs:
        send_ref[pl.ds(2 * HEAD_DIM, 8), :] = logs


def scan_kernel(pay_ref, *refs):
    *got_refs, _, out_ref, held = refs
    count = pay_ref.shape[0]
    mine = lax.axis_index("seg")
    tails = [wide(pay_ref[c, tail_of(pay_ref), :]) for c in range(count)]
    at = iota((2 * count, LANES), 0)
    flows = jnp.zeros((2 * count, LANES), F32)
    powers = [[None] * 4 for _ in range(count)]
    for m in range(2):
        log = chunk_logs(tails, m)
        sent = [(jnp.exp(ref[pl.ds(2 * HEAD_DIM + m, 1), :]), ref[matrix(m), :]) for ref in got_refs]
        state = jnp.zeros((HEAD_DIM, HEAD_DIM), F32)
        for d in range(len(sent), 0, -1):
            state = jnp.where(mine >= d, sent[d - 1][0] * state + sent[d - 1][1], state)
        grad = jnp.zeros((HEAD_DIM, HEAD_DIM), F32)
        for d in range(1, len(sent) + 1):
            grad = jnp.where(mine < d, sent[d - 1][0] * grad + sent[d - 1][1], grad)
        for where, carry, order in ((m, state, range(count)), (2 + m, grad, range(count - 1, -1, -1))):
            for i, c in enumerate(order):
                steps, powers[c][where] = encode(carry)
                out_ref[c, matrix(where), :] = whole16(steps)
                passing = jnp.exp(log[c])
                if where == m:
                    held[c] = carry
                else:
                    flow = passing * jnp.sum(held[c] * carry, axis=0, keepdims=True)
                    flows = jnp.where(at == 2 * c + m, flow, flows)
                if i < count - 1:
                    carry = passing * carry + decode(pay_ref[c, matrix(where), :], tails[c][where : where + 1])
    parts = encode2(jnp.sum(flows, axis=1, keepdims=True))
    for c in range(count):
        out_ref[c, tail_of(out_ref), :] = rows16(
            *powers[c], *(part[2 * c + m : 2 * c + m + 1] for m in range(2) for part in parts)
        )


def local_kernel(
    query_ref, key_ref, value_ref, dout_ref, gate_ref, bias_ref, offsets_ref,
    dq_ref, dk_ref, dv_ref, rows_ref, cols_ref, held, sems,
):
    heads, length = gate_ref.shape[1:]
    copies = fetch((query_ref, key_ref, value_ref, dout_ref), held, sems)
    first, logits, step, causal, cumulative, doc, entry, tail, passes = decays(
        gate_ref[0], bias_ref[...], offsets_ref
    )
    cumulative_row = nt(step, causal.astype(F32), HIGHEST)
    linked = causal & (doc == doc_of(first + iota((1, length), 1), offsets_ref))
    lane = iota((length, heads), 1)
    sublane = iota((heads, length), 0)
    ends = jnp.zeros((length, heads), F32)
    ends_row = jnp.zeros((heads, length), F32)
    for h in range(heads):
        arrive(copies, h, heads)
        cols = matrix(h)
        q, k, v, d = (held[i, :, cols] for i in range(4))
        weights = jnp.where(
            linked,
            jnp.exp(jnp.where(linked, cumulative[:, h : h + 1] - cumulative_row[h : h + 1, :], 0.0)),
            0.0,
        ) * SCALE
        probs = nt(q, k) * weights
        dprobs = nt(d, v)
        pairs = probs * dprobs
        probs = probs.astype(BF16)
        dscores = (dprobs * weights).astype(BF16)
        dq_ref[:, cols] = nn(dscores, k)
        dk_ref[:, cols] = tn(dscores, q)
        dv_ref[:, cols] = tn(probs, d)
        ends = jnp.where(lane == h, jnp.sum(pairs, axis=1, keepdims=True), ends)
        ends_row = jnp.where(sublane == h, jnp.sum(pairs, axis=0, keepdims=True), ends_row)
    causal = causal.astype(F32)
    rows_ref[0] = tn(ends, causal, HIGHEST) - nn(ends_row, causal, HIGHEST)
    rows_ref[1] = -1.0 / (1.0 + jnp.exp(-logits))
    cols_ref[0] = entry * SCALE
    cols_ref[1] = tail


def received(state_ref, head):
    slot, m = divmod(head, 2)
    tail = wide(state_ref[slot, tail_of(state_ref), :])
    pair = tuple(decode(state_ref[slot, matrix(i), :], tail[i : i + 1]) for i in (m, 2 + m))
    return *pair, decode2(*(tail[i : i + 1, :1] for i in range(4 + 3 * m, 7 + 3 * m)))


def gates_kernel(
    query_ref, key_ref, value_ref, dout_ref, rows_ref, cols_ref, state_ref, dgate_ref, dbias_ref
):
    heads, length = dgate_ref.shape[1:]
    lane = iota((length, heads), 1)
    sublane = iota((heads, 1), 0)
    ends = jnp.zeros((length, heads), F32)
    starts = jnp.zeros((length, heads), F32)
    flows = jnp.zeros((heads, 1), F32)
    for h in range(heads):
        state32, grad32, flow = received(state_ref, h)
        state, state_low = split2(state32)
        grad, grad_low = split2(grad32)
        q, k, v, d = (ref[0, :, matrix(h)] for ref in (query_ref, key_ref, value_ref, dout_ref))
        at_end = jnp.sum(q.astype(F32) * (nt(d, state) + nt(d, state_low)), axis=1, keepdims=True)
        at_start = jnp.sum(k.astype(F32) * (nt(v, grad) + nt(v, grad_low)), axis=1, keepdims=True)
        ends = jnp.where(lane == h, at_end, ends)
        starts = jnp.where(lane == h, at_start, starts)
        flows = jnp.where(sublane == h, flow, flows)
    behind = iota((length, length), 0) - iota((length, length), 1)
    dstep = (
        rows_ref[0]
        + tn(ends * cols_ref[0], (behind >= 0).astype(F32), HIGHEST)
        + tn(starts * cols_ref[1], (behind < 0).astype(F32), HIGHEST)
        + flows
    )
    dlogit = dstep * rows_ref[1]
    dgate_ref[0] = dlogit.astype(BF16)
    same = iota((heads, heads), 0) == iota((heads, heads), 1)
    total = jnp.sum(jnp.where(same, jnp.sum(dlogit, axis=1, keepdims=True), 0.0), axis=0, keepdims=True)
    dbias_ref[...] = jnp.broadcast_to(total[None], dbias_ref.shape)


def output_kernel(
    key_ref, value_ref, dout_ref, cols_ref, state_ref, dq_near_ref, dk_near_ref, dv_near_ref,
    dq_ref, dk_ref, dv_ref,
):
    for h in range(cols_ref.shape[2]):
        cols = matrix(h)
        entry, tail = (cols_ref[i, :, h : h + 1] for i in range(2))
        state, grad = (x.astype(BF16) for x in received(state_ref, h)[:2])
        for near_ref, out_ref, far, decay in (
            (dq_near_ref, dq_ref, nt(dout_ref[0, :, cols], state), entry),
            (dk_near_ref, dk_ref, nt(value_ref[0, :, cols], grad), tail),
            (dv_near_ref, dv_ref, nn(key_ref[0, :, cols], grad), tail),
        ):
            out_ref[0, :, cols] = (near_ref[:, cols] + decay * far).astype(BF16)


def call(kernel, out_shape, in_specs, **more):
    several = isinstance(out_shape, tuple)
    return pl.pallas_call(
        kernel,
        out_shape=out_shape,
        in_specs=in_specs,
        out_specs=(VMEM,) * len(out_shape) if several else VMEM,
        compiler_params=PARAMS,
        **more,
    )


def shards(query, key, value, dout, gate_in, gate_bias, offsets):
    heads = gate_bias.shape[0]
    length, width = query.shape[1:]
    count, segments = lax.axis_size("grp"), lax.axis_size("seg")
    gates = jnp.swapaxes(gate_in, 1, 2)
    small = (gates, gate_bias.reshape(1, heads), offsets)
    pin = lambda xs: tuple(pltpu.with_memory_space_constraint(x, pltpu.HBM) for x in xs)
    big = pin((query, key, value, dout))
    scratch = [pltpu.VMEM((4, length, width), BF16), pltpu.SemaphoreType.DMA((4, 8))]
    packed = jax.ShapeDtypeStruct((count, 4 * HEAD_DIM + TAIL, LANES), I16)
    pay = call(
        states_kernel,
        packed,
        [HBM] * 7,
        scratch_shapes=scratch
        + [
            pltpu.VMEM((heads, length), BF16),
            pltpu.VMEM((1, heads), F32),
            pltpu.SMEM(offsets.shape, jnp.int32),
            pltpu.SemaphoreType.DMA((3,)),
        ],
    )(*big, *pin(small))
    pay = lax.all_to_all(pay, "grp", split_axis=0, concat_axis=0, tiled=True)
    total = jax.ShapeDtypeStruct((2 * HEAD_DIM + 8, LANES), F32)
    sends = call(totals_kernel, (total,) * (segments - 1), [VMEM])(pay)
    got = [
        lax.ppermute(send, "seg", [(i, (i + d) % segments) for i in range(segments)])
        for d, send in enumerate(sends, 1)
    ]
    near_like = jax.ShapeDtypeStruct((length, width), F32)
    *near, rows, cols = call(
        local_kernel,
        (near_like,) * 3
        + (jax.ShapeDtypeStruct((2, heads, length), F32), jax.ShapeDtypeStruct((2, length, heads), F32)),
        [HBM] * 4 + [VMEM] * 2 + [SMEM],
        scratch_shapes=scratch,
    )(*big, *small)
    carried = call(
        scan_kernel,
        packed,
        [VMEM] * segments + [pl.BlockSpec(memory_space=pl.ANY)],
        scratch_shapes=[pltpu.VMEM((count, HEAD_DIM, LANES), F32)],
    )(pay, *got, rows)
    carried = lax.all_to_all(carried, "grp", split_axis=0, concat_axis=0, tiled=True)
    dgate, dbias = call(
        gates_kernel,
        (
            jax.ShapeDtypeStruct(gates.shape, BF16),
            jax.ShapeDtypeStruct((lax.axis_size(ALL), 1, heads), F32),
        ),
        [VMEM] * 7,
    )(query, key, value, dout, rows, cols, carried)
    everywhere = lax.all_to_all(dbias, ALL, split_axis=0, concat_axis=0, tiled=True)
    like = jax.ShapeDtypeStruct(query.shape, BF16)
    dq, dk, dv = call(output_kernel, (like,) * 3, [VMEM] * 8)(key, value, dout, cols, carried, *near)
    return dq, dk, dv, jnp.swapaxes(dgate, 1, 2), jnp.sum(everywhere, axis=(0, 1))


def solution(mesh):
    rows = P("dp", LINE, None)
    return jax.shard_map(
        shards,
        mesh=mesh,
        in_specs=(rows, rows, rows, rows, rows, P(), P("dp", None)),
        out_specs=(rows, rows, rows, rows, P()),
        check_vma=False,
    )
```

time: 115 us -> 115 us (level)
  blocking collectives: 36.5 us -> 65.3 us
  waiting for transfers between devices: 26.2 us -> 7.36 us
  starting transfers between devices: 19.6 us -> 14.9 us
  Pallas kernels: 21.6 us -> 18.8 us
  local copies, waits for them, and re-layouts: 9.31 us -> 6.62 us
    all_to_all x0 -> x1, blocking collectives: none -> 28.8 us  [shards(): lax.all_to_all(carried, 'grp', split_axis=0, concat_axis=0, tiled=True)]
    all_to_all x2 -> x1, waiting for transfers between devices: 23.8 us -> 7.35 us  [shards(): lax.all_to_all(dbias, ALL, split_axis=0, concat_axis=0, tiled=True)]
    all_to_all x2 -> x1, starting transfers between devices: 14.6 us -> 9.76 us  [shards(): lax.all_to_all(dbias, ALL, split_axis=0, concat_axis=0, tiled=True)]
    pallas_call x1, Pallas kernels: 5.36 us -> 2.81 us  [shards(): call(gates_kernel, (jax.ShapeDtypeStruct(gates.shape, BF16), jax.ShapeDty...]
    ppermute x3, waiting for transfers between devices: 2.38 us -> 0.01 us  [shards(): lax.ppermute(send, 'seg', [(i, (i + d) % segments) for i in range(segment...]
    unnamed x30 -> x26, local copies, waits for them, and re-layouts: 8.59 us -> 6.62 us
  transfers between devices with their start and end apart: 5 -> 4, of which waited for: 4 -> 1; matrix products, arithmetic and copies ran while one was open for 0% -> 0% of each run, Pallas kernels for 8% -> 8%
where the time goes in v3:
time: 115 us
  blocking collectives  65.3 us (57%)
  Pallas kernels  18.8 us (16%)
  starting transfers between devices  14.9 us (13%)
  waiting for transfers between devices  7.36 us (6%)
  local copies, waits for them, and re-layouts  6.62 us (6%)
    all_to_all x1, blocking collectives, shards(): pay = lax.all_to_all(pay, 'grp', split_axis=0, concat_axis=0, tiled=True)  36.5 us
    all_to_all x1, blocking collectives, shards(): lax.all_to_all(carried, 'grp', split_axis=0, concat_axis=0, tiled=True)  28.8 us
    all_to_all x1, starting transfers between devices, shards(): lax.all_to_all(dbias, ALL, split_axis=0, concat_axis=0, tiled=True)  9.76 us
    all_to_all x1, waiting for transfers between devices, shards(): lax.all_to_all(dbias, ALL, split_axis=0, concat_axis=0, tiled=True)  7.35 us
    pallas_call x1, Pallas kernels, shards(): call(local_kernel, (near_like,) * 3 + (jax.ShapeDtypeStruct((2, heads, le...  6.85 us
    unnamed x26, local copies, waits for them, and re-layouts  6.62 us
    pallas_call x1, Pallas kernels, shards(): call(states_kernel, packed, [HBM] * 7, scratch_shapes=scratch + [pltpu.VM...  5.45 us
    ppermute x3, starting transfers between devices, shards(): lax.ppermute(send, 'seg', [(i, (i + d) % segments) for i in range(segment...  5.09 us
  transfers between devices with their start and end apart: 4, of which 1 were waited for; matrix products, arithmetic and copies ran while one was open for 0% of the time, Pallas kernels for 8%

profile of v3, /device:TPU:1, one launch (start us, length us, event | category | flops | bytes accessed | tf_op | source)
XLA Modules:
  0.0 114.5 jit_solution(5984764987025033078)
XLA Ops:
  0.6 5.5 %shard_map.111 = s16[8,528,128]{2,1,0:T(8,128)(2,1)S(1)} custom-call(bf16[1,128,2048]{2,1,0:T(8,128)(2,1)} %query_ref.5, bf16[1,128,2048]{2,1,0:T(8,128)(2,1)} %key_ref.7, bf16[1,128,2048]{2,1,0:T(8,128)(2,1)} %value_ref.7, bf16[1,128,2048]{2,1,0:T(8,128)(2,1)} %dout_ref.7, bf16[1,16,128]{2,1,0:T(8,128)(2,1)} %bitcast.3, f32[1,16]{1,0:T(1,128)} %bitcast.5, ...), custom_call_target="tpu_custom_call" | custom-call | tf_op jit(solution)/shard_map/pallas_call | solution.py:375
  6.1 36.5 %all_to_all.15.pay_ref = s16[8,528,128]{2,1,0:T(8,128)(2,1)S(1)} all-to-all(s16[8,528,128]{2,1,0:T(8,128)(2,1)S(1)} %shard_map.111), channel_id=1, replica_groups=mesh['dp'=8,'seg'=4,'grp'=8] {'grp'}, dimensions={0} | all-to-all | bytes 2162688 | tf_op jit(solution)/shard_map/all_to_all | solution.py:387
  42.6 0.0 copy-start.10
  42.6 0.0 copy-start.11
  42.6 0.0 copy-start.12
  42.6 0.4 shard_map.112
  43.0 1.4 %collective-permute-start = (f32[264,128]{1,0:T(8,128)S(1)}, f32[264,128]{1,0:T(8,128)S(1)}, u32[]{:S(2)}, u32[]{:S(2)}) collective-permute-start(f32[264,128]{1,0:T(8,128)S(1)} %get-tuple-element.19), channel_id=1, source_target_pairs={{0,8},{8,16},{16,24},{24,0},{1,9},{9,17},{17,25},{25,1},{2,10},{10... | collective-permute-start | bytes 405512 | tf_op jit(solution)/shard_map/ppermute | solution.py:391
  44.4 2.6 %collective-permute-start.1 = (f32[264,128]{1,0:T(8,128)S(1)}, f32[264,128]{1,0:T(8,128)S(1)}, u32[]{:S(2)}, u32[]{:S(2)}) collective-permute-start(f32[264,128]{1,0:T(8,128)S(1)} %get-tuple-element.20), channel_id=1, source_target_pairs={{0,16},{8,24},{16,0},{24,8},{1,17},{9,25},{17,1},{25,9},{2,18},{10... | collective-permute-start | bytes 405512 | tf_op jit(solution)/shard_map/ppermute | solution.py:391
  47.0 1.1 collective-permute-start.2
  48.1 0.0 copy-done.10
  48.1 0.0 copy-done.11
  48.1 0.0 copy-done.12
  48.1 6.9 %shard_map.110 = (f32[128,2048]{1,0:T(8,128)S(1)}, f32[128,2048]{1,0:T(8,128)S(1)}, f32[128,2048]{1,0:T(8,128)S(1)}, f32[2,16,128]{2,1,0:T(8,128)S(1)}, f32[2,128,16]{2,1,0:T(8,128)S(1)}) custom-call(bf16[1,128,2048]{2,1,0:T(8,128)(2,1)} %query_ref.5, bf16[1,128,2048]{2,1,0:T(8,128)(2,1)} %key_ref.7, bf16[1,128,2048]{2,1,0:T(8,128)(2,1)} %value_ref.7, ...), custom_call_target="tpu_custom_call" | custom-call | tf_op jit(solution)/shard_map/pallas_call | solution.py:395
  54.9 0.0 copy-start.4
  55.0 1.0 copy-done.4
  55.9 0.0 copy-start.6
  55.9 1.0 copy-done.6
  56.9 0.0 copy-start.8
  56.9 1.0 copy-done.8
  57.9 0.0 collective-permute-done.refs_0_
  57.9 0.0 collective-permute-done.1.refs_1_
  57.9 0.0 collective-permute-done.2.refs_2_
  57.9 1.1 shard_map.113
  59.0 0.0 copy-start
  59.0 0.0 copy-start.1
  59.1 0.0 copy-start.2
  59.1 0.0 copy-start.3
  59.1 28.8 %all_to_all.16.state_ref = s16[8,528,128]{2,1,0:T(8,128)(2,1)S(1)} all-to-all(s16[8,528,128]{2,1,0:T(8,128)(2,1)S(1)} %shard_map.113), channel_id=1, replica_groups=mesh['dp'=8,'seg'=4,'grp'=8] {'grp'}, dimensions={0} | all-to-all | bytes 2162688 | tf_op jit(solution)/shard_map/all_to_all | solution.py:408
  87.9 0.0 copy-done
  87.9 0.0 copy-done.1
  87.9 0.0 copy-done.2
  87.9 0.0 copy-done.3
  87.9 2.8 %shard_map.115 = (bf16[1,16,128]{2,1,0:T(8,128)(2,1)}, f32[256,1,16]{2,1,0:T(1,128)}) custom-call(bf16[1,128,2048]{2,1,0:T(8,128)(2,1)S(1)} %copy-done.3, bf16[1,128,2048]{2,1,0:T(8,128)(2,1)S(1)} %copy-done, bf16[1,128,2048]{2,1,0:T(8,128)(2,1)S(1)} %copy-done.1, bf16[1,128,2048]{2,1,0:T(8,128)(2,1)S(1)} %copy-done.2, ...), custom_call_target="tpu_custom_call" | custom-call | tf_op jit(solution)/shard_map/pallas_call | solution.py:409
  90.8 9.8 %all-to-all-start.2 = ((f32[256,1,16]{2,1,0:T(1,128)}), f32[256,1,16]{2,1,0:T(1,128)S(1)}, u32[]{:S(2)}, u32[]{:S(2)}) async-start(f32[256,1,16]{2,1,0:T(1,128)} %get-tuple-element.30), calls=%async_computation.2 | async-start | bytes 262144 | tf_op jit(solution)/shard_map/all_to_all | solution.py:417
  100.5 0.0 copy-start.5
  100.5 1.2 %copy-done.5 = f32[128,2048]{1,0:T(8,128)S(1)} copy-done((f32[128,2048]{1,0:T(8,128)S(1)}, f32[128,2048]{1,0:T(8,128)}, u32[]{:S(2)}) %copy-start.5) | copy-done | bytes 1048600
  101.8 0.0 copy-start.7
  101.8 1.2 %copy-done.7 = f32[128,2048]{1,0:T(8,128)S(1)} copy-done((f32[128,2048]{1,0:T(8,128)S(1)}, f32[128,2048]{1,0:T(8,128)}, u32[]{:S(2)}) %copy-start.7) | copy-done | bytes 1048600
  103.0 0.0 copy-start.9
  103.0 1.2 %copy-done.9 = f32[128,2048]{1,0:T(8,128)S(1)} copy-done((f32[128,2048]{1,0:T(8,128)S(1)}, f32[128,2048]{1,0:T(8,128)}, u32[]{:S(2)}) %copy-start.9) | copy-done | bytes 1048600
  104.2 2.2 %shard_map.114 = (bf16[1,128,2048]{2,1,0:T(8,128)(2,1)}, bf16[1,128,2048]{2,1,0:T(8,128)(2,1)}, bf16[1,128,2048]{2,1,0:T(8,128)(2,1)}) custom-call(bf16[1,128,2048]{2,1,0:T(8,128)(2,1)S(1)} %copy-done, bf16[1,128,2048]{2,1,0:T(8,128)(2,1)S(1)} %copy-done.1, bf16[1,128,2048]{2,1,0:T(8,128)(2,1)S(1)} %copy-done.2, ...), custom_call_target="tpu_custom_call" | custom-call | tf_op jit(solution)/shard_map/pallas_call | solution.py:419
  106.4 7.4 %all-to-all-done.2 = f32[256,1,16]{2,1,0:T(1,128)S(1)} async-done(((f32[256,1,16]{2,1,0:T(1,128)}), f32[256,1,16]{2,1,0:T(1,128)S(1)}, u32[]{:S(2)}, u32[]{:S(2)}) %all-to-all-start.2) | async-done | bytes 16416 | tf_op jit(solution)/shard_map/all_to_all | solution.py:417
  113.7 0.8 reduce_sum.9
Async XLA Ops:
  42.6 5.5 %copy-start.10 = (bf16[1,128,16]{1,2,0:T(8,128)(2,1)S(1)}, bf16[1,128,16]{1,2,0:T(8,128)(2,1)}, u32[]{:S(2)}) copy-start(bf16[1,128,16]{1,2,0:T(8,128)(2,1)} %param.11) | copy-start | bytes 12292
  42.6 5.5 %copy-start.11 = (f32[16]{0:T(128)S(1)}, f32[16]{0:T(128)}, u32[]{:S(2)}) copy-start(f32[16]{0:T(128)} %param.12) | copy-start | bytes 196
  42.6 5.5 %copy-start.12 = (s32[1,4]{1,0:T(1,128)S(1)}, s32[1,4]{1,0:T(1,128)}, u32[]{:S(2)}) copy-start(s32[1,4]{1,0:T(1,128)} %offsets_ref.3) | copy-start | bytes 52
  43.0 14.9 %collective-permute-start = (f32[264,128]{1,0:T(8,128)S(1)}, f32[264,128]{1,0:T(8,128)S(1)}, u32[]{:S(2)}, u32[]{:S(2)}) collective-permute-start(f32[264,128]{1,0:T(8,128)S(1)} %get-tuple-element.19), channel_id=1, source_target_pairs={{0,8},{8,16},{16,24},{24,0},{1,9},{9,17},{17,25},{25,1},{2,10},{10... | collective-permute-start | bytes 405512 | tf_op jit(solution)/shard_map/ppermute | solution.py:391
  44.4 13.5 %collective-permute-start.1 = (f32[264,128]{1,0:T(8,128)S(1)}, f32[264,128]{1,0:T(8,128)S(1)}, u32[]{:S(2)}, u32[]{:S(2)}) collective-permute-start(f32[264,128]{1,0:T(8,128)S(1)} %get-tuple-element.20), channel_id=1, source_target_pairs={{0,16},{8,24},{16,0},{24,8},{1,17},{9,25},{17,1},{25,9},{2,18},{10... | collective-permute-start | bytes 405512 | tf_op jit(solution)/shard_map/ppermute | solution.py:391
  47.0 10.9 %collective-permute-start.2 = (f32[264,128]{1,0:T(8,128)S(1)}, f32[264,128]{1,0:T(8,128)S(1)}, u32[]{:S(2)}, u32[]{:S(2)}) collective-permute-start(f32[264,128]{1,0:T(8,128)S(1)} %get-tuple-element.21), channel_id=1, source_target_pairs={{0,24},{8,0},{16,8},{24,16},{1,25},{9,1},{17,9},{25,17},{2,26},{10... | collective-permute-start | bytes 405512 | tf_op jit(solution)/shard_map/ppermute | solution.py:391
  54.9 1.0 copy-start.4
  55.9 1.0 copy-start.6
  56.9 1.0 copy-start.8
  59.0 28.9 %copy-start = (bf16[1,128,2048]{2,1,0:T(8,128)(2,1)S(1)}, bf16[1,128,2048]{2,1,0:T(8,128)(2,1)}, u32[]{:S(2)}) copy-start(bf16[1,128,2048]{2,1,0:T(8,128)(2,1)} %key_ref.7) | copy-start | bytes 1572868
  59.0 28.9 %copy-start.1 = (bf16[1,128,2048]{2,1,0:T(8,128)(2,1)S(1)}, bf16[1,128,2048]{2,1,0:T(8,128)(2,1)}, u32[]{:S(2)}) copy-start(bf16[1,128,2048]{2,1,0:T(8,128)(2,1)} %value_ref.7) | copy-start | bytes 1572868
  59.1 28.9 %copy-start.2 = (bf16[1,128,2048]{2,1,0:T(8,128)(2,1)S(1)}, bf16[1,128,2048]{2,1,0:T(8,128)(2,1)}, u32[]{:S(2)}) copy-start(bf16[1,128,2048]{2,1,0:T(8,128)(2,1)} %dout_ref.7) | copy-start | bytes 1572868
  59.1 28.9 %copy-start.3 = (bf16[1,128,2048]{2,1,0:T(8,128)(2,1)S(1)}, bf16[1,128,2048]{2,1,0:T(8,128)(2,1)}, u32[]{:S(2)}) copy-start(bf16[1,128,2048]{2,1,0:T(8,128)(2,1)} %query_ref.5) | copy-start | bytes 1572868
  90.8 23.0 %all-to-all-start.2 = ((f32[256,1,16]{2,1,0:T(1,128)}), f32[256,1,16]{2,1,0:T(1,128)S(1)}, u32[]{:S(2)}, u32[]{:S(2)}) async-start(f32[256,1,16]{2,1,0:T(1,128)} %get-tuple-element.30), calls=%async_computation.2 | async-start | bytes 262144 | tf_op jit(solution)/shard_map/all_to_all | solution.py:417
  100.5 1.2 %copy-start.5 = (f32[128,2048]{1,0:T(8,128)S(1)}, f32[128,2048]{1,0:T(8,128)}, u32[]{:S(2)}) copy-start(f32[128,2048]{1,0:T(8,128)} %copy-done.4) | copy-start | bytes 3145732
  101.8 1.2 %copy-start.7 = (f32[128,2048]{1,0:T(8,128)S(1)}, f32[128,2048]{1,0:T(8,128)}, u32[]{:S(2)}) copy-start(f32[128,2048]{1,0:T(8,128)} %copy-done.6) | copy-start | bytes 3145732
  103.0 1.2 %copy-start.9 = (f32[128,2048]{1,0:T(8,128)S(1)}, f32[128,2048]{1,0:T(8,128)}, u32[]{:S(2)}) copy-start(f32[128,2048]{1,0:T(8,128)} %copy-done.8) | copy-start | bytes 3145732

commit v4 on v3

--- a/solution.py
+++ b/solution.py
@@ -194,7 +194,7 @@
     return [log_whole(t[4 + 2 * m : 5 + 2 * m], t[5 + 2 * m : 6 + 2 * m]) for t in tails]
 
 
-def totals_kernel(pay_ref, *send_refs):
+def totals_kernel(pay_ref, _, *send_refs):
     count = pay_ref.shape[0]
     tails = [wide(pay_ref[c, tail_of(pay_ref), :]) for c in range(count)]
     mine, segments = lax.axis_index("seg"), lax.axis_size("seg")
@@ -218,7 +218,7 @@
 
 
 def scan_kernel(pay_ref, *refs):
-    *got_refs, _, out_ref, held = refs
+    *got_refs, out_ref, held = refs
     count = pay_ref.shape[0]
     mine = lax.axis_index("seg")
     tails = [wide(pay_ref[c, tail_of(pay_ref), :]) for c in range(count)]
@@ -385,12 +385,6 @@
         ],
     )(*big, *pin(small))
     pay = lax.all_to_all(pay, "grp", split_axis=0, concat_axis=0, tiled=True)
-    total = jax.ShapeDtypeStruct((2 * HEAD_DIM + 8, LANES), F32)
-    sends = call(totals_kernel, (total,) * (segments - 1), [VMEM])(pay)
-    got = [
-        lax.ppermute(send, "seg", [(i, (i + d) % segments) for i in range(segments)])
-        for d, send in enumerate(sends, 1)
-    ]
     near_like = jax.ShapeDtypeStruct((length, width), F32)
     *near, rows, cols = call(
         local_kernel,
@@ -399,12 +393,18 @@
         [HBM] * 4 + [VMEM] * 2 + [SMEM],
         scratch_shapes=scratch,
     )(*big, *small)
+    total = jax.ShapeDtypeStruct((2 * HEAD_DIM + 8, LANES), F32)
+    sends = call(totals_kernel, (total,) * (segments - 1), [VMEM, pl.BlockSpec(memory_space=pl.ANY)])(pay, rows)
+    got = [
+        lax.ppermute(send, "seg", [(i, (i + d) % segments) for i in range(segments)])
+        for d, send in enumerate(sends, 1)
+    ]
     carried = call(
         scan_kernel,
         packed,
-        [VMEM] * segments + [pl.BlockSpec(memory_space=pl.ANY)],
+        [VMEM] * segments,
         scratch_shapes=[pltpu.VMEM((count, HEAD_DIM, LANES), F32)],
-    )(pay, *got, rows)
+    )(pay, *got)
     carried = lax.all_to_all(carried, "grp", split_axis=0, concat_axis=0, tiled=True)
     dgate, dbias = call(
         gates_kernel,

time: 115 us -> 115 us (level)
  blocking collectives: 65.3 us -> 29.9 us
  waiting for transfers between devices: 7.36 us -> 32.3 us
  starting transfers between devices: 14.9 us -> 23.9 us
    all_to_all x1 -> x0, blocking collectives: 36.5 us -> none  [shards(): pay = lax.all_to_all(pay, 'grp', split_axis=0, concat_axis=0, tiled=True)]
    all_to_all x0 -> x1, waiting for transfers between devices: none -> 20.1 us  [shards(): pay = lax.all_to_all(pay, 'grp', split_axis=0, concat_axis=0, tiled=True)]
    all_to_all x0 -> x1, starting transfers between devices: none -> 9.16 us  [shards(): pay = lax.all_to_all(pay, 'grp', split_axis=0, concat_axis=0, tiled=True)]
    ppermute x3, waiting for transfers between devices: 0.01 us -> 5.02 us  [shards(): lax.ppermute(send, 'seg', [(i, (i + d) % segments) for i in range(segment...]
  transfers between devices with their start and end apart: 4 -> 5, of which waited for: 1 -> 4; matrix products, arithmetic and copies ran while one was open for 0% -> 0% of each run, Pallas kernels for 8% -> 8%
where the time goes in v4:
time: 115 us; the launch traced here: 114 us
  waiting for transfers between devices  32.3 us (28%)
  blocking collectives  29.9 us (26%)
  starting transfers between devices  23.9 us (21%)
  Pallas kernels  19.8 us (17%)
  local copies, waits for them, and re-layouts  6.61 us (6%)
    all_to_all x1, blocking collectives, shards(): lax.all_to_all(carried, 'grp', split_axis=0, concat_axis=0, tiled=True)  29.9 us
    all_to_all x1, waiting for transfers between devices, shards(): pay = lax.all_to_all(pay, 'grp', split_axis=0, concat_axis=0, tiled=True)  20.1 us
    all_to_all x1, starting transfers between devices, shards(): lax.all_to_all(dbias, ALL, split_axis=0, concat_axis=0, tiled=True)  9.68 us
    all_to_all x1, starting transfers between devices, shards(): pay = lax.all_to_all(pay, 'grp', split_axis=0, concat_axis=0, tiled=True)  9.16 us
    all_to_all x1, waiting for transfers between devices, shards(): lax.all_to_all(dbias, ALL, split_axis=0, concat_axis=0, tiled=True)  7.16 us
    pallas_call x1, Pallas kernels, shards(): call(local_kernel, (near_like,) * 3 + (jax.ShapeDtypeStruct((2, heads, le...  6.86 us
    unnamed x26, local copies, waits for them, and re-layouts  6.61 us
    pallas_call x1, Pallas kernels, shards(): call(states_kernel, packed, [HBM] * 7, scratch_shapes=scratch + [pltpu.VM...  6.46 us
  transfers between devices with their start and end apart: 5, of which 4 were waited for; matrix products, arithmetic and copies ran while one was open for 0% of the time, Pallas kernels for 8%

profile of v4, /device:TPU:1, one launch (start us, length us, event | category | flops | bytes accessed | tf_op | source)
XLA Modules:
  0.0 114.1 jit_solution(15237593055406861416)
XLA Ops:
  0.6 6.5 %shard_map.111 = s16[8,528,128]{2,1,0:T(8,128)(2,1)} custom-call(bf16[1,128,2048]{2,1,0:T(8,128)(2,1)} %query_ref.5, bf16[1,128,2048]{2,1,0:T(8,128)(2,1)} %key_ref.7, bf16[1,128,2048]{2,1,0:T(8,128)(2,1)} %value_ref.7, bf16[1,128,2048]{2,1,0:T(8,128)(2,1)} %dout_ref.7, bf16[1,16,128]{2,1,0:T(8,128)(2,1)} %bitcast.3, f32[1,16]{1,0:T(1,128)} %bitcast.5, ...), custom_call_target="tpu_custom_call" | custom-call | tf_op jit(solution)/shard_map/pallas_call | solution.py:375
  7.1 0.0 copy-start.10
  7.1 0.0 copy-start.11
  7.1 0.0 copy-start.12
  7.1 9.2 %all-to-all-start = ((s16[8,528,128]{2,1,0:T(8,128)(2,1)}), s16[8,528,128]{2,1,0:T(8,128)(2,1)S(1)}, u32[]{:S(2)}, u32[]{:S(2)}) async-start(s16[8,528,128]{2,1,0:T(8,128)(2,1)} %shard_map.111), calls=%async_computation | async-start | bytes 2162688 | tf_op jit(solution)/shard_map/all_to_all | solution.py:387
  16.3 0.0 copy-done.10
  16.3 0.0 copy-done.11
  16.3 0.0 copy-done.12
  16.3 6.9 %shard_map.110 = (f32[128,2048]{1,0:T(8,128)S(1)}, f32[128,2048]{1,0:T(8,128)S(1)}, f32[128,2048]{1,0:T(8,128)S(1)}, f32[2,16,128]{2,1,0:T(8,128)S(1)}, f32[2,128,16]{2,1,0:T(8,128)S(1)}) custom-call(bf16[1,128,2048]{2,1,0:T(8,128)(2,1)} %query_ref.5, bf16[1,128,2048]{2,1,0:T(8,128)(2,1)} %key_ref.7, bf16[1,128,2048]{2,1,0:T(8,128)(2,1)} %value_ref.7, ...), custom_call_target="tpu_custom_call" | custom-call | tf_op jit(solution)/shard_map/pallas_call | solution.py:389
  23.2 0.0 copy-start.4
  23.2 1.0 copy-done.4
  24.1 0.0 copy-start.6
  24.1 1.0 copy-done.6
  25.1 0.0 copy-start.8
  25.1 1.0 copy-done.8
  26.1 20.1 %all-to-all-done.pay_ref = s16[8,528,128]{2,1,0:T(8,128)(2,1)S(1)} async-done(((s16[8,528,128]{2,1,0:T(8,128)(2,1)}), s16[8,528,128]{2,1,0:T(8,128)(2,1)S(1)}, u32[]{:S(2)}, u32[]{:S(2)}) %all-to-all-start) | async-done | bytes 1081376 | tf_op jit(solution)/shard_map/all_to_all | solution.py:387
  46.2 0.4 shard_map.112
  46.6 1.4 %collective-permute-start = (f32[264,128]{1,0:T(8,128)S(1)}, f32[264,128]{1,0:T(8,128)S(1)}, u32[]{:S(2)}, u32[]{:S(2)}) collective-permute-start(f32[264,128]{1,0:T(8,128)S(1)} %get-tuple-element.20), channel_id=1, source_target_pairs={{0,8},{8,16},{16,24},{24,0},{1,9},{9,17},{17,25},{25,1},{2,10},{10... | collective-permute-start | bytes 405512 | tf_op jit(solution)/shard_map/ppermute | solution.py:399
  48.0 2.6 %collective-permute-start.1 = (f32[264,128]{1,0:T(8,128)S(1)}, f32[264,128]{1,0:T(8,128)S(1)}, u32[]{:S(2)}, u32[]{:S(2)}) collective-permute-start(f32[264,128]{1,0:T(8,128)S(1)} %get-tuple-element.21), channel_id=1, source_target_pairs={{0,16},{8,24},{16,0},{24,8},{1,17},{9,25},{17,1},{25,9},{2,18},{10... | collective-permute-start | bytes 405512 | tf_op jit(solution)/shard_map/ppermute | solution.py:399
  50.6 1.1 collective-permute-start.2
  51.7 1.0 collective-permute-done.refs_0_
  52.7 4.0 %collective-permute-done.1.refs_1_ = f32[264,128]{1,0:T(8,128)S(1)} collective-permute-done((f32[264,128]{1,0:T(8,128)S(1)}, f32[264,128]{1,0:T(8,128)S(1)}, u32[]{:S(2)}, u32[]{:S(2)}) %collective-permute-start.1) | collective-permute-done | bytes 135200 | tf_op jit(solution)/shard_map/ppermute | solution.py:399
  56.7 0.0 collective-permute-done.2.refs_2_
  56.7 1.1 shard_map.113
  57.8 0.0 copy-start
  57.8 0.0 copy-start.1
  57.8 0.0 copy-start.2
  57.9 0.0 copy-start.3
  57.9 29.9 %all_to_all.15.state_ref = s16[8,528,128]{2,1,0:T(8,128)(2,1)S(1)} all-to-all(s16[8,528,128]{2,1,0:T(8,128)(2,1)S(1)} %shard_map.113), channel_id=1, replica_groups=mesh['dp'=8,'seg'=4,'grp'=8] {'grp'}, dimensions={0} | all-to-all | bytes 2162688 | tf_op jit(solution)/shard_map/all_to_all | solution.py:408
  87.8 0.0 copy-done
  87.8 0.0 copy-done.1
  87.8 0.0 copy-done.2
  87.8 0.0 copy-done.3
  87.8 2.8 %shard_map.115 = (bf16[1,16,128]{2,1,0:T(8,128)(2,1)}, f32[256,1,16]{2,1,0:T(1,128)}) custom-call(bf16[1,128,2048]{2,1,0:T(8,128)(2,1)S(1)} %copy-done.3, bf16[1,128,2048]{2,1,0:T(8,128)(2,1)S(1)} %copy-done, bf16[1,128,2048]{2,1,0:T(8,128)(2,1)S(1)} %copy-done.1, bf16[1,128,2048]{2,1,0:T(8,128)(2,1)S(1)} %copy-done.2, ...), custom_call_target="tpu_custom_call" | custom-call | tf_op jit(solution)/shard_map/pallas_call | solution.py:409
  90.6 9.7 %all-to-all-start.2 = ((f32[256,1,16]{2,1,0:T(1,128)}), f32[256,1,16]{2,1,0:T(1,128)S(1)}, u32[]{:S(2)}, u32[]{:S(2)}) async-start(f32[256,1,16]{2,1,0:T(1,128)} %get-tuple-element.30), calls=%async_computation.2 | async-start | bytes 262144 | tf_op jit(solution)/shard_map/all_to_all | solution.py:417
  100.3 0.0 copy-start.5
  100.3 1.2 %copy-done.5 = f32[128,2048]{1,0:T(8,128)S(1)} copy-done((f32[128,2048]{1,0:T(8,128)S(1)}, f32[128,2048]{1,0:T(8,128)}, u32[]{:S(2)}) %copy-start.5) | copy-done | bytes 1048600
  101.5 0.0 copy-start.7
  101.5 1.2 %copy-done.7 = f32[128,2048]{1,0:T(8,128)S(1)} copy-done((f32[128,2048]{1,0:T(8,128)S(1)}, f32[128,2048]{1,0:T(8,128)}, u32[]{:S(2)}) %copy-start.7) | copy-done | bytes 1048600
  102.7 0.0 copy-start.9
  102.7 1.2 %copy-done.9 = f32[128,2048]{1,0:T(8,128)S(1)} copy-done((f32[128,2048]{1,0:T(8,128)S(1)}, f32[128,2048]{1,0:T(8,128)}, u32[]{:S(2)}) %copy-start.9) | copy-done | bytes 1048600
  103.9 2.2 %shard_map.114 = (bf16[1,128,2048]{2,1,0:T(8,128)(2,1)}, bf16[1,128,2048]{2,1,0:T(8,128)(2,1)}, bf16[1,128,2048]{2,1,0:T(8,128)(2,1)}) custom-call(bf16[1,128,2048]{2,1,0:T(8,128)(2,1)S(1)} %copy-done, bf16[1,128,2048]{2,1,0:T(8,128)(2,1)S(1)} %copy-done.1, bf16[1,128,2048]{2,1,0:T(8,128)(2,1)S(1)} %copy-done.2, ...), custom_call_target="tpu_custom_call" | custom-call | tf_op jit(solution)/shard_map/pallas_call | solution.py:419
  106.1 7.2 %all-to-all-done.2 = f32[256,1,16]{2,1,0:T(1,128)S(1)} async-done(((f32[256,1,16]{2,1,0:T(1,128)}), f32[256,1,16]{2,1,0:T(1,128)S(1)}, u32[]{:S(2)}, u32[]{:S(2)}) %all-to-all-start.2) | async-done | bytes 16416 | tf_op jit(solution)/shard_map/all_to_all | solution.py:417
  113.3 0.8 reduce_sum.9
Async XLA Ops:
  7.1 9.2 %copy-start.10 = (bf16[1,128,16]{1,2,0:T(8,128)(2,1)S(1)}, bf16[1,128,16]{1,2,0:T(8,128)(2,1)}, u32[]{:S(2)}) copy-start(bf16[1,128,16]{1,2,0:T(8,128)(2,1)} %param.11) | copy-start | bytes 12292
  7.1 9.2 %copy-start.11 = (f32[16]{0:T(128)S(1)}, f32[16]{0:T(128)}, u32[]{:S(2)}) copy-start(f32[16]{0:T(128)} %param.12) | copy-start | bytes 196
  7.1 9.2 %copy-start.12 = (s32[1,4]{1,0:T(1,128)S(1)}, s32[1,4]{1,0:T(1,128)}, u32[]{:S(2)}) copy-start(s32[1,4]{1,0:T(1,128)} %offsets_ref.3) | copy-start | bytes 52
  7.1 39.1 %all-to-all-start = ((s16[8,528,128]{2,1,0:T(8,128)(2,1)}), s16[8,528,128]{2,1,0:T(8,128)(2,1)S(1)}, u32[]{:S(2)}, u32[]{:S(2)}) async-start(s16[8,528,128]{2,1,0:T(8,128)(2,1)} %shard_map.111), calls=%async_computation | async-start | bytes 2162688 | tf_op jit(solution)/shard_map/all_to_all | solution.py:387
  23.2 1.0 copy-start.4
  24.1 1.0 copy-start.6
  25.1 1.0 copy-start.8
  46.6 6.1 %collective-permute-start = (f32[264,128]{1,0:T(8,128)S(1)}, f32[264,128]{1,0:T(8,128)S(1)}, u32[]{:S(2)}, u32[]{:S(2)}) collective-permute-start(f32[264,128]{1,0:T(8,128)S(1)} %get-tuple-element.20), channel_id=1, source_target_pairs={{0,8},{8,16},{16,24},{24,0},{1,9},{9,17},{17,25},{25,1},{2,10},{10... | collective-permute-start | bytes 405512 | tf_op jit(solution)/shard_map/ppermute | solution.py:399
  48.0 8.7 %collective-permute-start.1 = (f32[264,128]{1,0:T(8,128)S(1)}, f32[264,128]{1,0:T(8,128)S(1)}, u32[]{:S(2)}, u32[]{:S(2)}) collective-permute-start(f32[264,128]{1,0:T(8,128)S(1)} %get-tuple-element.21), channel_id=1, source_target_pairs={{0,16},{8,24},{16,0},{24,8},{1,17},{9,25},{17,1},{25,9},{2,18},{10... | collective-permute-start | bytes 405512 | tf_op jit(solution)/shard_map/ppermute | solution.py:399
  50.6 6.1 %collective-permute-start.2 = (f32[264,128]{1,0:T(8,128)S(1)}, f32[264,128]{1,0:T(8,128)S(1)}, u32[]{:S(2)}, u32[]{:S(2)}) collective-permute-start(f32[264,128]{1,0:T(8,128)S(1)} %get-tuple-element.22), channel_id=1, source_target_pairs={{0,24},{8,0},{16,8},{24,16},{1,25},{9,1},{17,9},{25,17},{2,26},{10... | collective-permute-start | bytes 405512 | tf_op jit(solution)/shard_map/ppermute | solution.py:399
  57.8 29.9 %copy-start = (bf16[1,128,2048]{2,1,0:T(8,128)(2,1)S(1)}, bf16[1,128,2048]{2,1,0:T(8,128)(2,1)}, u32[]{:S(2)}) copy-start(bf16[1,128,2048]{2,1,0:T(8,128)(2,1)} %key_ref.7) | copy-start | bytes 1572868
  57.8 29.9 %copy-start.1 = (bf16[1,128,2048]{2,1,0:T(8,128)(2,1)S(1)}, bf16[1,128,2048]{2,1,0:T(8,128)(2,1)}, u32[]{:S(2)}) copy-start(bf16[1,128,2048]{2,1,0:T(8,128)(2,1)} %value_ref.7) | copy-start | bytes 1572868
  57.8 29.9 %copy-start.2 = (bf16[1,128,2048]{2,1,0:T(8,128)(2,1)S(1)}, bf16[1,128,2048]{2,1,0:T(8,128)(2,1)}, u32[]{:S(2)}) copy-start(bf16[1,128,2048]{2,1,0:T(8,128)(2,1)} %dout_ref.7) | copy-start | bytes 1572868
  57.9 29.9 %copy-start.3 = (bf16[1,128,2048]{2,1,0:T(8,128)(2,1)S(1)}, bf16[1,128,2048]{2,1,0:T(8,128)(2,1)}, u32[]{:S(2)}) copy-start(bf16[1,128,2048]{2,1,0:T(8,128)(2,1)} %query_ref.5) | copy-start | bytes 1572868
  90.6 22.7 %all-to-all-start.2 = ((f32[256,1,16]{2,1,0:T(1,128)}), f32[256,1,16]{2,1,0:T(1,128)S(1)}, u32[]{:S(2)}, u32[]{:S(2)}) async-start(f32[256,1,16]{2,1,0:T(1,128)} %get-tuple-element.30), calls=%async_computation.2 | async-start | bytes 262144 | tf_op jit(solution)/shard_map/all_to_all | solution.py:417
  100.3 1.2 %copy-start.5 = (f32[128,2048]{1,0:T(8,128)S(1)}, f32[128,2048]{1,0:T(8,128)}, u32[]{:S(2)}) copy-start(f32[128,2048]{1,0:T(8,128)} %copy-done.4) | copy-start | bytes 3145732
  101.5 1.2 %copy-start.7 = (f32[128,2048]{1,0:T(8,128)S(1)}, f32[128,2048]{1,0:T(8,128)}, u32[]{:S(2)}) copy-start(f32[128,2048]{1,0:T(8,128)} %copy-done.6) | copy-start | bytes 3145732
  102.7 1.2 %copy-start.9 = (f32[128,2048]{1,0:T(8,128)S(1)}, f32[128,2048]{1,0:T(8,128)}, u32[]{:S(2)}) copy-start(f32[128,2048]{1,0:T(8,128)} %copy-done.8) | copy-start | bytes 3145732

commit v5 on v4

--- a/solution.py
+++ b/solution.py
@@ -43,6 +43,16 @@
 def split2(x):
     hi = x.astype(BF16)
     return hi, (x - hi.astype(F32)).astype(BF16)
+
+
+def tn2(a, b):
+    both = tn(a, jnp.concatenate(split2(b), axis=1))
+    return both[:, : b.shape[1]] + both[:, b.shape[1] :]
+
+
+def nt2(a, b):
+    both = nt(a, jnp.concatenate(split2(b), axis=0))
+    return both[:, : b.shape[0]] + both[:, b.shape[0] :]
 
 
 def matrix(m):
@@ -157,7 +167,7 @@
 
 def states_kernel(
     query_ref, key_ref, value_ref, dout_ref, gate_ref, bias_ref, offsets_ref,
-    pay_ref, held, sems, gate_held, bias_held, offsets_held, small_sems,
+    pay_ref, held, sems, gate_held, bias_held, offsets_held, small_sems, pay, pay_sems,
 ):
     heads = bias_ref.shape[1]
     small = [
@@ -172,22 +182,25 @@
         copy.wait()
     _, _, _, _, cumulative, _, entry, tail, passes = decays(gate_held[...], bias_held[...], offsets_held)
     coarse, fine = log_parts(jnp.where(passes, jnp.maximum(cumulative[-1:, :], -120.0), -128.0))
-    powers = {}
+    powers, sent = {}, []
     for h in range(heads):
         arrive(copies, h, heads)
         cols = matrix(h)
         one = slice(h, h + 1)
         slot, m = divmod(h, 2)
         for at, left, right, weight in ((m, 1, 2, tail[:, one]), (2 + m, 0, 3, entry[:, one] * SCALE)):
-            upper, lower = split2(held[left, :, cols].astype(F32) * weight)
-            right = held[right, :, cols]
-            steps, powers[at] = encode(tn(upper, right) + tn(lower, right))
-            pay_ref[slot, matrix(at), :] = whole16(steps)
+            own = tn2(held[left, :, cols], held[right, :, cols].astype(F32) * weight)
+            steps, powers[at] = encode(own)
+            pay[slot, matrix(at), :] = whole16(steps)
         if m == 1:
-            pay_ref[slot, tail_of(pay_ref), :] = rows16(
+            pay[slot, tail_of(pay), :] = rows16(
                 *(powers[i] for i in range(4)),
                 *(x[:, i : i + 1] for i in (h - 1, h) for x in (coarse, fine)),
             )
+            sent.append(pltpu.make_async_copy(pay.at[slot], pay_ref.at[slot], pay_sems.at[slot]))
+            sent[-1].start()
+    for copy in sent:
+        copy.wait()
 
 
 def chunk_logs(tails, m):
@@ -312,11 +325,9 @@
     flows = jnp.zeros((heads, 1), F32)
     for h in range(heads):
         state32, grad32, flow = received(state_ref, h)
-        state, state_low = split2(state32)
-        grad, grad_low = split2(grad32)
         q, k, v, d = (ref[0, :, matrix(h)] for ref in (query_ref, key_ref, value_ref, dout_ref))
-        at_end = jnp.sum(q.astype(F32) * (nt(d, state) + nt(d, state_low)), axis=1, keepdims=True)
-        at_start = jnp.sum(k.astype(F32) * (nt(v, grad) + nt(v, grad_low)), axis=1, keepdims=True)
+        at_end = jnp.sum(q.astype(F32) * nt2(d, state32), axis=1, keepdims=True)
+        at_start = jnp.sum(k.astype(F32) * nt2(v, grad32), axis=1, keepdims=True)
         ends = jnp.where(lane == h, at_end, ends)
         starts = jnp.where(lane == h, at_start, starts)
         flows = jnp.where(sublane == h, flow, flows)
@@ -351,14 +362,9 @@
 
 
 def call(kernel, out_shape, in_specs, **more):
-    several = isinstance(out_shape, tuple)
+    more.setdefault("out_specs", (VMEM,) * len(out_shape) if isinstance(out_shape, tuple) else VMEM)
     return pl.pallas_call(
-        kernel,
-        out_shape=out_shape,
-        in_specs=in_specs,
-        out_specs=(VMEM,) * len(out_shape) if several else VMEM,
-        compiler_params=PARAMS,
-        **more,
+        kernel, out_shape=out_shape, in_specs=in_specs, compiler_params=PARAMS, **more
     )
 
 
@@ -382,7 +388,10 @@
             pltpu.VMEM((1, heads), F32),
             pltpu.SMEM(offsets.shape, jnp.int32),
             pltpu.SemaphoreType.DMA((3,)),
+            pltpu.VMEM(packed.shape, I16),
+            pltpu.SemaphoreType.DMA((count,)),
         ],
+        out_specs=HBM,
     )(*big, *pin(small))
     pay = lax.all_to_all(pay, "grp", split_axis=0, concat_axis=0, tiled=True)
     near_like = jax.ShapeDtypeStruct((length, width), F32)

time: 115 us -> 113 us (0.983)
  Pallas kernels: 19.8 us -> 18.6 us
where the time goes in v5:
time: 113 us
  waiting for transfers between devices  32.3 us (29%)
  blocking collectives  29.9 us (26%)
  starting transfers between devices  23.9 us (21%)
  Pallas kernels  18.6 us (16%)
  local copies, waits for them, and re-layouts  6.61 us (6%)
    all_to_all x1, blocking collectives, shards(): lax.all_to_all(carried, 'grp', split_axis=0, concat_axis=0, tiled=True)  29.9 us
    all_to_all x1, waiting for transfers between devices, shards(): pay = lax.all_to_all(pay, 'grp', split_axis=0, concat_axis=0, tiled=True)  20.1 us
    all_to_all x1, starting transfers between devices, shards(): lax.all_to_all(dbias, ALL, split_axis=0, concat_axis=0, tiled=True)  9.67 us
    all_to_all x1, starting transfers between devices, shards(): pay = lax.all_to_all(pay, 'grp', split_axis=0, concat_axis=0, tiled=True)  9.16 us
    all_to_all x1, waiting for transfers between devices, shards(): lax.all_to_all(dbias, ALL, split_axis=0, concat_axis=0, tiled=True)  7.17 us
    pallas_call x1, Pallas kernels, shards(): call(local_kernel, (near_like,) * 3 + (jax.ShapeDtypeStruct((2, heads, le...  6.86 us
    unnamed x26, local copies, waits for them, and re-layouts  6.61 us
    pallas_call x1, Pallas kernels, shards(): call(states_kernel, packed, [HBM] * 7, scratch_shapes=scratch + [pltpu.VM...  5.97 us
  transfers between devices with their start and end apart: 5, of which 4 were waited for; matrix products, arithmetic and copies ran while one was open for 0% of the time, Pallas kernels for 8%

profile of v5, /device:TPU:1, one launch (start us, length us, event | category | flops | bytes accessed | tf_op | source)
XLA Modules:
  0.0 112.8 jit_solution(12510935791552751298)
XLA Ops:
  0.6 6.0 %shard_map.111 = s16[8,528,128]{2,1,0:T(8,128)(2,1)} custom-call(bf16[1,128,2048]{2,1,0:T(8,128)(2,1)} %query_ref.5, bf16[1,128,2048]{2,1,0:T(8,128)(2,1)} %key_ref.7, bf16[1,128,2048]{2,1,0:T(8,128)(2,1)} %value_ref.7, bf16[1,128,2048]{2,1,0:T(8,128)(2,1)} %dout_ref.7, bf16[1,16,128]{2,1,0:T(8,128)(2,1)} %bitcast.3, f32[1,16]{1,0:T(1,128)} %bitcast.5, ...), custom_call_target="tpu_custom_call" | custom-call | tf_op jit(solution)/shard_map/pallas_call | solution.py:381
  6.6 0.0 copy-start.10
  6.6 0.0 copy-start.11
  6.6 0.0 copy-start.12
  6.6 9.2 %all-to-all-start = ((s16[8,528,128]{2,1,0:T(8,128)(2,1)}), s16[8,528,128]{2,1,0:T(8,128)(2,1)S(1)}, u32[]{:S(2)}, u32[]{:S(2)}) async-start(s16[8,528,128]{2,1,0:T(8,128)(2,1)} %shard_map.111), calls=%async_computation | async-start | bytes 2162688 | tf_op jit(solution)/shard_map/all_to_all | solution.py:396
  15.8 0.0 copy-done.10
  15.8 0.0 copy-done.11
  15.8 0.0 copy-done.12
  15.8 6.9 %shard_map.110 = (f32[128,2048]{1,0:T(8,128)S(1)}, f32[128,2048]{1,0:T(8,128)S(1)}, f32[128,2048]{1,0:T(8,128)S(1)}, f32[2,16,128]{2,1,0:T(8,128)S(1)}, f32[2,128,16]{2,1,0:T(8,128)S(1)}) custom-call(bf16[1,128,2048]{2,1,0:T(8,128)(2,1)} %query_ref.5, bf16[1,128,2048]{2,1,0:T(8,128)(2,1)} %key_ref.7, bf16[1,128,2048]{2,1,0:T(8,128)(2,1)} %value_ref.7, ...), custom_call_target="tpu_custom_call" | custom-call | tf_op jit(solution)/shard_map/pallas_call | solution.py:398
  22.7 0.0 copy-start.4
  22.7 1.0 copy-done.4
  23.7 0.0 copy-start.6
  23.7 1.0 copy-done.6
  24.6 0.0 copy-start.8
  24.6 1.0 copy-done.8
  25.6 20.1 %all-to-all-done.pay_ref = s16[8,528,128]{2,1,0:T(8,128)(2,1)S(1)} async-done(((s16[8,528,128]{2,1,0:T(8,128)(2,1)}), s16[8,528,128]{2,1,0:T(8,128)(2,1)S(1)}, u32[]{:S(2)}, u32[]{:S(2)}) %all-to-all-start) | async-done | bytes 1081376 | tf_op jit(solution)/shard_map/all_to_all | solution.py:396
  45.7 0.4 shard_map.112
  46.1 1.4 %collective-permute-start = (f32[264,128]{1,0:T(8,128)S(1)}, f32[264,128]{1,0:T(8,128)S(1)}, u32[]{:S(2)}, u32[]{:S(2)}) collective-permute-start(f32[264,128]{1,0:T(8,128)S(1)} %get-tuple-element.20), channel_id=1, source_target_pairs={{0,8},{8,16},{16,24},{24,0},{1,9},{9,17},{17,25},{25,1},{2,10},{10... | collective-permute-start | bytes 405512 | tf_op jit(solution)/shard_map/ppermute | solution.py:408
  47.5 2.6 %collective-permute-start.1 = (f32[264,128]{1,0:T(8,128)S(1)}, f32[264,128]{1,0:T(8,128)S(1)}, u32[]{:S(2)}, u32[]{:S(2)}) collective-permute-start(f32[264,128]{1,0:T(8,128)S(1)} %get-tuple-element.21), channel_id=1, source_target_pairs={{0,16},{8,24},{16,0},{24,8},{1,17},{9,25},{17,1},{25,9},{2,18},{10... | collective-permute-start | bytes 405512 | tf_op jit(solution)/shard_map/ppermute | solution.py:408
  50.1 1.1 collective-permute-start.2
  51.2 1.0 collective-permute-done.refs_0_
  52.2 4.0 %collective-permute-done.1.refs_1_ = f32[264,128]{1,0:T(8,128)S(1)} collective-permute-done((f32[264,128]{1,0:T(8,128)S(1)}, f32[264,128]{1,0:T(8,128)S(1)}, u32[]{:S(2)}, u32[]{:S(2)}) %collective-permute-start.1) | collective-permute-done | bytes 135200 | tf_op jit(solution)/shard_map/ppermute | solution.py:408
  56.2 0.0 collective-permute-done.2.refs_2_
  56.2 1.1 %shard_map.113 = s16[8,528,128]{2,1,0:T(8,128)(2,1)S(1)} custom-call(s16[8,528,128]{2,1,0:T(8,128)(2,1)S(1)} %all-to-all-done.pay_ref, f32[264,128]{1,0:T(8,128)S(1)} %collective-permute-done.refs_0_, f32[264,128]{1,0:T(8,128)S(1)} %collective-permute-done.1.refs_1_, f32[264,128]{1,0:T(8,128)S(1)} %collective-permute-done.2.refs_2_), custom_call_target="tpu_custom_call" | custom-call | tf_op jit(solution)/shard_map/pallas_call | solution.py:411
  57.3 0.0 copy-start
  57.3 0.0 copy-start.1
  57.4 0.0 copy-start.2
  57.4 0.0 copy-start.3
  57.4 29.9 %all_to_all.15.state_ref = s16[8,528,128]{2,1,0:T(8,128)(2,1)S(1)} all-to-all(s16[8,528,128]{2,1,0:T(8,128)(2,1)S(1)} %shard_map.113), channel_id=1, replica_groups=mesh['dp'=8,'seg'=4,'grp'=8] {'grp'}, dimensions={0} | all-to-all | bytes 2162688 | tf_op jit(solution)/shard_map/all_to_all | solution.py:417
  87.3 0.0 copy-done
  87.3 0.0 copy-done.1
  87.3 0.0 copy-done.2
  87.3 0.0 copy-done.3
  87.3 2.1 %shard_map.115 = (bf16[1,16,128]{2,1,0:T(8,128)(2,1)}, f32[256,1,16]{2,1,0:T(1,128)}) custom-call(bf16[1,128,2048]{2,1,0:T(8,128)(2,1)S(1)} %copy-done.3, bf16[1,128,2048]{2,1,0:T(8,128)(2,1)S(1)} %copy-done, bf16[1,128,2048]{2,1,0:T(8,128)(2,1)S(1)} %copy-done.1, bf16[1,128,2048]{2,1,0:T(8,128)(2,1)S(1)} %copy-done.2, ...), custom_call_target="tpu_custom_call" | custom-call | tf_op jit(solution)/shard_map/pallas_call | solution.py:418
  89.4 9.7 %all-to-all-start.2 = ((f32[256,1,16]{2,1,0:T(1,128)}), f32[256,1,16]{2,1,0:T(1,128)S(1)}, u32[]{:S(2)}, u32[]{:S(2)}) async-start(f32[256,1,16]{2,1,0:T(1,128)} %get-tuple-element.30), calls=%async_computation.2 | async-start | bytes 262144 | tf_op jit(solution)/shard_map/all_to_all | solution.py:426
  99.0 0.0 copy-start.5
  99.0 1.2 %copy-done.5 = f32[128,2048]{1,0:T(8,128)S(1)} copy-done((f32[128,2048]{1,0:T(8,128)S(1)}, f32[128,2048]{1,0:T(8,128)}, u32[]{:S(2)}) %copy-start.5) | copy-done | bytes 1048600
  100.3 0.0 copy-start.7
  100.3 1.2 %copy-done.7 = f32[128,2048]{1,0:T(8,128)S(1)} copy-done((f32[128,2048]{1,0:T(8,128)S(1)}, f32[128,2048]{1,0:T(8,128)}, u32[]{:S(2)}) %copy-start.7) | copy-done | bytes 1048600
  101.5 0.0 copy-start.9
  101.5 1.2 %copy-done.9 = f32[128,2048]{1,0:T(8,128)S(1)} copy-done((f32[128,2048]{1,0:T(8,128)S(1)}, f32[128,2048]{1,0:T(8,128)}, u32[]{:S(2)}) %copy-start.9) | copy-done | bytes 1048600
  102.7 2.2 %shard_map.114 = (bf16[1,128,2048]{2,1,0:T(8,128)(2,1)}, bf16[1,128,2048]{2,1,0:T(8,128)(2,1)}, bf16[1,128,2048]{2,1,0:T(8,128)(2,1)}) custom-call(bf16[1,128,2048]{2,1,0:T(8,128)(2,1)S(1)} %copy-done, bf16[1,128,2048]{2,1,0:T(8,128)(2,1)S(1)} %copy-done.1, bf16[1,128,2048]{2,1,0:T(8,128)(2,1)S(1)} %copy-done.2, ...), custom_call_target="tpu_custom_call" | custom-call | tf_op jit(solution)/shard_map/pallas_call | solution.py:428
  104.9 7.2 %all-to-all-done.2 = f32[256,1,16]{2,1,0:T(1,128)S(1)} async-done(((f32[256,1,16]{2,1,0:T(1,128)}), f32[256,1,16]{2,1,0:T(1,128)S(1)}, u32[]{:S(2)}, u32[]{:S(2)}) %all-to-all-start.2) | async-done | bytes 16416 | tf_op jit(solution)/shard_map/all_to_all | solution.py:426
  112.0 0.8 reduce_sum.9
Async XLA Ops:
  6.6 9.2 %copy-start.10 = (bf16[1,128,16]{1,2,0:T(8,128)(2,1)S(1)}, bf16[1,128,16]{1,2,0:T(8,128)(2,1)}, u32[]{:S(2)}) copy-start(bf16[1,128,16]{1,2,0:T(8,128)(2,1)} %param.11) | copy-start | bytes 12292
  6.6 9.2 %copy-start.11 = (f32[16]{0:T(128)S(1)}, f32[16]{0:T(128)}, u32[]{:S(2)}) copy-start(f32[16]{0:T(128)} %param.12) | copy-start | bytes 196
  6.6 9.2 %copy-start.12 = (s32[1,4]{1,0:T(1,128)S(1)}, s32[1,4]{1,0:T(1,128)}, u32[]{:S(2)}) copy-start(s32[1,4]{1,0:T(1,128)} %offsets_ref.3) | copy-start | bytes 52
  6.6 39.1 %all-to-all-start = ((s16[8,528,128]{2,1,0:T(8,128)(2,1)}), s16[8,528,128]{2,1,0:T(8,128)(2,1)S(1)}, u32[]{:S(2)}, u32[]{:S(2)}) async-start(s16[8,528,128]{2,1,0:T(8,128)(2,1)} %shard_map.111), calls=%async_computation | async-start | bytes 2162688 | tf_op jit(solution)/shard_map/all_to_all | solution.py:396
  22.7 1.0 copy-start.4
  23.7 1.0 copy-start.6
  24.6 1.0 copy-start.8
  46.1 6.1 %collective-permute-start = (f32[264,128]{1,0:T(8,128)S(1)}, f32[264,128]{1,0:T(8,128)S(1)}, u32[]{:S(2)}, u32[]{:S(2)}) collective-permute-start(f32[264,128]{1,0:T(8,128)S(1)} %get-tuple-element.20), channel_id=1, source_target_pairs={{0,8},{8,16},{16,24},{24,0},{1,9},{9,17},{17,25},{25,1},{2,10},{10... | collective-permute-start | bytes 405512 | tf_op jit(solution)/shard_map/ppermute | solution.py:408
  47.5 8.7 %collective-permute-start.1 = (f32[264,128]{1,0:T(8,128)S(1)}, f32[264,128]{1,0:T(8,128)S(1)}, u32[]{:S(2)}, u32[]{:S(2)}) collective-permute-start(f32[264,128]{1,0:T(8,128)S(1)} %get-tuple-element.21), channel_id=1, source_target_pairs={{0,16},{8,24},{16,0},{24,8},{1,17},{9,25},{17,1},{25,9},{2,18},{10... | collective-permute-start | bytes 405512 | tf_op jit(solution)/shard_map/ppermute | solution.py:408
  50.1 6.1 %collective-permute-start.2 = (f32[264,128]{1,0:T(8,128)S(1)}, f32[264,128]{1,0:T(8,128)S(1)}, u32[]{:S(2)}, u32[]{:S(2)}) collective-permute-start(f32[264,128]{1,0:T(8,128)S(1)} %get-tuple-element.22), channel_id=1, source_target_pairs={{0,24},{8,0},{16,8},{24,16},{1,25},{9,1},{17,9},{25,17},{2,26},{10... | collective-permute-start | bytes 405512 | tf_op jit(solution)/shard_map/ppermute | solution.py:408
  57.3 29.9 %copy-start = (bf16[1,128,2048]{2,1,0:T(8,128)(2,1)S(1)}, bf16[1,128,2048]{2,1,0:T(8,128)(2,1)}, u32[]{:S(2)}) copy-start(bf16[1,128,2048]{2,1,0:T(8,128)(2,1)} %key_ref.7) | copy-start | bytes 1572868
  57.3 29.9 %copy-start.1 = (bf16[1,128,2048]{2,1,0:T(8,128)(2,1)S(1)}, bf16[1,128,2048]{2,1,0:T(8,128)(2,1)}, u32[]{:S(2)}) copy-start(bf16[1,128,2048]{2,1,0:T(8,128)(2,1)} %value_ref.7) | copy-start | bytes 1572868
  57.4 29.9 %copy-start.2 = (bf16[1,128,2048]{2,1,0:T(8,128)(2,1)S(1)}, bf16[1,128,2048]{2,1,0:T(8,128)(2,1)}, u32[]{:S(2)}) copy-start(bf16[1,128,2048]{2,1,0:T(8,128)(2,1)} %dout_ref.7) | copy-start | bytes 1572868
  57.4 29.9 %copy-start.3 = (bf16[1,128,2048]{2,1,0:T(8,128)(2,1)S(1)}, bf16[1,128,2048]{2,1,0:T(8,128)(2,1)}, u32[]{:S(2)}) copy-start(bf16[1,128,2048]{2,1,0:T(8,128)(2,1)} %query_ref.5) | copy-start | bytes 1572868
  89.4 22.7 %all-to-all-start.2 = ((f32[256,1,16]{2,1,0:T(1,128)}), f32[256,1,16]{2,1,0:T(1,128)S(1)}, u32[]{:S(2)}, u32[]{:S(2)}) async-start(f32[256,1,16]{2,1,0:T(1,128)} %get-tuple-element.30), calls=%async_computation.2 | async-start | bytes 262144 | tf_op jit(solution)/shard_map/all_to_all | solution.py:426
  99.0 1.2 %copy-start.5 = (f32[128,2048]{1,0:T(8,128)S(1)}, f32[128,2048]{1,0:T(8,128)}, u32[]{:S(2)}) copy-start(f32[128,2048]{1,0:T(8,128)} %copy-done.4) | copy-start | bytes 3145732
  100.3 1.2 %copy-start.7 = (f32[128,2048]{1,0:T(8,128)S(1)}, f32[128,2048]{1,0:T(8,128)}, u32[]{:S(2)}) copy-start(f32[128,2048]{1,0:T(8,128)} %copy-done.6) | copy-start | bytes 3145732
  101.5 1.2 %copy-start.9 = (f32[128,2048]{1,0:T(8,128)S(1)}, f32[128,2048]{1,0:T(8,128)}, u32[]{:S(2)}) copy-start(f32[128,2048]{1,0:T(8,128)} %copy-done.8) | copy-start | bytes 3145732

commit v6 on v5

--- a/solution.py
+++ b/solution.py
@@ -12,6 +12,8 @@
 ALL = ("dp", "seg", "grp")
 TAIL = 16
 LANES = 128
+EXTRA = HEAD_DIM // 8
+SLOT = 4 * HEAD_DIM + 4 * EXTRA + TAIL
 F32 = jnp.float32
 BF16 = jnp.bfloat16
 I16 = jnp.int16
@@ -63,6 +65,10 @@
     return pl.ds(ref.shape[-2] - TAIL, TAIL)
 
 
+def extra(m):
+    return pl.ds(4 * HEAD_DIM + m * EXTRA, EXTRA)
+
+
 def iota(shape, dim):
     return lax.broadcasted_iota(jnp.int32, shape, dim)
 
@@ -75,14 +81,29 @@
     return x.astype(jnp.int32).astype(F32)
 
 
-def encode(x):
+def encode(x, ref, at, *slot):
     top = jnp.maximum(jnp.max(jnp.abs(x), axis=0, keepdims=True), 1e-30)
     power = jnp.ceil(jnp.log2(top) * 8.0)
-    return jnp.clip(jnp.floor(x * jnp.exp2(15.0 - power / 8.0) + 0.5), -32767.0, 32767.0), power
-
-
-def decode(steps, power):
-    return wide(steps) * jnp.exp2(power / 8.0 - 15.0)
+    steps = jnp.clip(jnp.floor(x * jnp.exp2(17.0 - power / 8.0) + 0.5), -131071.0, 131071.0)
+    high = jnp.floor(steps * 0.25)
+    low = steps - 4.0 * high
+    packed = sum(low[k * EXTRA : (k + 1) * EXTRA] * 4.0**k for k in range(8))
+    ref[*slot, matrix(at), :] = whole16(high)
+    ref[*slot, extra(at), :] = whole16(packed - 32768.0)
+    return power
+
+
+def decode(ref, at, power, *slot):
+    packed = wide(ref[*slot, extra(at), :]) + 32768.0
+    digits = [jnp.floor(packed * 0.25**k) for k in range(8)]
+    low = jnp.concatenate(
+        [d - 4.0 * above for d, above in zip(digits, digits[1:] + [jnp.zeros_like(packed)])], axis=0
+    )
+    return (wide(ref[*slot, matrix(at), :]) * 4.0 + low) * jnp.exp2(power / 8.0 - 17.0)
+
+
+def decode_high(ref, at, power, *slot):
+    return wide(ref[*slot, matrix(at), :]) * jnp.exp2(power / 8.0 - 15.0)
 
 
 def encode2(x):
@@ -190,8 +211,7 @@
         slot, m = divmod(h, 2)
         for at, left, right, weight in ((m, 1, 2, tail[:, one]), (2 + m, 0, 3, entry[:, one] * SCALE)):
             own = tn2(held[left, :, cols], held[right, :, cols].astype(F32) * weight)
-            steps, powers[at] = encode(own)
-            pay[slot, matrix(at), :] = whole16(steps)
+            powers[at] = encode(own, pay, at, slot)
         if m == 1:
             pay[slot, tail_of(pay), :] = rows16(
                 *(powers[i] for i in range(4)),
@@ -220,9 +240,7 @@
         for where, order in ((m, range(count)), (2 + m, range(count - 1, -1, -1))):
             carry = jnp.zeros((HEAD_DIM, HEAD_DIM), F32)
             for c in order:
-                carry = jnp.exp(log[c]) * carry + decode(
-                    pay_ref[c, matrix(where), :], tails[c][where : where + 1]
-                )
+                carry = jnp.exp(log[c]) * carry + decode(pay_ref, where, tails[c][where : where + 1], c)
             ends.append(carry)
         for distance, send_ref in enumerate(send_refs, 1):
             send_ref[matrix(m), :] = jnp.where(mine + distance < segments, *ends)
@@ -249,8 +267,7 @@
             grad = jnp.where(mine < d, sent[d - 1][0] * grad + sent[d - 1][1], grad)
         for where, carry, order in ((m, state, range(count)), (2 + m, grad, range(count - 1, -1, -1))):
             for i, c in enumerate(order):
-                steps, powers[c][where] = encode(carry)
-                out_ref[c, matrix(where), :] = whole16(steps)
+                powers[c][where] = encode(carry, out_ref, where, c)
                 passing = jnp.exp(log[c])
                 if where == m:
                     held[c] = carry
@@ -258,7 +275,7 @@
                     flow = passing * jnp.sum(held[c] * carry, axis=0, keepdims=True)
                     flows = jnp.where(at == 2 * c + m, flow, flows)
                 if i < count - 1:
-                    carry = passing * carry + decode(pay_ref[c, matrix(where), :], tails[c][where : where + 1])
+                    carry = passing * carry + decode(pay_ref, where, tails[c][where : where + 1], c)
     parts = encode2(jnp.sum(flows, axis=1, keepdims=True))
     for c in range(count):
         out_ref[c, tail_of(out_ref), :] = rows16(
@@ -307,10 +324,10 @@
     cols_ref[1] = tail
 
 
-def received(state_ref, head):
+def received(state_ref, head, decode):
     slot, m = divmod(head, 2)
     tail = wide(state_ref[slot, tail_of(state_ref), :])
-    pair = tuple(decode(state_ref[slot, matrix(i), :], tail[i : i + 1]) for i in (m, 2 + m))
+    pair = tuple(decode(state_ref, i, tail[i : i + 1], slot) for i in (m, 2 + m))
     return *pair, decode2(*(tail[i : i + 1, :1] for i in range(4 + 3 * m, 7 + 3 * m)))
 
 
@@ -324,7 +341,7 @@
     starts = jnp.zeros((length, heads), F32)
     flows = jnp.zeros((heads, 1), F32)
     for h in range(heads):
-        state32, grad32, flow = received(state_ref, h)
+        state32, grad32, flow = received(state_ref, h, decode)
         q, k, v, d = (ref[0, :, matrix(h)] for ref in (query_ref, key_ref, value_ref, dout_ref))
         at_end = jnp.sum(q.astype(F32) * nt2(d, state32), axis=1, keepdims=True)
         at_start = jnp.sum(k.astype(F32) * nt2(v, grad32), axis=1, keepdims=True)
@@ -352,7 +369,7 @@
     for h in range(cols_ref.shape[2]):
         cols = matrix(h)
         entry, tail = (cols_ref[i, :, h : h + 1] for i in range(2))
-        state, grad = (x.astype(BF16) for x in received(state_ref, h)[:2])
+        state, grad = (x.astype(BF16) for x in received(state_ref, h, decode_high)[:2])
         for near_ref, out_ref, far, decay in (
             (dq_near_ref, dq_ref, nt(dout_ref[0, :, cols], state), entry),
             (dk_near_ref, dk_ref, nt(value_ref[0, :, cols], grad), tail),
@@ -377,7 +394,7 @@
     pin = lambda xs: tuple(pltpu.with_memory_space_constraint(x, pltpu.HBM) for x in xs)
     big = pin((query, key, value, dout))
     scratch = [pltpu.VMEM((4, length, width), BF16), pltpu.SemaphoreType.DMA((4, 8))]
-    packed = jax.ShapeDtypeStruct((count, 4 * HEAD_DIM + TAIL, LANES), I16)
+    packed = jax.ShapeDtypeStruct((count, SLOT, LANES), I16)
     pay = call(
         states_kernel,
         packed,

time: 113 us -> 121 us (1.071)
  blocking collectives: 29.9 us -> 33.3 us
  waiting for transfers between devices: 32.3 us -> 35.1 us
  Pallas kernels: 18.6 us -> 21 us
    all_to_all x1, blocking collectives: 29.9 us -> 33.3 us  [shards(): lax.all_to_all(carried, 'grp', split_axis=0, concat_axis=0, tiled=True)]
    all_to_all x1, waiting for transfers between devices: 20.1 us -> 22.9 us  [shards(): pay = lax.all_to_all(pay, 'grp', split_axis=0, concat_axis=0, tiled=True)]
  transfers between devices with their start and end apart: 5 -> 5, of which waited for: 4 -> 4; matrix products, arithmetic and copies ran while one was open for 0% -> 0% of each run, Pallas kernels for 8% -> 7%
where the time goes in v6:
time: 121 us
  waiting for transfers between devices  35.1 us (29%)
  blocking collectives  33.3 us (28%)
  starting transfers between devices  23.3 us (19%)
  Pallas kernels  21 us (17%)
  local copies, waits for them, and re-layouts  6.62 us (5%)
    all_to_all x1, blocking collectives, shards(): lax.all_to_all(carried, 'grp', split_axis=0, concat_axis=0, tiled=True)  33.3 us
    all_to_all x1, waiting for transfers between devices, shards(): pay = lax.all_to_all(pay, 'grp', split_axis=0, concat_axis=0, tiled=True)  22.9 us
    all_to_all x1, starting transfers between devices, shards(): pay = lax.all_to_all(pay, 'grp', split_axis=0, concat_axis=0, tiled=True)  9.16 us
    all_to_all x1, starting transfers between devices, shards(): lax.all_to_all(dbias, ALL, split_axis=0, concat_axis=0, tiled=True)  9.11 us
    all_to_all x1, waiting for transfers between devices, shards(): lax.all_to_all(dbias, ALL, split_axis=0, concat_axis=0, tiled=True)  7.17 us
    pallas_call x1, Pallas kernels, shards(): call(local_kernel, (near_like,) * 3 + (jax.ShapeDtypeStruct((2, heads, le...  6.85 us
    unnamed x26, local copies, waits for them, and re-layouts  6.62 us
    pallas_call x1, Pallas kernels, shards(): call(states_kernel, packed, [HBM] * 7, scratch_shapes=scratch + [pltpu.VM...  6.54 us
  transfers between devices with their start and end apart: 5, of which 4 were waited for; matrix products, arithmetic and copies ran while one was open for 0% of the time, Pallas kernels for 7%

profile of v6, /device:TPU:1, one launch (start us, length us, event | category | flops | bytes accessed | tf_op | source)
XLA Modules:
  0.0 121.0 jit_solution(17646070958045917486)
XLA Ops:
  0.6 6.5 %shard_map.111 = s16[8,592,128]{2,1,0:T(8,128)(2,1)} custom-call(bf16[1,128,2048]{2,1,0:T(8,128)(2,1)} %query_ref.5, bf16[1,128,2048]{2,1,0:T(8,128)(2,1)} %key_ref.7, bf16[1,128,2048]{2,1,0:T(8,128)(2,1)} %value_ref.7, bf16[1,128,2048]{2,1,0:T(8,128)(2,1)} %dout_ref.7, bf16[1,16,128]{2,1,0:T(8,128)(2,1)} %bitcast.3, f32[1,16]{1,0:T(1,128)} %bitcast.5, ...), custom_call_target="tpu_custom_call" | custom-call | tf_op jit(solution)/shard_map/pallas_call | solution.py:398
  7.2 0.0 copy-start.10
  7.2 0.0 copy-start.11
  7.2 0.0 copy-start.12
  7.2 9.2 %all-to-all-start = ((s16[8,592,128]{2,1,0:T(8,128)(2,1)}), s16[8,592,128]{2,1,0:T(8,128)(2,1)S(1)}, u32[]{:S(2)}, u32[]{:S(2)}) async-start(s16[8,592,128]{2,1,0:T(8,128)(2,1)} %shard_map.111), calls=%async_computation | async-start | bytes 2424832 | tf_op jit(solution)/shard_map/all_to_all | solution.py:413
  16.4 0.0 copy-done.10
  16.4 0.0 copy-done.11
  16.4 0.0 copy-done.12
  16.4 6.9 %shard_map.110 = (f32[128,2048]{1,0:T(8,128)S(1)}, f32[128,2048]{1,0:T(8,128)S(1)}, f32[128,2048]{1,0:T(8,128)S(1)}, f32[2,16,128]{2,1,0:T(8,128)S(1)}, f32[2,128,16]{2,1,0:T(8,128)S(1)}) custom-call(bf16[1,128,2048]{2,1,0:T(8,128)(2,1)} %query_ref.5, bf16[1,128,2048]{2,1,0:T(8,128)(2,1)} %key_ref.7, bf16[1,128,2048]{2,1,0:T(8,128)(2,1)} %value_ref.7, ...), custom_call_target="tpu_custom_call" | custom-call | tf_op jit(solution)/shard_map/pallas_call | solution.py:415
  23.3 0.0 copy-start.4
  23.3 1.0 copy-done.4
  24.2 0.0 copy-start.6
  24.2 1.0 copy-done.6
  25.2 0.0 copy-start.8
  25.2 1.0 copy-done.8
  26.2 22.9 %all-to-all-done.pay_ref = s16[8,592,128]{2,1,0:T(8,128)(2,1)S(1)} async-done(((s16[8,592,128]{2,1,0:T(8,128)(2,1)}), s16[8,592,128]{2,1,0:T(8,128)(2,1)S(1)}, u32[]{:S(2)}, u32[]{:S(2)}) %all-to-all-start) | async-done | bytes 1212448 | tf_op jit(solution)/shard_map/all_to_all | solution.py:413
  49.1 0.9 shard_map.112
  50.0 1.4 %collective-permute-start = (f32[264,128]{1,0:T(8,128)S(1)}, f32[264,128]{1,0:T(8,128)S(1)}, u32[]{:S(2)}, u32[]{:S(2)}) collective-permute-start(f32[264,128]{1,0:T(8,128)S(1)} %get-tuple-element.20), channel_id=1, source_target_pairs={{0,8},{8,16},{16,24},{24,0},{1,9},{9,17},{17,25},{25,1},{2,10},{10... | collective-permute-start | bytes 405512 | tf_op jit(solution)/shard_map/ppermute | solution.py:425
  51.4 2.6 %collective-permute-start.1 = (f32[264,128]{1,0:T(8,128)S(1)}, f32[264,128]{1,0:T(8,128)S(1)}, u32[]{:S(2)}, u32[]{:S(2)}) collective-permute-start(f32[264,128]{1,0:T(8,128)S(1)} %get-tuple-element.21), channel_id=1, source_target_pairs={{0,16},{8,24},{16,0},{24,8},{1,17},{9,25},{17,1},{25,9},{2,18},{10... | collective-permute-start | bytes 405512 | tf_op jit(solution)/shard_map/ppermute | solution.py:425
  54.0 1.1 collective-permute-start.2
  55.1 1.0 collective-permute-done.refs_0_
  56.1 4.0 %collective-permute-done.1.refs_1_ = f32[264,128]{1,0:T(8,128)S(1)} collective-permute-done((f32[264,128]{1,0:T(8,128)S(1)}, f32[264,128]{1,0:T(8,128)S(1)}, u32[]{:S(2)}, u32[]{:S(2)}) %collective-permute-start.1) | collective-permute-done | bytes 135200 | tf_op jit(solution)/shard_map/ppermute | solution.py:425
  60.1 0.0 collective-permute-done.2.refs_2_
  60.1 2.1 %shard_map.113 = s16[8,592,128]{2,1,0:T(8,128)(2,1)S(1)} custom-call(s16[8,592,128]{2,1,0:T(8,128)(2,1)S(1)} %all-to-all-done.pay_ref, f32[264,128]{1,0:T(8,128)S(1)} %collective-permute-done.refs_0_, f32[264,128]{1,0:T(8,128)S(1)} %collective-permute-done.1.refs_1_, f32[264,128]{1,0:T(8,128)S(1)} %collective-permute-done.2.refs_2_), custom_call_target="tpu_custom_call" | custom-call | tf_op jit(solution)/shard_map/pallas_call | solution.py:428
  62.2 0.0 copy-start
  62.2 0.0 copy-start.1
  62.2 0.0 copy-start.2
  62.3 0.0 copy-start.3
  62.3 33.3 %all_to_all.15.state_ref = s16[8,592,128]{2,1,0:T(8,128)(2,1)S(1)} all-to-all(s16[8,592,128]{2,1,0:T(8,128)(2,1)S(1)} %shard_map.113), channel_id=1, replica_groups=mesh['dp'=8,'seg'=4,'grp'=8] {'grp'}, dimensions={0} | all-to-all | bytes 2424832 | tf_op jit(solution)/shard_map/all_to_all | solution.py:434
  95.6 0.0 copy-done
  95.6 0.0 copy-done.1
  95.6 0.0 copy-done.2
  95.6 0.0 copy-done.3
  95.6 2.5 %shard_map.115 = (bf16[1,16,128]{2,1,0:T(8,128)(2,1)}, f32[256,1,16]{2,1,0:T(1,128)}) custom-call(bf16[1,128,2048]{2,1,0:T(8,128)(2,1)S(1)} %copy-done.3, bf16[1,128,2048]{2,1,0:T(8,128)(2,1)S(1)} %copy-done, bf16[1,128,2048]{2,1,0:T(8,128)(2,1)S(1)} %copy-done.1, bf16[1,128,2048]{2,1,0:T(8,128)(2,1)S(1)} %copy-done.2, ...), custom_call_target="tpu_custom_call" | custom-call | tf_op jit(solution)/shard_map/pallas_call | solution.py:435
  98.1 9.1 %all-to-all-start.2 = ((f32[256,1,16]{2,1,0:T(1,128)}), f32[256,1,16]{2,1,0:T(1,128)S(1)}, u32[]{:S(2)}, u32[]{:S(2)}) async-start(f32[256,1,16]{2,1,0:T(1,128)} %get-tuple-element.30), calls=%async_computation.2 | async-start | bytes 262144 | tf_op jit(solution)/shard_map/all_to_all | solution.py:443
  107.2 0.0 copy-start.5
  107.2 1.2 %copy-done.5 = f32[128,2048]{1,0:T(8,128)S(1)} copy-done((f32[128,2048]{1,0:T(8,128)S(1)}, f32[128,2048]{1,0:T(8,128)}, u32[]{:S(2)}) %copy-start.5) | copy-done | bytes 1048600
  108.4 0.0 copy-start.7
  108.4 1.2 %copy-done.7 = f32[128,2048]{1,0:T(8,128)S(1)} copy-done((f32[128,2048]{1,0:T(8,128)S(1)}, f32[128,2048]{1,0:T(8,128)}, u32[]{:S(2)}) %copy-start.7) | copy-done | bytes 1048600
  109.7 0.0 copy-start.9
  109.7 1.2 %copy-done.9 = f32[128,2048]{1,0:T(8,128)S(1)} copy-done((f32[128,2048]{1,0:T(8,128)S(1)}, f32[128,2048]{1,0:T(8,128)}, u32[]{:S(2)}) %copy-start.9) | copy-done | bytes 1048600
  110.9 2.2 %shard_map.114 = (bf16[1,128,2048]{2,1,0:T(8,128)(2,1)}, bf16[1,128,2048]{2,1,0:T(8,128)(2,1)}, bf16[1,128,2048]{2,1,0:T(8,128)(2,1)}) custom-call(bf16[1,128,2048]{2,1,0:T(8,128)(2,1)S(1)} %copy-done, bf16[1,128,2048]{2,1,0:T(8,128)(2,1)S(1)} %copy-done.1, bf16[1,128,2048]{2,1,0:T(8,128)(2,1)S(1)} %copy-done.2, ...), custom_call_target="tpu_custom_call" | custom-call | tf_op jit(solution)/shard_map/pallas_call | solution.py:445
  113.0 7.2 %all-to-all-done.2 = f32[256,1,16]{2,1,0:T(1,128)S(1)} async-done(((f32[256,1,16]{2,1,0:T(1,128)}), f32[256,1,16]{2,1,0:T(1,128)S(1)}, u32[]{:S(2)}, u32[]{:S(2)}) %all-to-all-start.2) | async-done | bytes 16416 | tf_op jit(solution)/shard_map/all_to_all | solution.py:443
  120.2 0.8 reduce_sum.9
Async XLA Ops:
  7.2 9.2 %copy-start.10 = (bf16[1,128,16]{1,2,0:T(8,128)(2,1)S(1)}, bf16[1,128,16]{1,2,0:T(8,128)(2,1)}, u32[]{:S(2)}) copy-start(bf16[1,128,16]{1,2,0:T(8,128)(2,1)} %param.11) | copy-start | bytes 12292
  7.2 9.2 %copy-start.11 = (f32[16]{0:T(128)S(1)}, f32[16]{0:T(128)}, u32[]{:S(2)}) copy-start(f32[16]{0:T(128)} %param.12) | copy-start | bytes 196
  7.2 9.2 %copy-start.12 = (s32[1,4]{1,0:T(1,128)S(1)}, s32[1,4]{1,0:T(1,128)}, u32[]{:S(2)}) copy-start(s32[1,4]{1,0:T(1,128)} %offsets_ref.3) | copy-start | bytes 52
  7.2 41.9 %all-to-all-start = ((s16[8,592,128]{2,1,0:T(8,128)(2,1)}), s16[8,592,128]{2,1,0:T(8,128)(2,1)S(1)}, u32[]{:S(2)}, u32[]{:S(2)}) async-start(s16[8,592,128]{2,1,0:T(8,128)(2,1)} %shard_map.111), calls=%async_computation | async-start | bytes 2424832 | tf_op jit(solution)/shard_map/all_to_all | solution.py:413
  23.3 1.0 copy-start.4
  24.2 1.0 copy-start.6
  25.2 1.0 copy-start.8
  50.0 6.1 %collective-permute-start = (f32[264,128]{1,0:T(8,128)S(1)}, f32[264,128]{1,0:T(8,128)S(1)}, u32[]{:S(2)}, u32[]{:S(2)}) collective-permute-start(f32[264,128]{1,0:T(8,128)S(1)} %get-tuple-element.20), channel_id=1, source_target_pairs={{0,8},{8,16},{16,24},{24,0},{1,9},{9,17},{17,25},{25,1},{2,10},{10... | collective-permute-start | bytes 405512 | tf_op jit(solution)/shard_map/ppermute | solution.py:425
  51.4 8.7 %collective-permute-start.1 = (f32[264,128]{1,0:T(8,128)S(1)}, f32[264,128]{1,0:T(8,128)S(1)}, u32[]{:S(2)}, u32[]{:S(2)}) collective-permute-start(f32[264,128]{1,0:T(8,128)S(1)} %get-tuple-element.21), channel_id=1, source_target_pairs={{0,16},{8,24},{16,0},{24,8},{1,17},{9,25},{17,1},{25,9},{2,18},{10... | collective-permute-start | bytes 405512 | tf_op jit(solution)/shard_map/ppermute | solution.py:425
  54.0 6.1 %collective-permute-start.2 = (f32[264,128]{1,0:T(8,128)S(1)}, f32[264,128]{1,0:T(8,128)S(1)}, u32[]{:S(2)}, u32[]{:S(2)}) collective-permute-start(f32[264,128]{1,0:T(8,128)S(1)} %get-tuple-element.22), channel_id=1, source_target_pairs={{0,24},{8,0},{16,8},{24,16},{1,25},{9,1},{17,9},{25,17},{2,26},{10... | collective-permute-start | bytes 405512 | tf_op jit(solution)/shard_map/ppermute | solution.py:425
  62.2 33.4 %copy-start = (bf16[1,128,2048]{2,1,0:T(8,128)(2,1)S(1)}, bf16[1,128,2048]{2,1,0:T(8,128)(2,1)}, u32[]{:S(2)}) copy-start(bf16[1,128,2048]{2,1,0:T(8,128)(2,1)} %key_ref.7) | copy-start | bytes 1572868
  62.2 33.3 %copy-start.1 = (bf16[1,128,2048]{2,1,0:T(8,128)(2,1)S(1)}, bf16[1,128,2048]{2,1,0:T(8,128)(2,1)}, u32[]{:S(2)}) copy-start(bf16[1,128,2048]{2,1,0:T(8,128)(2,1)} %value_ref.7) | copy-start | bytes 1572868
  62.2 33.3 %copy-start.2 = (bf16[1,128,2048]{2,1,0:T(8,128)(2,1)S(1)}, bf16[1,128,2048]{2,1,0:T(8,128)(2,1)}, u32[]{:S(2)}) copy-start(bf16[1,128,2048]{2,1,0:T(8,128)(2,1)} %dout_ref.7) | copy-start | bytes 1572868
  62.3 33.3 %copy-start.3 = (bf16[1,128,2048]{2,1,0:T(8,128)(2,1)S(1)}, bf16[1,128,2048]{2,1,0:T(8,128)(2,1)}, u32[]{:S(2)}) copy-start(bf16[1,128,2048]{2,1,0:T(8,128)(2,1)} %query_ref.5) | copy-start | bytes 1572868
  98.1 22.1 %all-to-all-start.2 = ((f32[256,1,16]{2,1,0:T(1,128)}), f32[256,1,16]{2,1,0:T(1,128)S(1)}, u32[]{:S(2)}, u32[]{:S(2)}) async-start(f32[256,1,16]{2,1,0:T(1,128)} %get-tuple-element.30), calls=%async_computation.2 | async-start | bytes 262144 | tf_op jit(solution)/shard_map/all_to_all | solution.py:443
  107.2 1.2 %copy-start.5 = (f32[128,2048]{1,0:T(8,128)S(1)}, f32[128,2048]{1,0:T(8,128)}, u32[]{:S(2)}) copy-start(f32[128,2048]{1,0:T(8,128)} %copy-done.4) | copy-start | bytes 3145732
  108.4 1.2 %copy-start.7 = (f32[128,2048]{1,0:T(8,128)S(1)}, f32[128,2048]{1,0:T(8,128)}, u32[]{:S(2)}) copy-start(f32[128,2048]{1,0:T(8,128)} %copy-done.6) | copy-start | bytes 3145732
  109.7 1.2 %copy-start.9 = (f32[128,2048]{1,0:T(8,128)S(1)}, f32[128,2048]{1,0:T(8,128)}, u32[]{:S(2)}) copy-start(f32[128,2048]{1,0:T(8,128)} %copy-done.8) | copy-start | bytes 3145732

commit v7 on v5

--- a/solution.py
+++ b/solution.py
@@ -1,3 +1,5 @@
+import functools
+
 import jax
 import jax.numpy as jnp
 from jax import lax
@@ -122,6 +124,26 @@
 
 def place():
     return lax.axis_index("seg") * lax.axis_size("grp") + lax.axis_index("grp")
+
+
+def spread(whole, *piece_refs):
+    count, mine = lax.axis_size("grp"), lax.axis_index("grp")
+    for d, ref in enumerate(piece_refs):
+        ref[...] = whole[lax.rem(mine + d, count)]
+
+
+def gather(whole, *piece_refs):
+    count, mine = lax.axis_size("grp"), lax.axis_index("grp")
+    for d, ref in enumerate(piece_refs):
+        whole[lax.rem(mine + count - d, count)] = ref[...]
+
+
+def exchange(pieces):
+    count = len(pieces)
+    got = {0: pieces[0]}
+    for d in sorted(range(1, count), key=lambda d: (-min(d, count - d), d)):
+        got[d] = lax.ppermute(pieces[d], "grp", [(i, (i + d) % count) for i in range(count)])
+    return [got[d] for d in range(count)]
 
 
 def decays(gates, bias, offsets_ref):
@@ -166,9 +188,9 @@
 
 
 def states_kernel(
-    query_ref, key_ref, value_ref, dout_ref, gate_ref, bias_ref, offsets_ref,
-    pay_ref, held, sems, gate_held, bias_held, offsets_held, small_sems, pay, pay_sems,
+    query_ref, key_ref, value_ref, dout_ref, gate_ref, bias_ref, offsets_ref, *refs
 ):
+    *piece_refs, held, sems, gate_held, bias_held, offsets_held, small_sems, pay = refs
     heads = bias_ref.shape[1]
     small = [
         pltpu.make_async_copy(gate_ref.at[0], gate_held, small_sems.at[0]),
@@ -182,7 +204,7 @@
         copy.wait()
     _, _, _, _, cumulative, _, entry, tail, passes = decays(gate_held[...], bias_held[...], offsets_held)
     coarse, fine = log_parts(jnp.where(passes, jnp.maximum(cumulative[-1:, :], -120.0), -128.0))
-    powers, sent = {}, []
+    powers = {}
     for h in range(heads):
         arrive(copies, h, heads)
         cols = matrix(h)
@@ -197,18 +219,16 @@
                 *(powers[i] for i in range(4)),
                 *(x[:, i : i + 1] for i in (h - 1, h) for x in (coarse, fine)),
             )
-            sent.append(pltpu.make_async_copy(pay.at[slot], pay_ref.at[slot], pay_sems.at[slot]))
-            sent[-1].start()
-    for copy in sent:
-        copy.wait()
+    spread(pay, *piece_refs)
 
 
 def chunk_logs(tails, m):
     return [log_whole(t[4 + 2 * m : 5 + 2 * m], t[5 + 2 * m : 6 + 2 * m]) for t in tails]
 
 
-def totals_kernel(pay_ref, _, *send_refs):
-    count = pay_ref.shape[0]
+def totals_kernel(count, *refs):
+    piece_refs, (pay_ref, *send_refs) = refs[:count], refs[count + 1 :]
+    gather(pay_ref, *piece_refs)
     tails = [wide(pay_ref[c, tail_of(pay_ref), :]) for c in range(count)]
     mine, segments = lax.axis_index("seg"), lax.axis_size("seg")
     at = iota((8, LANES), 0)
@@ -230,8 +250,8 @@
         send_ref[pl.ds(2 * HEAD_DIM, 8), :] = logs
 
 
-def scan_kernel(pay_ref, *refs):
-    *got_refs, out_ref, held = refs
+def scan_kernel(segments, pay_ref, *refs):
+    got_refs, (*piece_refs, out_ref, held) = refs[: segments - 1], refs[segments - 1 :]
     count = pay_ref.shape[0]
     mine = lax.axis_index("seg")
     tails = [wide(pay_ref[c, tail_of(pay_ref), :]) for c in range(count)]
@@ -264,6 +284,7 @@
         out_ref[c, tail_of(out_ref), :] = rows16(
             *powers[c], *(part[2 * c + m : 2 * c + m + 1] for m in range(2) for part in parts)
         )
+    spread(out_ref, *piece_refs)
 
 
 def local_kernel(
@@ -314,9 +335,9 @@
     return *pair, decode2(*(tail[i : i + 1, :1] for i in range(4 + 3 * m, 7 + 3 * m)))
 
 
-def gates_kernel(
-    query_ref, key_ref, value_ref, dout_ref, rows_ref, cols_ref, state_ref, dgate_ref, dbias_ref
-):
+def gates_kernel(query_ref, key_ref, value_ref, dout_ref, rows_ref, cols_ref, *refs):
+    *piece_refs, dgate_ref, dbias_ref, state_ref = refs
+    gather(state_ref, *piece_refs)
     heads, length = dgate_ref.shape[1:]
     lane = iota((length, heads), 1)
     sublane = iota((heads, 1), 0)
@@ -346,9 +367,10 @@
 
 
 def output_kernel(
-    key_ref, value_ref, dout_ref, cols_ref, state_ref, dq_near_ref, dk_near_ref, dv_near_ref,
-    dq_ref, dk_ref, dv_ref,
+    key_ref, value_ref, dout_ref, cols_ref, dq_near_ref, dk_near_ref, dv_near_ref, *refs
 ):
+    *piece_refs, dq_ref, dk_ref, dv_ref, state_ref = refs
+    gather(state_ref, *piece_refs)
     for h in range(cols_ref.shape[2]):
         cols = matrix(h)
         entry, tail = (cols_ref[i, :, h : h + 1] for i in range(2))
@@ -377,10 +399,11 @@
     pin = lambda xs: tuple(pltpu.with_memory_space_constraint(x, pltpu.HBM) for x in xs)
     big = pin((query, key, value, dout))
     scratch = [pltpu.VMEM((4, length, width), BF16), pltpu.SemaphoreType.DMA((4, 8))]
-    packed = jax.ShapeDtypeStruct((count, 4 * HEAD_DIM + TAIL, LANES), I16)
-    pay = call(
+    piece = jax.ShapeDtypeStruct((4 * HEAD_DIM + TAIL, LANES), I16)
+    packed = jax.ShapeDtypeStruct((count,) + piece.shape, I16)
+    pieces = call(
         states_kernel,
-        packed,
+        (piece,) * count,
         [HBM] * 7,
         scratch_shapes=scratch
         + [
@@ -389,11 +412,9 @@
             pltpu.SMEM(offsets.shape, jnp.int32),
             pltpu.SemaphoreType.DMA((3,)),
             pltpu.VMEM(packed.shape, I16),
-            pltpu.SemaphoreType.DMA((count,)),
         ],
-        out_specs=HBM,
     )(*big, *pin(small))
-    pay = lax.all_to_all(pay, "grp", split_axis=0, concat_axis=0, tiled=True)
+    pieces = exchange(pieces)
     near_like = jax.ShapeDtypeStruct((length, width), F32)
     *near, rows, cols = call(
         local_kernel,
@@ -403,29 +424,37 @@
         scratch_shapes=scratch,
     )(*big, *small)
     total = jax.ShapeDtypeStruct((2 * HEAD_DIM + 8, LANES), F32)
-    sends = call(totals_kernel, (total,) * (segments - 1), [VMEM, pl.BlockSpec(memory_space=pl.ANY)])(pay, rows)
+    pay, *sends = call(
+        functools.partial(totals_kernel, count),
+        (packed,) + (total,) * (segments - 1),
+        [VMEM] * count + [pl.BlockSpec(memory_space=pl.ANY)],
+    )(*pieces, rows)
     got = [
         lax.ppermute(send, "seg", [(i, (i + d) % segments) for i in range(segments)])
         for d, send in enumerate(sends, 1)
     ]
     carried = call(
-        scan_kernel,
-        packed,
+        functools.partial(scan_kernel, segments),
+        (piece,) * count,
         [VMEM] * segments,
-        scratch_shapes=[pltpu.VMEM((count, HEAD_DIM, LANES), F32)],
+        scratch_shapes=[pltpu.VMEM(packed.shape, I16), pltpu.VMEM((count, HEAD_DIM, LANES), F32)],
     )(pay, *got)
-    carried = lax.all_to_all(carried, "grp", split_axis=0, concat_axis=0, tiled=True)
+    carried = exchange(carried)
+    assembled = [pltpu.VMEM(packed.shape, I16)]
     dgate, dbias = call(
         gates_kernel,
         (
             jax.ShapeDtypeStruct(gates.shape, BF16),
             jax.ShapeDtypeStruct((lax.axis_size(ALL), 1, heads), F32),
         ),
-        [VMEM] * 7,
-    )(query, key, value, dout, rows, cols, carried)
+        [VMEM] * (6 + count),
+        scratch_shapes=assembled,
+    )(query, key, value, dout, rows, cols, *carried)
     everywhere = lax.all_to_all(dbias, ALL, split_axis=0, concat_axis=0, tiled=True)
     like = jax.ShapeDtypeStruct(query.shape, BF16)
-    dq, dk, dv = call(output_kernel, (like,) * 3, [VMEM] * 8)(key, value, dout, cols, carried, *near)
+    dq, dk, dv = call(output_kernel, (like,) * 3, [VMEM] * (7 + count), scratch_shapes=assembled)(
+        key, value, dout, cols, *near, *carried
+    )
     return dq, dk, dv, jnp.swapaxes(dgate, 1, 2), jnp.sum(everywhere, axis=(0, 1))
 
 

time: 113 us -> 116 us (1.027)
  blocking collectives: 29.9 us -> 0 us
  starting transfers between devices: 23.9 us -> 47.8 us
  waiting for transfers between devices: 32.3 us -> 39.8 us
  local copies, waits for them, and re-layouts: 6.61 us -> 7.78 us
    ppermute x0 -> x14, waiting for transfers between devices: none -> 30.1 us  [exchange(): lax.ppermute(pieces[d], 'grp', [(i, (i + d) % count) for i in range(count)])]
    all_to_all x1 -> x0, blocking collectives: 29.9 us -> none  [shards(): lax.all_to_all(carried, 'grp', split_axis=0, concat_axis=0, tiled=True)]
    ppermute x0 -> x14, starting transfers between devices: none -> 29.8 us  [exchange(): lax.ppermute(pieces[d], 'grp', [(i, (i + d) % count) for i in range(count)])]
    all_to_all x1 -> x0, waiting for transfers between devices: 20.1 us -> none  [shards(): pay = lax.all_to_all(pay, 'grp', split_axis=0, concat_axis=0, tiled=True)]
    all_to_all x1 -> x0, starting transfers between devices: 9.16 us -> none  [shards(): pay = lax.all_to_all(pay, 'grp', split_axis=0, concat_axis=0, tiled=True)]
    all_to_all x1, starting transfers between devices: 9.67 us -> 12.8 us  [shards(): lax.all_to_all(dbias, ALL, split_axis=0, concat_axis=0, tiled=True)]
    all_to_all x1, waiting for transfers between devices: 7.17 us -> 4.9 us  [shards(): lax.all_to_all(dbias, ALL, split_axis=0, concat_axis=0, tiled=True)]
    unnamed x26 -> x36, local copies, waits for them, and re-layouts: 6.61 us -> 7.78 us
  transfers between devices with their start and end apart: 5 -> 18, of which waited for: 4 -> 11; matrix products, arithmetic and copies ran while one was open for 0% -> 0% of each run, Pallas kernels for 8% -> 8%
where the time goes in v7:
time: 116 us
  starting transfers between devices  47.8 us (41%)
  waiting for transfers between devices  39.8 us (34%)
  Pallas kernels  18.1 us (16%)
  local copies, waits for them, and re-layouts  7.78 us (7%)
  other arithmetic  1.7 us (1%)
    ppermute x14, waiting for transfers between devices, exchange(): lax.ppermute(pieces[d], 'grp', [(i, (i + d) % count) for i in range(count)])  30.1 us
    ppermute x14, starting transfers between devices, exchange(): lax.ppermute(pieces[d], 'grp', [(i, (i + d) % count) for i in range(count)])  29.8 us
    all_to_all x1, starting transfers between devices, shards(): lax.all_to_all(dbias, ALL, split_axis=0, concat_axis=0, tiled=True)  12.8 us
    unnamed x36, local copies, waits for them, and re-layouts  7.78 us
    pallas_call x1, Pallas kernels, shards(): call(local_kernel, (near_like,) * 3 + (jax.ShapeDtypeStruct((2, heads, le...  6.85 us
    pallas_call x1, Pallas kernels, shards(): call(states_kernel, (piece,) * count, [HBM] * 7, scratch_shapes=scratch +...  5.34 us
    ppermute x3, starting transfers between devices, shards(): lax.ppermute(send, 'seg', [(i, (i + d) % segments) for i in range(segment...  5.24 us
    all_to_all x1, waiting for transfers between devices, shards(): lax.all_to_all(dbias, ALL, split_axis=0, concat_axis=0, tiled=True)  4.9 us
  transfers between devices with their start and end apart: 18, of which 11 were waited for; matrix products, arithmetic and copies ran while one was open for 0% of the time, Pallas kernels for 8%

profile of v7, /device:TPU:1, one launch (start us, length us, event | category | flops | bytes accessed | tf_op | source)
XLA Modules:
  0.0 115.9 jit_solution(4859896022838534113)
XLA Ops:
  0.7 5.3 %shard_map.111 = (s16[528,128]{1,0:T(8,128)(2,1)S(1)}, s16[528,128]{1,0:T(8,128)(2,1)S(1)}, s16[528,128]{1,0:T(8,128)(2,1)S(1)}, s16[528,128]{1,0:T(8,128)(2,1)S...) custom-call(bf16[1,128,2048]{2,1,0:T(8,128)(2,1)} %query_ref.5, ...), custom_call_target="tpu_custom_call" | custom-call | tf_op jit(solution)/shard_map/pallas_call | solution.py:404
  6.0 2.5 %collective-permute-start = (s16[528,128]{1,0:T(8,128)(2,1)S(1)}, s16[528,128]{1,0:T(8,128)(2,1)S(1)}, u32[]{:S(2)}, u32[]{:S(2)}) collective-permute-start(s16[528,128]{1,0:T(8,128)(2,1)S(1)} %get-tuple-element.40), channel_id=1, source_target_pairs={{0,1},{1,2},{2,3},{3,4},{4,5},{5,6},{6,7},{7,0},{8,9},{9,10},{10,1... | collective-permute-start | bytes 405512 | tf_op jit(solution)/shard_map/ppermute | solution.py:145
  8.5 3.0 %collective-permute-start.1 = (s16[528,128]{1,0:T(8,128)(2,1)S(1)}, s16[528,128]{1,0:T(8,128)(2,1)S(1)}, u32[]{:S(2)}, u32[]{:S(2)}) collective-permute-start(s16[528,128]{1,0:T(8,128)(2,1)S(1)} %get-tuple-element.41), channel_id=1, source_target_pairs={{0,2},{1,3},{2,4},{3,5},{4,6},{5,7},{6,0},{7,1},{8,10},{9,11},{10,... | collective-permute-start | bytes 405512 | tf_op jit(solution)/shard_map/ppermute | solution.py:145
  11.5 3.8 %collective-permute-start.2 = (s16[528,128]{1,0:T(8,128)(2,1)S(1)}, s16[528,128]{1,0:T(8,128)(2,1)S(1)}, u32[]{:S(2)}, u32[]{:S(2)}) collective-permute-start(s16[528,128]{1,0:T(8,128)(2,1)S(1)} %get-tuple-element.42), channel_id=1, source_target_pairs={{0,3},{1,4},{2,5},{3,6},{4,7},{5,0},{6,1},{7,2},{8,11},{9,12},{10,... | collective-permute-start | bytes 405512 | tf_op jit(solution)/shard_map/ppermute | solution.py:145
  15.3 0.5 collective-permute-start.3
  15.8 4.5 %collective-permute-start.4 = (s16[528,128]{1,0:T(8,128)(2,1)S(1)}, s16[528,128]{1,0:T(8,128)(2,1)S(1)}, u32[]{:S(2)}, u32[]{:S(2)}) collective-permute-start(s16[528,128]{1,0:T(8,128)(2,1)S(1)} %get-tuple-element.44), channel_id=1, source_target_pairs={{0,5},{1,6},{2,7},{3,0},{4,1},{5,2},{6,3},{7,4},{8,13},{9,14},{10,... | collective-permute-start | bytes 405512 | tf_op jit(solution)/shard_map/ppermute | solution.py:145
  20.2 0.0 collective-permute-done.refs_1_
  20.2 2.4 %collective-permute-start.5 = (s16[528,128]{1,0:T(8,128)(2,1)S(1)}, s16[528,128]{1,0:T(8,128)(2,1)S(1)}, u32[]{:S(2)}, u32[]{:S(2)}) collective-permute-start(s16[528,128]{1,0:T(8,128)(2,1)S(1)} %get-tuple-element.45), channel_id=1, source_target_pairs={{0,6},{1,7},{2,0},{3,1},{4,2},{5,3},{6,4},{7,5},{8,14},{9,15},{10,... | collective-permute-start | bytes 405512 | tf_op jit(solution)/shard_map/ppermute | solution.py:145
  22.6 0.0 collective-permute-done.1.refs_2_
  22.6 0.9 collective-permute-start.6
  23.6 6.9 %shard_map.110 = (f32[128,2048]{1,0:T(8,128)S(1)}, f32[128,2048]{1,0:T(8,128)S(1)}, f32[128,2048]{1,0:T(8,128)S(1)}, f32[2,16,128]{2,1,0:T(8,128)S(1)}, f32[2,128,16]{2,1,0:T(8,128)S(1)}) custom-call(bf16[1,128,2048]{2,1,0:T(8,128)(2,1)} %query_ref.5, bf16[1,128,2048]{2,1,0:T(8,128)(2,1)} %key_ref.7, bf16[1,128,2048]{2,1,0:T(8,128)(2,1)} %value_ref.7, ...), custom_call_target="tpu_custom_call" | custom-call | tf_op jit(solution)/shard_map/pallas_call | solution.py:419
  30.4 1.0 copy-done.4
  31.4 1.0 copy-done.6
  32.4 0.5 collective-permute-done.3.refs_4_
  32.9 0.0 collective-permute-done.4.refs_5_
  32.9 7.9 %collective-permute-done.5.refs_6_ = s16[528,128]{1,0:T(8,128)(2,1)S(1)} collective-permute-done((s16[528,128]{1,0:T(8,128)(2,1)S(1)}, s16[528,128]{1,0:T(8,128)(2,1)S(1)}, u32[]{:S(2)}, u32[]{:S(2)}) %collective-permute-start.5) | collective-permute-done | bytes 135200 | tf_op jit(solution)/shard_map/ppermute | solution.py:145
  40.7 1.1 collective-permute-done.6.refs_7_
  41.9 0.5 shard_map.112
  42.3 1.6 %collective-permute-start.7 = (f32[264,128]{1,0:T(8,128)S(1)}, f32[264,128]{1,0:T(8,128)S(1)}, u32[]{:S(2)}, u32[]{:S(2)}) collective-permute-start(f32[264,128]{1,0:T(8,128)S(1)} %get-tuple-element.49), channel_id=1, source_target_pairs={{0,8},{8,16},{16,24},{24,0},{1,9},{9,17},{17,25},{25,1},{2,10},{10... | collective-permute-start | bytes 405512 | tf_op jit(solution)/shard_map/ppermute | solution.py:433
  43.9 2.6 %collective-permute-start.8 = (f32[264,128]{1,0:T(8,128)S(1)}, f32[264,128]{1,0:T(8,128)S(1)}, u32[]{:S(2)}, u32[]{:S(2)}) collective-permute-start(f32[264,128]{1,0:T(8,128)S(1)} %get-tuple-element.50), channel_id=1, source_target_pairs={{0,16},{8,24},{16,0},{24,8},{1,17},{9,25},{17,1},{25,9},{2,18},{10... | collective-permute-start | bytes 405512 | tf_op jit(solution)/shard_map/ppermute | solution.py:433
  46.5 1.1 collective-permute-start.9
  47.6 0.8 collective-permute-done.7.refs_0_
  48.4 4.0 %collective-permute-done.8.refs_1_ = f32[264,128]{1,0:T(8,128)S(1)} collective-permute-done((f32[264,128]{1,0:T(8,128)S(1)}, f32[264,128]{1,0:T(8,128)S(1)}, u32[]{:S(2)}, u32[]{:S(2)}) %collective-permute-start.8) | collective-permute-done | bytes 135200 | tf_op jit(solution)/shard_map/ppermute | solution.py:433
  52.4 0.0 collective-permute-done.9.refs_2_
  52.4 1.2 %shard_map.113 = (s16[528,128]{1,0:T(8,128)(2,1)S(1)}, s16[528,128]{1,0:T(8,128)(2,1)S(1)}, s16[528,128]{1,0:T(8,128)(2,1)S(1)}, s16[528,128]{1,0:T(8,128)(2,1)S...) custom-call(s16[8,528,128]{2,1,0:T(8,128)(2,1)S(1)} %get-tuple-eleme, ...), custom_call_target="tpu_custom_call" | custom-call | tf_op jit(solution)/shard_map/pallas_call | solution.py:436
  53.6 3.3 %collective-permute-start.10 = (s16[528,128]{1,0:T(8,128)(2,1)S(1)}, s16[528,128]{1,0:T(8,128)(2,1)S(1)}, u32[]{:S(2)}, u32[]{:S(2)}) collective-permute-start(s16[528,128]{1,0:T(8,128)(2,1)S(1)} %get-tuple-element.53), channel_id=1, source_target_pairs={{0,1},{1,2},{2,3},{3,4},{4,5},{5,6},{6,7},{7,0},{8,9},{9,10},{10,1... | collective-permute-start | bytes 405512 | tf_op jit(solution)/shard_map/ppermute | solution.py:145
  56.9 0.9 collective-permute-start.11
  57.8 0.1 collective-permute-start.12
  57.9 4.5 %collective-permute-start.13 = (s16[528,128]{1,0:T(8,128)(2,1)S(1)}, s16[528,128]{1,0:T(8,128)(2,1)S(1)}, u32[]{:S(2)}, u32[]{:S(2)}) collective-permute-start(s16[528,128]{1,0:T(8,128)(2,1)S(1)} %get-tuple-element.56), channel_id=1, source_target_pairs={{0,4},{1,5},{2,6},{3,7},{4,0},{5,1},{6,2},{7,3},{8,12},{9,13},{10,... | collective-permute-start | bytes 405512 | tf_op jit(solution)/shard_map/ppermute | solution.py:145
  62.4 1.0 collective-permute-start.14
  63.4 2.5 %collective-permute-start.15 = (s16[528,128]{1,0:T(8,128)(2,1)S(1)}, s16[528,128]{1,0:T(8,128)(2,1)S(1)}, u32[]{:S(2)}, u32[]{:S(2)}) collective-permute-start(s16[528,128]{1,0:T(8,128)(2,1)S(1)} %get-tuple-element.58), channel_id=1, source_target_pairs={{0,6},{1,7},{2,0},{3,1},{4,2},{5,3},{6,4},{7,5},{8,14},{9,15},{10,... | collective-permute-start | bytes 405512 | tf_op jit(solution)/shard_map/ppermute | solution.py:145
  65.8 1.6 %collective-permute-done.11.refs_2_ = s16[528,128]{1,0:T(8,128)(2,1)S(1)} collective-permute-done((s16[528,128]{1,0:T(8,128)(2,1)S(1)}, s16[528,128]{1,0:T(8,128)(2,1)S(1)}, u32[]{:S(2)}, u32[]{:S(2)}) %collective-permute-start.11) | collective-permute-done | bytes 135200 | tf_op jit(solution)/shard_map/ppermute | solution.py:145
  67.4 4.5 %collective-permute-done.12.refs_3_ = s16[528,128]{1,0:T(8,128)(2,1)S(1)} collective-permute-done((s16[528,128]{1,0:T(8,128)(2,1)S(1)}, s16[528,128]{1,0:T(8,128)(2,1)S(1)}, u32[]{:S(2)}, u32[]{:S(2)}) %collective-permute-start.12) | collective-permute-done | bytes 135200 | tf_op jit(solution)/shard_map/ppermute | solution.py:145
  71.9 3.7 %collective-permute-done.13.refs_4_ = s16[528,128]{1,0:T(8,128)(2,1)S(1)} collective-permute-done((s16[528,128]{1,0:T(8,128)(2,1)S(1)}, s16[528,128]{1,0:T(8,128)(2,1)S(1)}, u32[]{:S(2)}, u32[]{:S(2)}) %collective-permute-start.13) | collective-permute-done | bytes 135200 | tf_op jit(solution)/shard_map/ppermute | solution.py:145
  75.6 0.0 collective-permute-done.14.refs_5_
  75.6 8.9 %collective-permute-done.15.refs_6_ = s16[528,128]{1,0:T(8,128)(2,1)S(1)} collective-permute-done((s16[528,128]{1,0:T(8,128)(2,1)S(1)}, s16[528,128]{1,0:T(8,128)(2,1)S(1)}, u32[]{:S(2)}, u32[]{:S(2)}) %collective-permute-start.15) | collective-permute-done | bytes 135200 | tf_op jit(solution)/shard_map/ppermute | solution.py:145
  84.6 1.9 %collective-permute-done.16.refs_7_ = s16[528,128]{1,0:T(8,128)(2,1)S(1)} collective-permute-done((s16[528,128]{1,0:T(8,128)(2,1)S(1)}, s16[528,128]{1,0:T(8,128)(2,1)S(1)}, u32[]{:S(2)}, u32[]{:S(2)}) %collective-permute-start.16) | collective-permute-done | bytes 135200 | tf_op jit(solution)/shard_map/ppermute | solution.py:145
  86.5 1.9 %shard_map.115 = (bf16[1,16,128]{2,1,0:T(8,128)(2,1)}, f32[256,1,16]{2,1,0:T(1,128)S(1)}) custom-call(bf16[1,128,2048]{2,1,0:T(8,128)(2,1)S(1)} %copy-done.3, bf16[1,128,2048]{2,1,0:T(8,128)(2,1)S(1)} %copy-done, bf16[1,128,2048]{2,1,0:T(8,128)(2,1)S(1)} %copy-done.1, bf16[1,128,2048]{2,1,0:T(8,128)(2,1)S(1)} %copy-done.2, ...), custom_call_target="tpu_custom_call" | custom-call | tf_op jit(solution)/shard_map/pallas_call | solution.py:444
  88.4 0.6 copy-done.14
  89.1 12.8 %all-to-all-start = ((f32[256,1,16]{2,1,0:T(1,128)}), f32[256,1,16]{2,1,0:T(1,128)}, u32[]{:S(2)}, u32[]{:S(2)}) async-start(f32[256,1,16]{2,1,0:T(1,128)} %copy-done.14), calls=%async_computation | async-start | bytes 262144 | tf_op jit(solution)/shard_map/all_to_all | solution.py:453
  101.9 1.2 %copy-done.5 = f32[128,2048]{1,0:T(8,128)S(1)} copy-done((f32[128,2048]{1,0:T(8,128)S(1)}, f32[128,2048]{1,0:T(8,128)}, u32[]{:S(2)}) %copy-start.5) | copy-done | bytes 1048600
  103.1 1.2 %copy-done.7 = f32[128,2048]{1,0:T(8,128)S(1)} copy-done((f32[128,2048]{1,0:T(8,128)S(1)}, f32[128,2048]{1,0:T(8,128)}, u32[]{:S(2)}) %copy-start.7) | copy-done | bytes 1048600
  104.3 0.9 copy-done.9
  105.2 0.9 copy-done.11
  106.1 0.9 copy-done.13
  107.0 2.3 %shard_map.114 = (bf16[1,128,2048]{2,1,0:T(8,128)(2,1)}, bf16[1,128,2048]{2,1,0:T(8,128)(2,1)}, bf16[1,128,2048]{2,1,0:T(8,128)(2,1)}) custom-call(bf16[1,128,2048]{2,1,0:T(8,128)(2,1)S(1)} %copy-done, bf16[1,128,2048]{2,1,0:T(8,128)(2,1)S(1)} %copy-done.1, bf16[1,128,2048]{2,1,0:T(8,128)(2,1)S(1)} %copy-done.2, f32[2,128,16]{2,1,0:T(8,128)S(1)} %copy-done.13, ...), custom_call_target="tpu_custom_call" | custom-call | tf_op jit(solution)/shard_map/pallas_call | solution.py:455
  109.3 4.9 %all-to-all-done = f32[256,1,16]{2,1,0:T(1,128)} async-done(((f32[256,1,16]{2,1,0:T(1,128)}), f32[256,1,16]{2,1,0:T(1,128)}, u32[]{:S(2)}, u32[]{:S(2)}) %all-to-all-start) | async-done | bytes 16416 | tf_op jit(solution)/shard_map/all_to_all | solution.py:453
  114.2 1.7 %reduce_sum.9 = f32[16]{0:T(128)} reduce(f32[256,1,16]{2,1,0:T(1,128)} %all-to-all-done, f32[]{:T(128)} %constant.0.clone.1), dimensions={0,1}, to_apply=%region_0.0 | reduce | flops 4080 | bytes 16452 | tf_op jit(solution)/shard_map/reduce_sum | solution.py:458
  (31 shorter events, 0.1 us)
Async XLA Ops:
  0.6 22.9 %copy-start.15 = (bf16[1,128,16]{1,2,0:T(8,128)(2,1)S(1)}, bf16[1,128,16]{1,2,0:T(8,128)(2,1)}, u32[]{:S(2)}) copy-start(bf16[1,128,16]{1,2,0:T(8,128)(2,1)} %param.11) | copy-start | bytes 12292
  0.6 22.9 %copy-start.16 = (f32[16]{0:T(128)S(1)}, f32[16]{0:T(128)}, u32[]{:S(2)}) copy-start(f32[16]{0:T(128)} %param.12) | copy-start | bytes 196
  0.7 22.9 %copy-start.17 = (s32[1,4]{1,0:T(1,128)S(1)}, s32[1,4]{1,0:T(1,128)}, u32[]{:S(2)}) copy-start(s32[1,4]{1,0:T(1,128)} %offsets_ref.3) | copy-start | bytes 52
  6.0 14.2 %collective-permute-start = (s16[528,128]{1,0:T(8,128)(2,1)S(1)}, s16[528,128]{1,0:T(8,128)(2,1)S(1)}, u32[]{:S(2)}, u32[]{:S(2)}) collective-permute-start(s16[528,128]{1,0:T(8,128)(2,1)S(1)} %get-tuple-element.40), channel_id=1, source_target_pairs={{0,1},{1,2},{2,3},{3,4},{4,5},{5,6},{6,7},{7,0},{8,9},{9,10},{10,1... | collective-permute-start | bytes 405512 | tf_op jit(solution)/shard_map/ppermute | solution.py:145
  8.5 14.1 %collective-permute-start.1 = (s16[528,128]{1,0:T(8,128)(2,1)S(1)}, s16[528,128]{1,0:T(8,128)(2,1)S(1)}, u32[]{:S(2)}, u32[]{:S(2)}) collective-permute-start(s16[528,128]{1,0:T(8,128)(2,1)S(1)} %get-tuple-element.41), channel_id=1, source_target_pairs={{0,2},{1,3},{2,4},{3,5},{4,6},{5,7},{6,0},{7,1},{8,10},{9,11},{10,... | collective-permute-start | bytes 405512 | tf_op jit(solution)/shard_map/ppermute | solution.py:145
  11.5 20.8 %collective-permute-start.2 = (s16[528,128]{1,0:T(8,128)(2,1)S(1)}, s16[528,128]{1,0:T(8,128)(2,1)S(1)}, u32[]{:S(2)}, u32[]{:S(2)}) collective-permute-start(s16[528,128]{1,0:T(8,128)(2,1)S(1)} %get-tuple-element.42), channel_id=1, source_target_pairs={{0,3},{1,4},{2,5},{3,6},{4,7},{5,0},{6,1},{7,2},{8,11},{9,12},{10,... | collective-permute-start | bytes 405512 | tf_op jit(solution)/shard_map/ppermute | solution.py:145
  15.3 17.6 %collective-permute-start.3 = (s16[528,128]{1,0:T(8,128)(2,1)S(1)}, s16[528,128]{1,0:T(8,128)(2,1)S(1)}, u32[]{:S(2)}, u32[]{:S(2)}) collective-permute-start(s16[528,128]{1,0:T(8,128)(2,1)S(1)} %get-tuple-element.43), channel_id=1, source_target_pairs={{0,4},{1,5},{2,6},{3,7},{4,0},{5,1},{6,2},{7,3},{8,12},{9,13},{10,... | collective-permute-start | bytes 405512 | tf_op jit(solution)/shard_map/ppermute | solution.py:145
  15.8 17.1 %collective-permute-start.4 = (s16[528,128]{1,0:T(8,128)(2,1)S(1)}, s16[528,128]{1,0:T(8,128)(2,1)S(1)}, u32[]{:S(2)}, u32[]{:S(2)}) collective-permute-start(s16[528,128]{1,0:T(8,128)(2,1)S(1)} %get-tuple-element.44), channel_id=1, source_target_pairs={{0,5},{1,6},{2,7},{3,0},{4,1},{5,2},{6,3},{7,4},{8,13},{9,14},{10,... | collective-permute-start | bytes 405512 | tf_op jit(solution)/shard_map/ppermute | solution.py:145
  20.2 20.5 %collective-permute-start.5 = (s16[528,128]{1,0:T(8,128)(2,1)S(1)}, s16[528,128]{1,0:T(8,128)(2,1)S(1)}, u32[]{:S(2)}, u32[]{:S(2)}) collective-permute-start(s16[528,128]{1,0:T(8,128)(2,1)S(1)} %get-tuple-element.45), channel_id=1, source_target_pairs={{0,6},{1,7},{2,0},{3,1},{4,2},{5,3},{6,4},{7,5},{8,14},{9,15},{10,... | collective-permute-start | bytes 405512 | tf_op jit(solution)/shard_map/ppermute | solution.py:145
  22.6 19.2 %collective-permute-start.6 = (s16[528,128]{1,0:T(8,128)(2,1)S(1)}, s16[528,128]{1,0:T(8,128)(2,1)S(1)}, u32[]{:S(2)}, u32[]{:S(2)}) collective-permute-start(s16[528,128]{1,0:T(8,128)(2,1)S(1)} %get-tuple-element.46), channel_id=1, source_target_pairs={{0,7},{1,0},{2,1},{3,2},{4,3},{5,4},{6,5},{7,6},{8,15},{9,8},{10,9... | collective-permute-start | bytes 405512 | tf_op jit(solution)/shard_map/ppermute | solution.py:145
  30.4 1.0 copy-start.4
  31.4 1.0 copy-start.6
  32.4 54.1 %copy-start.12 = (f32[2,128,16]{2,1,0:T(8,128)}, f32[2,128,16]{2,1,0:T(8,128)S(1)}, u32[]{:S(2)}) copy-start(f32[2,128,16]{2,1,0:T(8,128)S(1)} %get-tuple-element.35.cols_ref) | copy-start | bytes 49156
  41.8 44.6 %copy-start = (bf16[1,128,2048]{2,1,0:T(8,128)(2,1)S(1)}, bf16[1,128,2048]{2,1,0:T(8,128)(2,1)}, u32[]{:S(2)}) copy-start(bf16[1,128,2048]{2,1,0:T(8,128)(2,1)} %key_ref.7) | copy-start | bytes 1572868
  41.8 44.6 %copy-start.1 = (bf16[1,128,2048]{2,1,0:T(8,128)(2,1)S(1)}, bf16[1,128,2048]{2,1,0:T(8,128)(2,1)}, u32[]{:S(2)}) copy-start(bf16[1,128,2048]{2,1,0:T(8,128)(2,1)} %value_ref.7) | copy-start | bytes 1572868
  41.8 44.6 %copy-start.2 = (bf16[1,128,2048]{2,1,0:T(8,128)(2,1)S(1)}, bf16[1,128,2048]{2,1,0:T(8,128)(2,1)}, u32[]{:S(2)}) copy-start(bf16[1,128,2048]{2,1,0:T(8,128)(2,1)} %dout_ref.7) | copy-start | bytes 1572868
  41.8 44.6 %copy-start.3 = (bf16[1,128,2048]{2,1,0:T(8,128)(2,1)S(1)}, bf16[1,128,2048]{2,1,0:T(8,128)(2,1)}, u32[]{:S(2)}) copy-start(bf16[1,128,2048]{2,1,0:T(8,128)(2,1)} %query_ref.5) | copy-start | bytes 1572868
  42.3 6.0 %collective-permute-start.7 = (f32[264,128]{1,0:T(8,128)S(1)}, f32[264,128]{1,0:T(8,128)S(1)}, u32[]{:S(2)}, u32[]{:S(2)}) collective-permute-start(f32[264,128]{1,0:T(8,128)S(1)} %get-tuple-element.49), channel_id=1, source_target_pairs={{0,8},{8,16},{16,24},{24,0},{1,9},{9,17},{17,25},{25,1},{2,10},{10... | collective-permute-start | bytes 405512 | tf_op jit(solution)/shard_map/ppermute | solution.py:433
  43.9 8.5 %collective-permute-start.8 = (f32[264,128]{1,0:T(8,128)S(1)}, f32[264,128]{1,0:T(8,128)S(1)}, u32[]{:S(2)}, u32[]{:S(2)}) collective-permute-start(f32[264,128]{1,0:T(8,128)S(1)} %get-tuple-element.50), channel_id=1, source_target_pairs={{0,16},{8,24},{16,0},{24,8},{1,17},{9,25},{17,1},{25,9},{2,18},{10... | collective-permute-start | bytes 405512 | tf_op jit(solution)/shard_map/ppermute | solution.py:433
  46.5 5.9 %collective-permute-start.9 = (f32[264,128]{1,0:T(8,128)S(1)}, f32[264,128]{1,0:T(8,128)S(1)}, u32[]{:S(2)}, u32[]{:S(2)}) collective-permute-start(f32[264,128]{1,0:T(8,128)S(1)} %get-tuple-element.51), channel_id=1, source_target_pairs={{0,24},{8,0},{16,8},{24,16},{1,25},{9,1},{17,9},{25,17},{2,26},{10... | collective-permute-start | bytes 405512 | tf_op jit(solution)/shard_map/ppermute | solution.py:433
  53.6 9.8 %collective-permute-start.10 = (s16[528,128]{1,0:T(8,128)(2,1)S(1)}, s16[528,128]{1,0:T(8,128)(2,1)S(1)}, u32[]{:S(2)}, u32[]{:S(2)}) collective-permute-start(s16[528,128]{1,0:T(8,128)(2,1)S(1)} %get-tuple-element.53), channel_id=1, source_target_pairs={{0,1},{1,2},{2,3},{3,4},{4,5},{5,6},{6,7},{7,0},{8,9},{9,10},{10,1... | collective-permute-start | bytes 405512 | tf_op jit(solution)/shard_map/ppermute | solution.py:145
  56.9 10.5 %collective-permute-start.11 = (s16[528,128]{1,0:T(8,128)(2,1)S(1)}, s16[528,128]{1,0:T(8,128)(2,1)S(1)}, u32[]{:S(2)}, u32[]{:S(2)}) collective-permute-start(s16[528,128]{1,0:T(8,128)(2,1)S(1)} %get-tuple-element.54), channel_id=1, source_target_pairs={{0,2},{1,3},{2,4},{3,5},{4,6},{5,7},{6,0},{7,1},{8,10},{9,11},{10,... | collective-permute-start | bytes 405512 | tf_op jit(solution)/shard_map/ppermute | solution.py:145
  57.8 14.1 %collective-permute-start.12 = (s16[528,128]{1,0:T(8,128)(2,1)S(1)}, s16[528,128]{1,0:T(8,128)(2,1)S(1)}, u32[]{:S(2)}, u32[]{:S(2)}) collective-permute-start(s16[528,128]{1,0:T(8,128)(2,1)S(1)} %get-tuple-element.55), channel_id=1, source_target_pairs={{0,3},{1,4},{2,5},{3,6},{4,7},{5,0},{6,1},{7,2},{8,11},{9,12},{10,... | collective-permute-start | bytes 405512 | tf_op jit(solution)/shard_map/ppermute | solution.py:145
  57.9 17.7 %collective-permute-start.13 = (s16[528,128]{1,0:T(8,128)(2,1)S(1)}, s16[528,128]{1,0:T(8,128)(2,1)S(1)}, u32[]{:S(2)}, u32[]{:S(2)}) collective-permute-start(s16[528,128]{1,0:T(8,128)(2,1)S(1)} %get-tuple-element.56), channel_id=1, source_target_pairs={{0,4},{1,5},{2,6},{3,7},{4,0},{5,1},{6,2},{7,3},{8,12},{9,13},{10,... | collective-permute-start | bytes 405512 | tf_op jit(solution)/shard_map/ppermute | solution.py:145
  62.4 13.2 %collective-permute-start.14 = (s16[528,128]{1,0:T(8,128)(2,1)S(1)}, s16[528,128]{1,0:T(8,128)(2,1)S(1)}, u32[]{:S(2)}, u32[]{:S(2)}) collective-permute-start(s16[528,128]{1,0:T(8,128)(2,1)S(1)} %get-tuple-element.57), channel_id=1, source_target_pairs={{0,5},{1,6},{2,7},{3,0},{4,1},{5,2},{6,3},{7,4},{8,13},{9,14},{10,... | collective-permute-start | bytes 405512 | tf_op jit(solution)/shard_map/ppermute | solution.py:145
  63.4 21.2 %collective-permute-start.15 = (s16[528,128]{1,0:T(8,128)(2,1)S(1)}, s16[528,128]{1,0:T(8,128)(2,1)S(1)}, u32[]{:S(2)}, u32[]{:S(2)}) collective-permute-start(s16[528,128]{1,0:T(8,128)(2,1)S(1)} %get-tuple-element.58), channel_id=1, source_target_pairs={{0,6},{1,7},{2,0},{3,1},{4,2},{5,3},{6,4},{7,5},{8,14},{9,15},{10,... | collective-permute-start | bytes 405512 | tf_op jit(solution)/shard_map/ppermute | solution.py:145
  67.4 19.0 %collective-permute-start.16 = (s16[528,128]{1,0:T(8,128)(2,1)S(1)}, s16[528,128]{1,0:T(8,128)(2,1)S(1)}, u32[]{:S(2)}, u32[]{:S(2)}) collective-permute-start(s16[528,128]{1,0:T(8,128)(2,1)S(1)} %get-tuple-element.59), channel_id=1, source_target_pairs={{0,7},{1,0},{2,1},{3,2},{4,3},{5,4},{6,5},{7,6},{8,15},{9,8},{10,9... | collective-permute-start | bytes 405512 | tf_op jit(solution)/shard_map/ppermute | solution.py:145
  84.6 3.9 %copy-start.8 = (s16[528,128]{1,0:T(8,128)(2,1)}, s16[528,128]{1,0:T(8,128)(2,1)S(1)}, u32[]{:S(2)}) copy-start(s16[528,128]{1,0:T(8,128)(2,1)S(1)} %collective-permute-done.15.refs_6_) | copy-start | bytes 405508
  86.5 2.0 %copy-start.10 = (s16[528,128]{1,0:T(8,128)(2,1)}, s16[528,128]{1,0:T(8,128)(2,1)S(1)}, u32[]{:S(2)}) copy-start(s16[528,128]{1,0:T(8,128)(2,1)S(1)} %collective-permute-done.16.refs_7_) | copy-start | bytes 405508
  88.4 0.6 copy-start.14
  89.1 25.1 %all-to-all-start = ((f32[256,1,16]{2,1,0:T(1,128)}), f32[256,1,16]{2,1,0:T(1,128)}, u32[]{:S(2)}, u32[]{:S(2)}) async-start(f32[256,1,16]{2,1,0:T(1,128)} %copy-done.14), calls=%async_computation | async-start | bytes 262144 | tf_op jit(solution)/shard_map/all_to_all | solution.py:453
  101.9 1.2 %copy-start.5 = (f32[128,2048]{1,0:T(8,128)S(1)}, f32[128,2048]{1,0:T(8,128)}, u32[]{:S(2)}) copy-start(f32[128,2048]{1,0:T(8,128)} %copy-done.4) | copy-start | bytes 3145732
  103.1 1.2 %copy-start.7 = (f32[128,2048]{1,0:T(8,128)S(1)}, f32[128,2048]{1,0:T(8,128)}, u32[]{:S(2)}) copy-start(f32[128,2048]{1,0:T(8,128)} %copy-done.6) | copy-start | bytes 3145732
  104.3 0.9 copy-start.9
  105.2 0.9 copy-start.11
  106.1 0.9 copy-start.13

commit v8 on v5

--- a/solution.py
+++ b/solution.py
@@ -12,6 +12,7 @@
 ALL = ("dp", "seg", "grp")
 TAIL = 16
 LANES = 128
+EXTRA = HEAD_DIM // 8
 F32 = jnp.float32
 BF16 = jnp.bfloat16
 I16 = jnp.int16
@@ -63,6 +64,14 @@
     return pl.ds(ref.shape[-2] - TAIL, TAIL)
 
 
+def extra(m):
+    return pl.ds(2 * HEAD_DIM + m * EXTRA, EXTRA)
+
+
+def extra_in(m):
+    return pl.ds(4 * HEAD_DIM + m * EXTRA, EXTRA)
+
+
 def iota(shape, dim):
     return lax.broadcasted_iota(jnp.int32, shape, dim)
 
@@ -83,6 +92,24 @@
 
 def decode(steps, power):
     return wide(steps) * jnp.exp2(power / 8.0 - 15.0)
+
+
+def encode18(x):
+    top = jnp.maximum(jnp.max(jnp.abs(x), axis=0, keepdims=True), 1e-30)
+    power = jnp.ceil(jnp.log2(top) * 8.0)
+    steps = jnp.clip(jnp.floor(x * jnp.exp2(17.0 - power / 8.0) + 0.5), -131071.0, 131071.0)
+    high = jnp.floor(steps * 0.25)
+    low = steps - 4.0 * high
+    return high, sum(low[k * EXTRA : (k + 1) * EXTRA] * 4.0**k for k in range(8)) - 32768.0, power
+
+
+def decode18(high, packed, power):
+    packed = wide(packed) + 32768.0
+    digits = [jnp.floor(packed * 0.25**k) for k in range(8)]
+    low = jnp.concatenate(
+        [d - 4.0 * above for d, above in zip(digits, digits[1:] + [jnp.zeros_like(packed)])], axis=0
+    )
+    return (wide(high) * 4.0 + low) * jnp.exp2(power / 8.0 - 17.0)
 
 
 def encode2(x):
@@ -190,8 +217,9 @@
         slot, m = divmod(h, 2)
         for at, left, right, weight in ((m, 1, 2, tail[:, one]), (2 + m, 0, 3, entry[:, one] * SCALE)):
             own = tn2(held[left, :, cols], held[right, :, cols].astype(F32) * weight)
-            steps, powers[at] = encode(own)
-            pay[slot, matrix(at), :] = whole16(steps)
+            high, low, powers[at] = encode18(own)
+            pay[slot, matrix(at), :] = whole16(high)
+            pay[slot, extra_in(at), :] = whole16(low)
         if m == 1:
             pay[slot, tail_of(pay), :] = rows16(
                 *(powers[i] for i in range(4)),
@@ -207,40 +235,52 @@
     return [log_whole(t[4 + 2 * m : 5 + 2 * m], t[5 + 2 * m : 6 + 2 * m]) for t in tails]
 
 
-def totals_kernel(pay_ref, _, *send_refs):
+def totals_kernel(pay_ref, _, own_ref, *send_refs):
     count = pay_ref.shape[0]
     tails = [wide(pay_ref[c, tail_of(pay_ref), :]) for c in range(count)]
     mine, segments = lax.axis_index("seg"), lax.axis_size("seg")
-    at = iota((8, LANES), 0)
-    logs = jnp.zeros((8, LANES), F32)
+    powers, logs = [], []
     for m in range(2):
         log = chunk_logs(tails, m)
-        logs = jnp.where(at == m, sum(log), logs)
+        logs.extend(log_parts(jnp.maximum(sum(log), -128.0)))
         ends = []
         for where, order in ((m, range(count)), (2 + m, range(count - 1, -1, -1))):
             carry = jnp.zeros((HEAD_DIM, HEAD_DIM), F32)
             for c in order:
-                carry = jnp.exp(log[c]) * carry + decode(
-                    pay_ref[c, matrix(where), :], tails[c][where : where + 1]
+                own = decode18(
+                    pay_ref[c, matrix(where), :], pay_ref[c, extra_in(where), :], tails[c][where : where + 1]
                 )
-            ends.append(carry)
+                own_ref[c, matrix(where), :] = own
+                carry = jnp.exp(log[c]) * carry + own
+            ends.append(encode18(carry))
+        powers.append([end[2] for end in ends])
         for distance, send_ref in enumerate(send_refs, 1):
-            send_ref[matrix(m), :] = jnp.where(mine + distance < segments, *ends)
-    for send_ref in send_refs:
-        send_ref[pl.ds(2 * HEAD_DIM, 8), :] = logs
-
-
-def scan_kernel(pay_ref, *refs):
+            later = mine + distance < segments
+            send_ref[matrix(m), :] = whole16(jnp.where(later, ends[0][0], ends[1][0]))
+            send_ref[extra(m), :] = whole16(jnp.where(later, ends[0][1], ends[1][1]))
+    for distance, send_ref in enumerate(send_refs, 1):
+        later = mine + distance < segments
+        send_ref[tail_of(send_ref), :] = rows16(*(jnp.where(later, *pair) for pair in powers), *logs)
+
+
+def scan_kernel(pay_ref, own_ref, *refs):
     *got_refs, out_ref, held = refs
     count = pay_ref.shape[0]
     mine = lax.axis_index("seg")
     tails = [wide(pay_ref[c, tail_of(pay_ref), :]) for c in range(count)]
+    got_tails = [wide(ref[tail_of(ref), :]) for ref in got_refs]
     at = iota((2 * count, LANES), 0)
     flows = jnp.zeros((2 * count, LANES), F32)
     powers = [[None] * 4 for _ in range(count)]
     for m in range(2):
         log = chunk_logs(tails, m)
-        sent = [(jnp.exp(ref[pl.ds(2 * HEAD_DIM + m, 1), :]), ref[matrix(m), :]) for ref in got_refs]
+        sent = [
+            (
+                jnp.exp(log_whole(t[2 + 2 * m : 3 + 2 * m], t[3 + 2 * m : 4 + 2 * m])),
+                decode18(ref[matrix(m), :], ref[extra(m), :], t[m : m + 1]),
+            )
+            for ref, t in zip(got_refs, got_tails)
+        ]
         state = jnp.zeros((HEAD_DIM, HEAD_DIM), F32)
         for d in range(len(sent), 0, -1):
             state = jnp.where(mine >= d, sent[d - 1][0] * state + sent[d - 1][1], state)
@@ -258,7 +298,7 @@
                     flow = passing * jnp.sum(held[c] * carry, axis=0, keepdims=True)
                     flows = jnp.where(at == 2 * c + m, flow, flows)
                 if i < count - 1:
-                    carry = passing * carry + decode(pay_ref[c, matrix(where), :], tails[c][where : where + 1])
+                    carry = passing * carry + own_ref[c, matrix(where), :]
     parts = encode2(jnp.sum(flows, axis=1, keepdims=True))
     for c in range(count):
         out_ref[c, tail_of(out_ref), :] = rows16(
@@ -378,9 +418,10 @@
     big = pin((query, key, value, dout))
     scratch = [pltpu.VMEM((4, length, width), BF16), pltpu.SemaphoreType.DMA((4, 8))]
     packed = jax.ShapeDtypeStruct((count, 4 * HEAD_DIM + TAIL, LANES), I16)
+    packed_in = jax.ShapeDtypeStruct((count, 4 * (HEAD_DIM + EXTRA) + TAIL, LANES), I16)
     pay = call(
         states_kernel,
-        packed,
+        packed_in,
         [HBM] * 7,
         scratch_shapes=scratch
         + [
@@ -388,7 +429,7 @@
             pltpu.VMEM((1, heads), F32),
             pltpu.SMEM(offsets.shape, jnp.int32),
             pltpu.SemaphoreType.DMA((3,)),
-            pltpu.VMEM(packed.shape, I16),
+            pltpu.VMEM(packed_in.shape, I16),
             pltpu.SemaphoreType.DMA((count,)),
         ],
         out_specs=HBM,
@@ -402,18 +443,23 @@
         [HBM] * 4 + [VMEM] * 2 + [SMEM],
         scratch_shapes=scratch,
     )(*big, *small)
-    total = jax.ShapeDtypeStruct((2 * HEAD_DIM + 8, LANES), F32)
-    sends = call(totals_kernel, (total,) * (segments - 1), [VMEM, pl.BlockSpec(memory_space=pl.ANY)])(pay, rows)
-    got = [
-        lax.ppermute(send, "seg", [(i, (i + d) % segments) for i in range(segments)])
-        for d, send in enumerate(sends, 1)
-    ]
+    total = jax.ShapeDtypeStruct((2 * HEAD_DIM + 2 * EXTRA + TAIL, LANES), I16)
+    own, *sends = call(
+        totals_kernel,
+        (jax.ShapeDtypeStruct((count, 4 * HEAD_DIM, LANES), F32),) + (total,) * (segments - 1),
+        [VMEM, pl.BlockSpec(memory_space=pl.ANY)],
+    )(pay, rows)
+    got = {
+        d: lax.ppermute(sends[d - 1], "seg", [(i, (i + d) % segments) for i in range(segments)])
+        for d in sorted(range(1, segments), key=lambda d: -min(d, segments - d))
+    }
+    got = [got[d] for d in range(1, segments)]
     carried = call(
         scan_kernel,
         packed,
-        [VMEM] * segments,
+        [VMEM] * (segments + 1),
         scratch_shapes=[pltpu.VMEM((count, HEAD_DIM, LANES), F32)],
-    )(pay, *got)
+    )(pay, own, *got)
     carried = lax.all_to_all(carried, "grp", split_axis=0, concat_axis=0, tiled=True)
     dgate, dbias = call(
         gates_kernel,

time: 113 us -> 115 us (1.018)
  starting transfers between devices: 23.9 us -> 25.2 us
  blocking collectives: 29.9 us -> 28.6 us
    all_to_all x1, waiting for transfers between devices: 20.1 us -> 22.9 us  [shards(): pay = lax.all_to_all(pay, 'grp', split_axis=0, concat_axis=0, tiled=True)]
    ppermute x3, waiting for transfers between devices: 5.02 us -> 2.47 us  [shards(): lax.ppermute(sends[d - 1], 'seg', [(i, (i + d) % segments) for i in range...]
    all_to_all x1, blocking collectives: 29.9 us -> 28.6 us  [shards(): lax.all_to_all(carried, 'grp', split_axis=0, concat_axis=0, tiled=True)]
    all_to_all x1, starting transfers between devices: 9.67 us -> 11 us  [shards(): lax.all_to_all(dbias, ALL, split_axis=0, concat_axis=0, tiled=True)]
where the time goes in v8:
time: 115 us; the launch traced here: 114 us
  waiting for transfers between devices  32.6 us (28%)
  blocking collectives  28.6 us (25%)
  starting transfers between devices  25.2 us (22%)
  Pallas kernels  19.7 us (17%)
  local copies, waits for them, and re-layouts  6.62 us (6%)
    all_to_all x1, blocking collectives, shards(): lax.all_to_all(carried, 'grp', split_axis=0, concat_axis=0, tiled=True)  28.6 us
    all_to_all x1, waiting for transfers between devices, shards(): pay = lax.all_to_all(pay, 'grp', split_axis=0, concat_axis=0, tiled=True)  22.9 us
    all_to_all x1, starting transfers between devices, shards(): lax.all_to_all(dbias, ALL, split_axis=0, concat_axis=0, tiled=True)  11 us
    all_to_all x1, starting transfers between devices, shards(): pay = lax.all_to_all(pay, 'grp', split_axis=0, concat_axis=0, tiled=True)  9.16 us
    all_to_all x1, waiting for transfers between devices, shards(): lax.all_to_all(dbias, ALL, split_axis=0, concat_axis=0, tiled=True)  7.16 us
    pallas_call x1, Pallas kernels, shards(): call(local_kernel, (near_like,) * 3 + (jax.ShapeDtypeStruct((2, heads, le...  6.86 us
    unnamed x26, local copies, waits for them, and re-layouts  6.62 us
    pallas_call x1, Pallas kernels, shards(): call(states_kernel, packed_in, [HBM] * 7, scratch_shapes=scratch + [pltpu...  6.54 us
  transfers between devices with their start and end apart: 5, of which 4 were waited for; matrix products, arithmetic and copies ran while one was open for 0% of the time, Pallas kernels for 8%

profile of v8, /device:TPU:1, one launch (start us, length us, event | category | flops | bytes accessed | tf_op | source)
XLA Modules:
  0.0 114.2 jit_solution(5624554753559651096)
XLA Ops:
  0.6 6.5 %shard_map.111 = s16[8,592,128]{2,1,0:T(8,128)(2,1)} custom-call(bf16[1,128,2048]{2,1,0:T(8,128)(2,1)} %query_ref.5, bf16[1,128,2048]{2,1,0:T(8,128)(2,1)} %key_ref.7, bf16[1,128,2048]{2,1,0:T(8,128)(2,1)} %value_ref.7, bf16[1,128,2048]{2,1,0:T(8,128)(2,1)} %dout_ref.7, bf16[1,16,128]{2,1,0:T(8,128)(2,1)} %bitcast.3, f32[1,16]{1,0:T(1,128)} %bitcast.5, ...), custom_call_target="tpu_custom_call" | custom-call | tf_op jit(solution)/shard_map/pallas_call | solution.py:422
  7.2 0.0 copy-start.10
  7.2 0.0 copy-start.11
  7.2 0.0 copy-start.12
  7.2 9.2 %all-to-all-start = ((s16[8,592,128]{2,1,0:T(8,128)(2,1)}), s16[8,592,128]{2,1,0:T(8,128)(2,1)S(1)}, u32[]{:S(2)}, u32[]{:S(2)}) async-start(s16[8,592,128]{2,1,0:T(8,128)(2,1)} %shard_map.111), calls=%async_computation | async-start | bytes 2424832 | tf_op jit(solution)/shard_map/all_to_all | solution.py:437
  16.4 0.0 copy-done.10
  16.4 0.0 copy-done.11
  16.4 0.0 copy-done.12
  16.4 6.9 %shard_map.110 = (f32[128,2048]{1,0:T(8,128)S(1)}, f32[128,2048]{1,0:T(8,128)S(1)}, f32[128,2048]{1,0:T(8,128)S(1)}, f32[2,16,128]{2,1,0:T(8,128)S(1)}, f32[2,128,16]{2,1,0:T(8,128)S(1)}) custom-call(bf16[1,128,2048]{2,1,0:T(8,128)(2,1)} %query_ref.5, bf16[1,128,2048]{2,1,0:T(8,128)(2,1)} %key_ref.7, bf16[1,128,2048]{2,1,0:T(8,128)(2,1)} %value_ref.7, ...), custom_call_target="tpu_custom_call" | custom-call | tf_op jit(solution)/shard_map/pallas_call | solution.py:439
  23.3 0.0 copy-start.4
  23.3 1.0 copy-done.4
  24.2 0.0 copy-start.6
  24.2 1.0 copy-done.6
  25.2 0.0 copy-start.8
  25.2 1.0 copy-done.8
  26.2 22.9 %all-to-all-done.pay_ref = s16[8,592,128]{2,1,0:T(8,128)(2,1)S(1)} async-done(((s16[8,592,128]{2,1,0:T(8,128)(2,1)}), s16[8,592,128]{2,1,0:T(8,128)(2,1)S(1)}, u32[]{:S(2)}, u32[]{:S(2)}) %all-to-all-start) | async-done | bytes 1212448 | tf_op jit(solution)/shard_map/all_to_all | solution.py:437
  49.1 1.0 shard_map.112
  50.1 1.4 %collective-permute-start = (s16[304,128]{1,0:T(8,128)(2,1)S(1)}, s16[304,128]{1,0:T(8,128)(2,1)S(1)}, u32[]{:S(2)}, u32[]{:S(2)}) collective-permute-start(s16[304,128]{1,0:T(8,128)(2,1)S(1)} %get-tuple-element.22), channel_id=1, source_target_pairs={{0,8},{8,16},{16,24},{24,0},{1,9},{9,17},{17,25},{25,1},{2,10},{10... | collective-permute-start | bytes 233480 | tf_op jit(solution)/shard_map/ppermute | solution.py:453
  51.5 2.6 %collective-permute-start.1 = (s16[304,128]{1,0:T(8,128)(2,1)S(1)}, s16[304,128]{1,0:T(8,128)(2,1)S(1)}, u32[]{:S(2)}, u32[]{:S(2)}) collective-permute-start(s16[304,128]{1,0:T(8,128)(2,1)S(1)} %get-tuple-element.23), channel_id=1, source_target_pairs={{0,16},{8,24},{16,0},{24,8},{1,17},{9,25},{17,1},{25,9},{2,18},{10... | collective-permute-start | bytes 233480 | tf_op jit(solution)/shard_map/ppermute | solution.py:453
  54.1 1.1 collective-permute-start.2
  55.2 0.0 collective-permute-done.refs_0_
  55.2 2.3 %collective-permute-done.1.refs_1_ = s16[304,128]{1,0:T(8,128)(2,1)S(1)} collective-permute-done((s16[304,128]{1,0:T(8,128)(2,1)S(1)}, s16[304,128]{1,0:T(8,128)(2,1)S(1)}, u32[]{:S(2)}, u32[]{:S(2)}) %collective-permute-start.1) | collective-permute-done | bytes 77856 | tf_op jit(solution)/shard_map/ppermute | solution.py:453
  57.4 0.2 collective-permute-done.2.refs_2_
  57.7 1.1 shard_map.113
  58.7 0.0 copy-start
  58.7 0.0 copy-start.1
  58.8 0.0 copy-start.2
  58.8 0.0 copy-start.3
  58.8 28.6 %all_to_all.15.state_ref = s16[8,528,128]{2,1,0:T(8,128)(2,1)S(1)} all-to-all(s16[8,528,128]{2,1,0:T(8,128)(2,1)S(1)} %shard_map.113), channel_id=1, replica_groups=mesh['dp'=8,'seg'=4,'grp'=8] {'grp'}, dimensions={0} | all-to-all | bytes 2162688 | tf_op jit(solution)/shard_map/all_to_all | solution.py:463
  87.4 0.0 copy-done
  87.4 0.0 copy-done.1
  87.4 0.0 copy-done.2
  87.4 0.0 copy-done.3
  87.4 2.1 %shard_map.115 = (bf16[1,16,128]{2,1,0:T(8,128)(2,1)}, f32[256,1,16]{2,1,0:T(1,128)}) custom-call(bf16[1,128,2048]{2,1,0:T(8,128)(2,1)S(1)} %copy-done.3, bf16[1,128,2048]{2,1,0:T(8,128)(2,1)S(1)} %copy-done, bf16[1,128,2048]{2,1,0:T(8,128)(2,1)S(1)} %copy-done.1, bf16[1,128,2048]{2,1,0:T(8,128)(2,1)S(1)} %copy-done.2, ...), custom_call_target="tpu_custom_call" | custom-call | tf_op jit(solution)/shard_map/pallas_call | solution.py:464
  89.5 11.0 %all-to-all-start.2 = ((f32[256,1,16]{2,1,0:T(1,128)}), f32[256,1,16]{2,1,0:T(1,128)S(1)}, u32[]{:S(2)}, u32[]{:S(2)}) async-start(f32[256,1,16]{2,1,0:T(1,128)} %get-tuple-element.32), calls=%async_computation.2 | async-start | bytes 262144 | tf_op jit(solution)/shard_map/all_to_all | solution.py:472
  100.4 0.0 copy-start.5
  100.4 1.2 %copy-done.5 = f32[128,2048]{1,0:T(8,128)S(1)} copy-done((f32[128,2048]{1,0:T(8,128)S(1)}, f32[128,2048]{1,0:T(8,128)}, u32[]{:S(2)}) %copy-start.5) | copy-done | bytes 1048600
  101.6 0.0 copy-start.7
  101.7 1.2 %copy-done.7 = f32[128,2048]{1,0:T(8,128)S(1)} copy-done((f32[128,2048]{1,0:T(8,128)S(1)}, f32[128,2048]{1,0:T(8,128)}, u32[]{:S(2)}) %copy-start.7) | copy-done | bytes 1048600
  102.9 0.0 copy-start.9
  102.9 1.2 %copy-done.9 = f32[128,2048]{1,0:T(8,128)S(1)} copy-done((f32[128,2048]{1,0:T(8,128)S(1)}, f32[128,2048]{1,0:T(8,128)}, u32[]{:S(2)}) %copy-start.9) | copy-done | bytes 1048600
  104.1 2.2 %shard_map.114 = (bf16[1,128,2048]{2,1,0:T(8,128)(2,1)}, bf16[1,128,2048]{2,1,0:T(8,128)(2,1)}, bf16[1,128,2048]{2,1,0:T(8,128)(2,1)}) custom-call(bf16[1,128,2048]{2,1,0:T(8,128)(2,1)S(1)} %copy-done, bf16[1,128,2048]{2,1,0:T(8,128)(2,1)S(1)} %copy-done.1, bf16[1,128,2048]{2,1,0:T(8,128)(2,1)S(1)} %copy-done.2, ...), custom_call_target="tpu_custom_call" | custom-call | tf_op jit(solution)/shard_map/pallas_call | solution.py:474
  106.3 7.2 %all-to-all-done.2 = f32[256,1,16]{2,1,0:T(1,128)S(1)} async-done(((f32[256,1,16]{2,1,0:T(1,128)}), f32[256,1,16]{2,1,0:T(1,128)S(1)}, u32[]{:S(2)}, u32[]{:S(2)}) %all-to-all-start.2) | async-done | bytes 16416 | tf_op jit(solution)/shard_map/all_to_all | solution.py:472
  113.4 0.8 reduce_sum.9
Async XLA Ops:
  7.2 9.2 %copy-start.10 = (bf16[1,128,16]{1,2,0:T(8,128)(2,1)S(1)}, bf16[1,128,16]{1,2,0:T(8,128)(2,1)}, u32[]{:S(2)}) copy-start(bf16[1,128,16]{1,2,0:T(8,128)(2,1)} %param.11) | copy-start | bytes 12292
  7.2 9.2 %copy-start.11 = (f32[16]{0:T(128)S(1)}, f32[16]{0:T(128)}, u32[]{:S(2)}) copy-start(f32[16]{0:T(128)} %param.12) | copy-start | bytes 196
  7.2 9.2 %copy-start.12 = (s32[1,4]{1,0:T(1,128)S(1)}, s32[1,4]{1,0:T(1,128)}, u32[]{:S(2)}) copy-start(s32[1,4]{1,0:T(1,128)} %offsets_ref.3) | copy-start | bytes 52
  7.2 41.9 %all-to-all-start = ((s16[8,592,128]{2,1,0:T(8,128)(2,1)}), s16[8,592,128]{2,1,0:T(8,128)(2,1)S(1)}, u32[]{:S(2)}, u32[]{:S(2)}) async-start(s16[8,592,128]{2,1,0:T(8,128)(2,1)} %shard_map.111), calls=%async_computation | async-start | bytes 2424832 | tf_op jit(solution)/shard_map/all_to_all | solution.py:437
  23.3 1.0 copy-start.4
  24.2 1.0 copy-start.6
  25.2 1.0 copy-start.8
  50.1 5.1 %collective-permute-start = (s16[304,128]{1,0:T(8,128)(2,1)S(1)}, s16[304,128]{1,0:T(8,128)(2,1)S(1)}, u32[]{:S(2)}, u32[]{:S(2)}) collective-permute-start(s16[304,128]{1,0:T(8,128)(2,1)S(1)} %get-tuple-element.22), channel_id=1, source_target_pairs={{0,8},{8,16},{16,24},{24,0},{1,9},{9,17},{17,25},{25,1},{2,10},{10... | collective-permute-start | bytes 233480 | tf_op jit(solution)/shard_map/ppermute | solution.py:453
  51.5 6.0 %collective-permute-start.1 = (s16[304,128]{1,0:T(8,128)(2,1)S(1)}, s16[304,128]{1,0:T(8,128)(2,1)S(1)}, u32[]{:S(2)}, u32[]{:S(2)}) collective-permute-start(s16[304,128]{1,0:T(8,128)(2,1)S(1)} %get-tuple-element.23), channel_id=1, source_target_pairs={{0,16},{8,24},{16,0},{24,8},{1,17},{9,25},{17,1},{25,9},{2,18},{10... | collective-permute-start | bytes 233480 | tf_op jit(solution)/shard_map/ppermute | solution.py:453
  54.1 3.5 %collective-permute-start.2 = (s16[304,128]{1,0:T(8,128)(2,1)S(1)}, s16[304,128]{1,0:T(8,128)(2,1)S(1)}, u32[]{:S(2)}, u32[]{:S(2)}) collective-permute-start(s16[304,128]{1,0:T(8,128)(2,1)S(1)} %get-tuple-element.24), channel_id=1, source_target_pairs={{0,24},{8,0},{16,8},{24,16},{1,25},{9,1},{17,9},{25,17},{2,26},{10... | collective-permute-start | bytes 233480 | tf_op jit(solution)/shard_map/ppermute | solution.py:453
  58.7 28.6 %copy-start = (bf16[1,128,2048]{2,1,0:T(8,128)(2,1)S(1)}, bf16[1,128,2048]{2,1,0:T(8,128)(2,1)}, u32[]{:S(2)}) copy-start(bf16[1,128,2048]{2,1,0:T(8,128)(2,1)} %key_ref.7) | copy-start | bytes 1572868
  58.7 28.6 %copy-start.1 = (bf16[1,128,2048]{2,1,0:T(8,128)(2,1)S(1)}, bf16[1,128,2048]{2,1,0:T(8,128)(2,1)}, u32[]{:S(2)}) copy-start(bf16[1,128,2048]{2,1,0:T(8,128)(2,1)} %value_ref.7) | copy-start | bytes 1572868
  58.8 28.6 %copy-start.2 = (bf16[1,128,2048]{2,1,0:T(8,128)(2,1)S(1)}, bf16[1,128,2048]{2,1,0:T(8,128)(2,1)}, u32[]{:S(2)}) copy-start(bf16[1,128,2048]{2,1,0:T(8,128)(2,1)} %dout_ref.7) | copy-start | bytes 1572868
  58.8 28.6 %copy-start.3 = (bf16[1,128,2048]{2,1,0:T(8,128)(2,1)S(1)}, bf16[1,128,2048]{2,1,0:T(8,128)(2,1)}, u32[]{:S(2)}) copy-start(bf16[1,128,2048]{2,1,0:T(8,128)(2,1)} %query_ref.5) | copy-start | bytes 1572868
  89.5 24.0 %all-to-all-start.2 = ((f32[256,1,16]{2,1,0:T(1,128)}), f32[256,1,16]{2,1,0:T(1,128)S(1)}, u32[]{:S(2)}, u32[]{:S(2)}) async-start(f32[256,1,16]{2,1,0:T(1,128)} %get-tuple-element.32), calls=%async_computation.2 | async-start | bytes 262144 | tf_op jit(solution)/shard_map/all_to_all | solution.py:472
  100.4 1.2 %copy-start.5 = (f32[128,2048]{1,0:T(8,128)S(1)}, f32[128,2048]{1,0:T(8,128)}, u32[]{:S(2)}) copy-start(f32[128,2048]{1,0:T(8,128)} %copy-done.4) | copy-start | bytes 3145732
  101.6 1.2 %copy-start.7 = (f32[128,2048]{1,0:T(8,128)S(1)}, f32[128,2048]{1,0:T(8,128)}, u32[]{:S(2)}) copy-start(f32[128,2048]{1,0:T(8,128)} %copy-done.6) | copy-start | bytes 3145732
  102.9 1.2 %copy-start.9 = (f32[128,2048]{1,0:T(8,128)S(1)}, f32[128,2048]{1,0:T(8,128)}, u32[]{:S(2)}) copy-start(f32[128,2048]{1,0:T(8,128)} %copy-done.8) | copy-start | bytes 3145732

commit v9 on v8

--- a/solution.py
+++ b/solution.py
@@ -46,6 +46,12 @@
     return hi, (x - hi.astype(F32)).astype(BF16)
 
 
+def split3(x, axis):
+    hi, rest = x.astype(BF16), x - x.astype(BF16).astype(F32)
+    mid = rest.astype(BF16)
+    return jnp.concatenate([hi, mid, (rest - mid.astype(F32)).astype(BF16)], axis=axis)
+
+
 def tn2(a, b):
     both = tn(a, jnp.concatenate(split2(b), axis=1))
     return both[:, : b.shape[1]] + both[:, b.shape[1] :]
@@ -158,7 +164,8 @@
     logits = gates.astype(F32) + jnp.sum(jnp.where(same, bias, 0.0), axis=1, keepdims=True)
     step = -(jnp.maximum(logits, 0.0) + jnp.log1p(jnp.exp(-jnp.abs(logits))))
     causal = iota((length, length), 0) >= iota((length, length), 1)
-    cumulative = nt(causal.astype(F32), step, HIGHEST)
+    terms = nt(causal.astype(BF16), split3(step, 0))
+    cumulative = terms[:, :heads] + (terms[:, heads : 2 * heads] + terms[:, 2 * heads :])
     doc = doc_of(first + iota((length, 1), 0), offsets_ref)
     doc_last = doc_of(first + length - 1, offsets_ref)
     before = jnp.where(first > 0, doc_of(first - 1, offsets_ref), -1)
@@ -372,12 +379,11 @@
         starts = jnp.where(lane == h, at_start, starts)
         flows = jnp.where(sublane == h, flow, flows)
     behind = iota((length, length), 0) - iota((length, length), 1)
-    dstep = (
-        rows_ref[0]
-        + tn(ends * cols_ref[0], (behind >= 0).astype(F32), HIGHEST)
-        + tn(starts * cols_ref[1], (behind < 0).astype(F32), HIGHEST)
-        + flows
-    )
+    masks = jnp.concatenate([(behind >= 0).astype(BF16), (behind < 0).astype(BF16)], axis=0)
+    sums = jnp.concatenate([ends * cols_ref[0], starts * cols_ref[1]], axis=0)
+    terms = tn(split3(sums, 1), masks)
+    terms = terms[:heads] + (terms[heads : 2 * heads] + terms[2 * heads :])
+    dstep = rows_ref[0] + terms + flows
     dlogit = dstep * rows_ref[1]
     dgate_ref[0] = dlogit.astype(BF16)
     same = iota((heads, heads), 0) == iota((heads, heads), 1)

time: 115 us -> 115 us (level)
  no operation moved by 1% of the time
where the time goes in v9:
time: 115 us; the launch traced here: 114 us
  waiting for transfers between devices  32.7 us (28%)
  blocking collectives  28.6 us (25%)
  starting transfers between devices  25.2 us (22%)
  Pallas kernels  19.5 us (17%)
  local copies, waits for them, and re-layouts  6.62 us (6%)
    all_to_all x1, blocking collectives, shards(): lax.all_to_all(carried, 'grp', split_axis=0, concat_axis=0, tiled=True)  28.6 us
    all_to_all x1, waiting for transfers between devices, shards(): pay = lax.all_to_all(pay, 'grp', split_axis=0, concat_axis=0, tiled=True)  23.1 us
    all_to_all x1, starting transfers between devices, shards(): lax.all_to_all(dbias, ALL, split_axis=0, concat_axis=0, tiled=True)  11 us
    all_to_all x1, starting transfers between devices, shards(): pay = lax.all_to_all(pay, 'grp', split_axis=0, concat_axis=0, tiled=True)  9.16 us
    all_to_all x1, waiting for transfers between devices, shards(): lax.all_to_all(dbias, ALL, split_axis=0, concat_axis=0, tiled=True)  7.16 us
    pallas_call x1, Pallas kernels, shards(): call(local_kernel, (near_like,) * 3 + (jax.ShapeDtypeStruct((2, heads, le...  6.71 us
    pallas_call x1, Pallas kernels, shards(): call(states_kernel, packed_in, [HBM] * 7, scratch_shapes=scratch + [pltpu...  6.62 us
    unnamed x26, local copies, waits for them, and re-layouts  6.62 us
  transfers between devices with their start and end apart: 5, of which 4 were waited for; matrix products, arithmetic and copies ran while one was open for 0% of the time, Pallas kernels for 8%

profile of v9, /device:TPU:1, one launch (start us, length us, event | category | flops | bytes accessed | tf_op | source)
XLA Modules:
  0.0 114.2 jit_solution(17116549113372668319)
XLA Ops:
  0.6 6.6 %shard_map.111 = s16[8,592,128]{2,1,0:T(8,128)(2,1)} custom-call(bf16[1,128,2048]{2,1,0:T(8,128)(2,1)} %query_ref.5, bf16[1,128,2048]{2,1,0:T(8,128)(2,1)} %key_ref.7, bf16[1,128,2048]{2,1,0:T(8,128)(2,1)} %value_ref.7, bf16[1,128,2048]{2,1,0:T(8,128)(2,1)} %dout_ref.7, bf16[1,16,128]{2,1,0:T(8,128)(2,1)} %bitcast.3, f32[1,16]{1,0:T(1,128)} %bitcast.5, ...), custom_call_target="tpu_custom_call" | custom-call | tf_op jit(solution)/shard_map/pallas_call | solution.py:428
  7.3 0.0 copy-start.10
  7.3 0.0 copy-start.11
  7.3 0.0 copy-start.12
  7.3 9.2 %all-to-all-start = ((s16[8,592,128]{2,1,0:T(8,128)(2,1)}), s16[8,592,128]{2,1,0:T(8,128)(2,1)S(1)}, u32[]{:S(2)}, u32[]{:S(2)}) async-start(s16[8,592,128]{2,1,0:T(8,128)(2,1)} %shard_map.111), calls=%async_computation | async-start | bytes 2424832 | tf_op jit(solution)/shard_map/all_to_all | solution.py:443
  16.5 0.0 copy-done.10
  16.5 0.0 copy-done.11
  16.5 0.0 copy-done.12
  16.5 6.7 %shard_map.110 = (f32[128,2048]{1,0:T(8,128)S(1)}, f32[128,2048]{1,0:T(8,128)S(1)}, f32[128,2048]{1,0:T(8,128)S(1)}, f32[2,16,128]{2,1,0:T(8,128)S(1)}, f32[2,128,16]{2,1,0:T(8,128)S(1)}) custom-call(bf16[1,128,2048]{2,1,0:T(8,128)(2,1)} %query_ref.5, bf16[1,128,2048]{2,1,0:T(8,128)(2,1)} %key_ref.7, bf16[1,128,2048]{2,1,0:T(8,128)(2,1)} %value_ref.7, ...), custom_call_target="tpu_custom_call" | custom-call | tf_op jit(solution)/shard_map/pallas_call | solution.py:445
  23.2 0.0 copy-start.4
  23.2 1.0 copy-done.4
  24.2 0.0 copy-start.6
  24.2 1.0 copy-done.6
  25.2 0.0 copy-start.8
  25.2 1.0 copy-done.8
  26.1 23.1 %all-to-all-done.pay_ref = s16[8,592,128]{2,1,0:T(8,128)(2,1)S(1)} async-done(((s16[8,592,128]{2,1,0:T(8,128)(2,1)}), s16[8,592,128]{2,1,0:T(8,128)(2,1)S(1)}, u32[]{:S(2)}, u32[]{:S(2)}) %all-to-all-start) | async-done | bytes 1212448 | tf_op jit(solution)/shard_map/all_to_all | solution.py:443
  49.2 1.0 shard_map.112
  50.2 1.4 %collective-permute-start = (s16[304,128]{1,0:T(8,128)(2,1)S(1)}, s16[304,128]{1,0:T(8,128)(2,1)S(1)}, u32[]{:S(2)}, u32[]{:S(2)}) collective-permute-start(s16[304,128]{1,0:T(8,128)(2,1)S(1)} %get-tuple-element.22), channel_id=1, source_target_pairs={{0,8},{8,16},{16,24},{24,0},{1,9},{9,17},{17,25},{25,1},{2,10},{10... | collective-permute-start | bytes 233480 | tf_op jit(solution)/shard_map/ppermute | solution.py:459
  51.6 2.6 %collective-permute-start.1 = (s16[304,128]{1,0:T(8,128)(2,1)S(1)}, s16[304,128]{1,0:T(8,128)(2,1)S(1)}, u32[]{:S(2)}, u32[]{:S(2)}) collective-permute-start(s16[304,128]{1,0:T(8,128)(2,1)S(1)} %get-tuple-element.23), channel_id=1, source_target_pairs={{0,16},{8,24},{16,0},{24,8},{1,17},{9,25},{17,1},{25,9},{2,18},{10... | collective-permute-start | bytes 233480 | tf_op jit(solution)/shard_map/ppermute | solution.py:459
  54.2 1.1 collective-permute-start.2
  55.3 0.0 collective-permute-done.refs_0_
  55.3 2.3 %collective-permute-done.1.refs_1_ = s16[304,128]{1,0:T(8,128)(2,1)S(1)} collective-permute-done((s16[304,128]{1,0:T(8,128)(2,1)S(1)}, s16[304,128]{1,0:T(8,128)(2,1)S(1)}, u32[]{:S(2)}, u32[]{:S(2)}) %collective-permute-start.1) | collective-permute-done | bytes 77856 | tf_op jit(solution)/shard_map/ppermute | solution.py:459
  57.5 0.2 collective-permute-done.2.refs_2_
  57.7 1.1 shard_map.113
  58.8 0.0 copy-start
  58.8 0.0 copy-start.1
  58.8 0.0 copy-start.2
  58.9 0.0 copy-start.3
  58.9 28.6 %all_to_all.15.state_ref = s16[8,528,128]{2,1,0:T(8,128)(2,1)S(1)} all-to-all(s16[8,528,128]{2,1,0:T(8,128)(2,1)S(1)} %shard_map.113), channel_id=1, replica_groups=mesh['dp'=8,'seg'=4,'grp'=8] {'grp'}, dimensions={0} | all-to-all | bytes 2162688 | tf_op jit(solution)/shard_map/all_to_all | solution.py:469
  87.5 0.0 copy-done
  87.5 0.0 copy-done.1
  87.5 0.0 copy-done.2
  87.5 0.0 copy-done.3
  87.5 2.0 %shard_map.115 = (bf16[1,16,128]{2,1,0:T(8,128)(2,1)}, f32[256,1,16]{2,1,0:T(1,128)}) custom-call(bf16[1,128,2048]{2,1,0:T(8,128)(2,1)S(1)} %copy-done.3, bf16[1,128,2048]{2,1,0:T(8,128)(2,1)S(1)} %copy-done, bf16[1,128,2048]{2,1,0:T(8,128)(2,1)S(1)} %copy-done.1, bf16[1,128,2048]{2,1,0:T(8,128)(2,1)S(1)} %copy-done.2, ...), custom_call_target="tpu_custom_call" | custom-call | tf_op jit(solution)/shard_map/pallas_call | solution.py:470
  89.5 11.0 %all-to-all-start.2 = ((f32[256,1,16]{2,1,0:T(1,128)}), f32[256,1,16]{2,1,0:T(1,128)S(1)}, u32[]{:S(2)}, u32[]{:S(2)}) async-start(f32[256,1,16]{2,1,0:T(1,128)} %get-tuple-element.32), calls=%async_computation.2 | async-start | bytes 262144 | tf_op jit(solution)/shard_map/all_to_all | solution.py:478
  100.4 0.0 copy-start.5
  100.5 1.2 %copy-done.5 = f32[128,2048]{1,0:T(8,128)S(1)} copy-done((f32[128,2048]{1,0:T(8,128)S(1)}, f32[128,2048]{1,0:T(8,128)}, u32[]{:S(2)}) %copy-start.5) | copy-done | bytes 1048600
  101.7 0.0 copy-start.7
  101.7 1.2 %copy-done.7 = f32[128,2048]{1,0:T(8,128)S(1)} copy-done((f32[128,2048]{1,0:T(8,128)S(1)}, f32[128,2048]{1,0:T(8,128)}, u32[]{:S(2)}) %copy-start.7) | copy-done | bytes 1048600
  102.9 0.0 copy-start.9
  102.9 1.2 %copy-done.9 = f32[128,2048]{1,0:T(8,128)S(1)} copy-done((f32[128,2048]{1,0:T(8,128)S(1)}, f32[128,2048]{1,0:T(8,128)}, u32[]{:S(2)}) %copy-start.9) | copy-done | bytes 1048600
  104.1 2.2 %shard_map.114 = (bf16[1,128,2048]{2,1,0:T(8,128)(2,1)}, bf16[1,128,2048]{2,1,0:T(8,128)(2,1)}, bf16[1,128,2048]{2,1,0:T(8,128)(2,1)}) custom-call(bf16[1,128,2048]{2,1,0:T(8,128)(2,1)S(1)} %copy-done, bf16[1,128,2048]{2,1,0:T(8,128)(2,1)S(1)} %copy-done.1, bf16[1,128,2048]{2,1,0:T(8,128)(2,1)S(1)} %copy-done.2, ...), custom_call_target="tpu_custom_call" | custom-call | tf_op jit(solution)/shard_map/pallas_call | solution.py:480
  106.3 7.2 %all-to-all-done.2 = f32[256,1,16]{2,1,0:T(1,128)S(1)} async-done(((f32[256,1,16]{2,1,0:T(1,128)}), f32[256,1,16]{2,1,0:T(1,128)S(1)}, u32[]{:S(2)}, u32[]{:S(2)}) %all-to-all-start.2) | async-done | bytes 16416 | tf_op jit(solution)/shard_map/all_to_all | solution.py:478
  113.5 0.8 reduce_sum.9
Async XLA Ops:
  7.3 9.2 %copy-start.10 = (bf16[1,128,16]{1,2,0:T(8,128)(2,1)S(1)}, bf16[1,128,16]{1,2,0:T(8,128)(2,1)}, u32[]{:S(2)}) copy-start(bf16[1,128,16]{1,2,0:T(8,128)(2,1)} %param.11) | copy-start | bytes 12292
  7.3 9.2 %copy-start.11 = (f32[16]{0:T(128)S(1)}, f32[16]{0:T(128)}, u32[]{:S(2)}) copy-start(f32[16]{0:T(128)} %param.12) | copy-start | bytes 196
  7.3 9.2 %copy-start.12 = (s32[1,4]{1,0:T(1,128)S(1)}, s32[1,4]{1,0:T(1,128)}, u32[]{:S(2)}) copy-start(s32[1,4]{1,0:T(1,128)} %offsets_ref.3) | copy-start | bytes 52
  7.3 41.9 %all-to-all-start = ((s16[8,592,128]{2,1,0:T(8,128)(2,1)}), s16[8,592,128]{2,1,0:T(8,128)(2,1)S(1)}, u32[]{:S(2)}, u32[]{:S(2)}) async-start(s16[8,592,128]{2,1,0:T(8,128)(2,1)} %shard_map.111), calls=%async_computation | async-start | bytes 2424832 | tf_op jit(solution)/shard_map/all_to_all | solution.py:443
  23.2 1.0 copy-start.4
  24.2 1.0 copy-start.6
  25.2 1.0 copy-start.8
  50.2 5.1 %collective-permute-start = (s16[304,128]{1,0:T(8,128)(2,1)S(1)}, s16[304,128]{1,0:T(8,128)(2,1)S(1)}, u32[]{:S(2)}, u32[]{:S(2)}) collective-permute-start(s16[304,128]{1,0:T(8,128)(2,1)S(1)} %get-tuple-element.22), channel_id=1, source_target_pairs={{0,8},{8,16},{16,24},{24,0},{1,9},{9,17},{17,25},{25,1},{2,10},{10... | collective-permute-start | bytes 233480 | tf_op jit(solution)/shard_map/ppermute | solution.py:459
  51.6 6.0 %collective-permute-start.1 = (s16[304,128]{1,0:T(8,128)(2,1)S(1)}, s16[304,128]{1,0:T(8,128)(2,1)S(1)}, u32[]{:S(2)}, u32[]{:S(2)}) collective-permute-start(s16[304,128]{1,0:T(8,128)(2,1)S(1)} %get-tuple-element.23), channel_id=1, source_target_pairs={{0,16},{8,24},{16,0},{24,8},{1,17},{9,25},{17,1},{25,9},{2,18},{10... | collective-permute-start | bytes 233480 | tf_op jit(solution)/shard_map/ppermute | solution.py:459
  54.2 3.5 %collective-permute-start.2 = (s16[304,128]{1,0:T(8,128)(2,1)S(1)}, s16[304,128]{1,0:T(8,128)(2,1)S(1)}, u32[]{:S(2)}, u32[]{:S(2)}) collective-permute-start(s16[304,128]{1,0:T(8,128)(2,1)S(1)} %get-tuple-element.24), channel_id=1, source_target_pairs={{0,24},{8,0},{16,8},{24,16},{1,25},{9,1},{17,9},{25,17},{2,26},{10... | collective-permute-start | bytes 233480 | tf_op jit(solution)/shard_map/ppermute | solution.py:459
  58.8 28.6 %copy-start = (bf16[1,128,2048]{2,1,0:T(8,128)(2,1)S(1)}, bf16[1,128,2048]{2,1,0:T(8,128)(2,1)}, u32[]{:S(2)}) copy-start(bf16[1,128,2048]{2,1,0:T(8,128)(2,1)} %key_ref.7) | copy-start | bytes 1572868
  58.8 28.6 %copy-start.1 = (bf16[1,128,2048]{2,1,0:T(8,128)(2,1)S(1)}, bf16[1,128,2048]{2,1,0:T(8,128)(2,1)}, u32[]{:S(2)}) copy-start(bf16[1,128,2048]{2,1,0:T(8,128)(2,1)} %value_ref.7) | copy-start | bytes 1572868
  58.8 28.6 %copy-start.2 = (bf16[1,128,2048]{2,1,0:T(8,128)(2,1)S(1)}, bf16[1,128,2048]{2,1,0:T(8,128)(2,1)}, u32[]{:S(2)}) copy-start(bf16[1,128,2048]{2,1,0:T(8,128)(2,1)} %dout_ref.7) | copy-start | bytes 1572868
  58.9 28.6 %copy-start.3 = (bf16[1,128,2048]{2,1,0:T(8,128)(2,1)S(1)}, bf16[1,128,2048]{2,1,0:T(8,128)(2,1)}, u32[]{:S(2)}) copy-start(bf16[1,128,2048]{2,1,0:T(8,128)(2,1)} %query_ref.5) | copy-start | bytes 1572868
  89.5 24.0 %all-to-all-start.2 = ((f32[256,1,16]{2,1,0:T(1,128)}), f32[256,1,16]{2,1,0:T(1,128)S(1)}, u32[]{:S(2)}, u32[]{:S(2)}) async-start(f32[256,1,16]{2,1,0:T(1,128)} %get-tuple-element.32), calls=%async_computation.2 | async-start | bytes 262144 | tf_op jit(solution)/shard_map/all_to_all | solution.py:478
  100.4 1.2 %copy-start.5 = (f32[128,2048]{1,0:T(8,128)S(1)}, f32[128,2048]{1,0:T(8,128)}, u32[]{:S(2)}) copy-start(f32[128,2048]{1,0:T(8,128)} %copy-done.4) | copy-start | bytes 3145732
  101.7 1.2 %copy-start.7 = (f32[128,2048]{1,0:T(8,128)S(1)}, f32[128,2048]{1,0:T(8,128)}, u32[]{:S(2)}) copy-start(f32[128,2048]{1,0:T(8,128)} %copy-done.6) | copy-start | bytes 3145732
  102.9 1.2 %copy-start.9 = (f32[128,2048]{1,0:T(8,128)S(1)}, f32[128,2048]{1,0:T(8,128)}, u32[]{:S(2)}) copy-start(f32[128,2048]{1,0:T(8,128)} %copy-done.8) | copy-start | bytes 3145732
